TPU v7x, 32 devices: a whole 2x2x4 slice. The times are simulated.
32 devices in a mesh: section: 2 (over x), dp: 8 (over z, y), mp: 2 (over core).
Axes of the slice: x: 2, y: 2, z: 4, core: 2. Of those that a mesh axis runs over, the one named last changes fastest.
Arguments:
- act_in: bfloat16 [2, 9408, 1024], P('section', ('dp', 'mp')), may hold values from -6 to 6
- packing: int32 [8, 2, 1176], P('dp'), may hold values from 0 to 195, as said below
- enc_weights: float32 [1024, 2, 6400], P(('section', 'dp'), 'mp'), as said below
- enc_first: float32 [1024, 2, 6400], P(('section', 'dp'), 'mp'), may hold values from -56 to 56
- enc_second: float32 [1024, 2, 6400], P(('section', 'dp'), 'mp'), may hold values from 1000 to 4000
- dec_weights: float32 [512, 2, 3072], P(('section', 'dp'), 'mp'), as said below
- dec_first: float32 [512, 2, 3072], P(('section', 'dp'), 'mp'), may hold values from -56 to 56
- dec_second: float32 [512, 2, 3072], P(('section', 'dp'), 'mp'), may hold values from 1000 to 4000
- enc_norms: float32 [4, 1024], P(None, ('section', 'dp')), as said below
- enc_norm_first: float32 [4, 1024], P(None, ('section', 'dp')), may hold values from -112 to 112
- enc_norm_second: float32 [4, 1024], P(None, ('section', 'dp')), may hold values from 2000 to 32000
- dec_norms: float32 [4, 512], P(None, ('section', 'dp')), as said below
- dec_norm_first: float32 [4, 512], P(None, ('section', 'dp')), may hold values from -112 to 112
- dec_norm_second: float32 [4, 512], P(None, ('section', 'dp')), may hold values from 2000 to 32000
- mask_token: float32 [512], replicated, may hold values from -6 to 6
- dec_position: float32 [196, 512], replicated, may hold values from -6 to 6
- learning_rate: float32 [2], replicated, may hold values from 0.5 to 10, as said below
- step_count: int32 [1], replicated, may hold values from 2 to 5
Outputs:
- act_out: float32 [2, 9408, 1024], P('section', ('dp', 'mp'))
- new_enc_weights: float32 [1024, 2, 6400], P(('section', 'dp'), 'mp')
- new_dec_weights: float32 [512, 2, 3072], P(('section', 'dp'), 'mp')
- new_enc_norms: float32 [4, 1024], P(None, ('section', 'dp'))
- new_dec_norms: float32 [4, 512], P(None, ('section', 'dp'))
- enc_grads: float32 [1024, 2, 6400], P(('section', 'dp'), 'mp')
- dec_grads: float32 [512, 2, 3072], P(('section', 'dp'), 'mp')
- enc_norm_grads: float32 [4, 1024], P(None, ('section', 'dp'))
- dec_norm_grads: float32 [4, 512], P(None, ('section', 'dp'))
- grad_norm: float32 [1], replicated
Inputs may be any that keep to these rules, and one draw needn't show every extreme that they name: For each index of dp, packing[., 0, :] holds image slots 0 to 11 in order, each a contiguous run of 24 to 73 rows, then 12 on every remaining (padding) row; at least one padding row exists. packing[., 1, :] holds distinct patches within an image and 0 on padding rows. Some image has exactly 73 visible patches and some exactly 24. `enc_weights`: normal entries within six standard deviations, each column group scaled by its own factor. `dec_weights`: normal entries within six standard deviations, each column group scaled by its own factor. `enc_norms`: gains between 0.5 and 1.5, biases within 1.2 of zero. `dec_norms`: gains between 0.5 and 1.5, biases within 1.2 of zero. learning_rate[0] lies between 0.5 and 2, learning_rate[1] between 5 and 10.
All inputs are finite; a program needn't handle non-finite values.
Results may differ from a plain program's by a relative error of at most 0.014.
Values may be sent and summed in bfloat16 or wider, within the bound.
A program may use at most 320 MiB of HBM per device.

v0:
```python
import math

import jax
import jax.numpy as jnp
from jax import lax
from jax.sharding import PartitionSpec as P

FF = 4096
HEADS = 16
FFD = 2048
GRID = 196
IMG = 12
PARAMS = 16259072


NORM_EPS = 1e-06
BETA_FIRST = 0.9
BETA_SECOND = 0.999
ADAM_EPS = 1e-08
WEIGHT_DECAY = 0.05
MASKED = -1e30


def from_behind(value, axis, by):
    length = lax.axis_size(axis)
    pairs = [(i, i + by) for i in range(length) if 0 <= i + by < length]
    return lax.ppermute(value, axis, pairs)


def on_side(active, action, *operands):

    def skipped(*values):
        return jax.tree.map(
            lambda leaf_value: jnp.zeros(leaf_value.shape, leaf_value.dtype), action(*values)
        )

    return lax.cond(active, action, skipped, *operands)


def normed(tokens, gain_row, shift_row):
    average = jnp.mean(tokens, axis=-1, keepdims=True)
    centred = tokens - average
    spread = jnp.mean(centred * centred, axis=-1, keepdims=True)
    return centred * lax.rsqrt(spread + NORM_EPS) * gain_row + shift_row


def norm_back(tokens, gain_row, shift_row, grad_output):
    pulled = jax.vjp(normed, tokens, gain_row, shift_row)[1](grad_output)
    return (pulled[0], jnp.stack([pulled[1], pulled[2]]))


def contract_first(left_side, right_side):
    return lax.dot_general(
        left_side, right_side, (((0,), (0,)), ((), ())), preferred_element_type=jnp.float32
    )


def contract_last(left_side, right_side):
    return lax.dot_general(
        left_side, right_side, (((1,), (1,)), ((), ())), preferred_element_type=jnp.float32
    )


def head_piece(matrix, begin_at, head_size, groups):
    columns = lax.slice_in_dim(matrix, begin_at, begin_at + head_size, axis=1)
    return columns.reshape(groups, matrix.shape[0] // groups, head_size)


def head_forward(queries, key_rows, values, allowed, scaling):
    scores = (
        jnp.einsum("gls,gms->glm", queries, key_rows, preferred_element_type=jnp.float32) * scaling
    )
    scores = jnp.where(allowed, scores, MASKED)
    highest = jnp.max(scores, axis=-1, keepdims=True)
    weights = jnp.exp(scores - highest)
    totals = jnp.sum(weights, axis=-1, keepdims=True)
    shares = (weights / totals).astype(jnp.bfloat16)
    mixture = jnp.einsum("glm,gms->gls", shares, values, preferred_element_type=jnp.float32)
    return (mixture, highest + jnp.log(totals))


def head_backward(queries, key_rows, values, allowed, scaling, log_sum, grad_mixture):
    scores = (
        jnp.einsum("gls,gms->glm", queries, key_rows, preferred_element_type=jnp.float32) * scaling
    )
    scores = jnp.where(allowed, scores, MASKED)
    shares = jnp.exp(scores - log_sum)
    grad_values = jnp.einsum(
        "glm,gls->gms",
        shares.astype(jnp.bfloat16),
        grad_mixture,
        preferred_element_type=jnp.float32,
    )
    grad_shares = jnp.einsum(
        "gls,gms->glm", grad_mixture, values, preferred_element_type=jnp.float32
    )
    inner = jnp.sum(shares * grad_shares, axis=-1, keepdims=True)
    grad_scores = (shares * (grad_shares - inner)).astype(jnp.bfloat16)
    grad_queries = (
        jnp.einsum("glm,gms->gls", grad_scores, key_rows, preferred_element_type=jnp.float32)
        * scaling
    )
    grad_keys = (
        jnp.einsum("glm,gls->gms", grad_scores, queries, preferred_element_type=jnp.float32)
        * scaling
    )
    return (grad_queries, grad_keys, grad_values)


def attend_all(qkv_rows, allowed, groups, head_count, scaling):
    part_width = qkv_rows.shape[1] // 3
    head_size = part_width // head_count
    outputs = []
    log_sums = []
    for head_index in range(head_count):
        begin_at = head_index * head_size
        mixture, log_sum = head_forward(
            head_piece(qkv_rows, begin_at, head_size, groups),
            head_piece(qkv_rows, part_width + begin_at, head_size, groups),
            head_piece(qkv_rows, 2 * part_width + begin_at, head_size, groups),
            allowed,
            scaling,
        )
        outputs.append(mixture.reshape(qkv_rows.shape[0], head_size))
        log_sums.append(log_sum)
    return (jnp.concatenate(outputs, axis=1).astype(jnp.bfloat16), jnp.stack(log_sums))


def attend_back(qkv_rows, allowed, groups, head_count, scaling, log_sums, grad_attended):
    part_width = qkv_rows.shape[1] // 3
    head_size = part_width // head_count
    collected = [[], [], []]
    for head_index in range(head_count):
        begin_at = head_index * head_size
        results = head_backward(
            head_piece(qkv_rows, begin_at, head_size, groups),
            head_piece(qkv_rows, part_width + begin_at, head_size, groups),
            head_piece(qkv_rows, 2 * part_width + begin_at, head_size, groups),
            allowed,
            scaling,
            log_sums[head_index],
            head_piece(grad_attended, begin_at, head_size, groups),
        )
        for which_part in range(3):
            collected[which_part].append(results[which_part].reshape(qkv_rows.shape[0], head_size))
    return jnp.concatenate(
        [jnp.concatenate(column_list, axis=1) for column_list in collected], axis=1
    )


def block_forward(active, stream, matrices, gain_rows, groups, allowed, gather_rows, sum_rows):
    qkv_weight, out_weight, up_weight, down_weight = matrices
    head_size = stream.shape[1] // HEADS
    head_count = qkv_weight.shape[1] // 3 // head_size
    scaling = head_size ** (-0.5)
    first_in = on_side(
        active,
        lambda tokens, gain_set: normed(tokens, gain_set[0], gain_set[1]).astype(jnp.bfloat16),
        stream,
        gain_rows,
    )
    first_all = gather_rows(first_in)

    def mixing(first_rows):
        qkv_rows = jnp.dot(first_rows, qkv_weight, preferred_element_type=jnp.float32).astype(
            jnp.bfloat16
        )
        attended, log_sums = attend_all(qkv_rows, allowed, groups, head_count, scaling)
        return (qkv_rows, attended, log_sums, contract_last(attended, out_weight))

    qkv_rows, attended, log_sums, partial_mix = on_side(active, mixing, first_all)
    after_mix = stream + sum_rows(partial_mix)
    second_in = on_side(
        active,
        lambda tokens, gain_set: normed(tokens, gain_set[2], gain_set[3]).astype(jnp.bfloat16),
        after_mix,
        gain_rows,
    )
    second_all = gather_rows(second_in)

    def feeding(second_rows):
        pre_act = jnp.dot(second_rows, up_weight, preferred_element_type=jnp.float32)
        hidden = jax.nn.gelu(pre_act, approximate=False).astype(jnp.bfloat16)
        return (pre_act, hidden, contract_last(hidden, down_weight))

    pre_act, hidden, partial_feed = on_side(active, feeding, second_all)
    result = after_mix + sum_rows(partial_feed)
    return (
        result,
        (first_all, qkv_rows, attended, log_sums, after_mix, second_all, pre_act, hidden),
    )


def block_backward(
    active, grad_result, stream, matrices, gain_rows, saved, groups, allowed, gather_rows, sum_rows
):
    qkv_weight, out_weight, up_weight, down_weight = matrices
    first_all, qkv_rows, attended, log_sums, after_mix, second_all, pre_act, hidden = saved
    head_size = stream.shape[1] // HEADS
    head_count = qkv_weight.shape[1] // 3 // head_size
    scaling = head_size ** (-0.5)
    grad_feed_all = gather_rows(grad_result.astype(jnp.bfloat16))

    def feed_back(grad_rows):
        grad_down = contract_first(grad_rows, hidden)
        grad_hidden = jnp.dot(grad_rows, down_weight, preferred_element_type=jnp.float32)
        gelu_pull = jax.vjp(
            lambda inside_value: jax.nn.gelu(inside_value, approximate=False), pre_act
        )[1]
        grad_pre = gelu_pull(grad_hidden)[0].astype(jnp.bfloat16)
        return (grad_down, contract_first(second_all, grad_pre), contract_last(grad_pre, up_weight))

    grad_down, grad_up, partial_second = on_side(active, feed_back, grad_feed_all)
    grad_second = sum_rows(partial_second)
    grad_after, grad_gains_two = on_side(
        active, norm_back, after_mix, gain_rows[2], gain_rows[3], grad_second
    )
    grad_after = grad_after + grad_result
    grad_mix_all = gather_rows(grad_after.astype(jnp.bfloat16))

    def mix_back(grad_rows):
        grad_out = contract_first(grad_rows, attended)
        grad_attended = jnp.dot(grad_rows, out_weight, preferred_element_type=jnp.float32).astype(
            jnp.bfloat16
        )
        grad_qkv = attend_back(
            qkv_rows, allowed, groups, head_count, scaling, log_sums, grad_attended
        ).astype(jnp.bfloat16)
        return (grad_out, contract_first(first_all, grad_qkv), contract_last(grad_qkv, qkv_weight))

    grad_out, grad_qkv_weight, partial_first = on_side(active, mix_back, grad_mix_all)
    grad_first = sum_rows(partial_first)
    grad_stream, grad_gains_one = on_side(
        active, norm_back, stream, gain_rows[0], gain_rows[1], grad_first
    )
    grad_stream = grad_stream + grad_after
    matrix_grad = jnp.concatenate([grad_qkv_weight, grad_out, grad_up, grad_down], axis=1)
    gain_grad = jnp.concatenate([grad_gains_one, grad_gains_two], axis=0)
    return (grad_stream, matrix_grad, gain_grad)


def split_matrices(gathered_pack, hidden_units, mp_count):
    matrix = gathered_pack[:, 0, :]
    part_width = matrix.shape[0] // mp_count
    part_hidden = hidden_units // mp_count
    borders = [
        3 * part_width,
        4 * part_width,
        4 * part_width + part_hidden,
        4 * part_width + 2 * part_hidden,
    ]
    return (
        (
            matrix[:, : borders[0]],
            matrix[:, borders[0] : borders[1]],
            matrix[:, borders[1] : borders[2]],
            matrix[:, borders[2] : borders[3]],
        ),
        matrix[:, borders[3] :],
    )


def update(
    weight,
    first_moment,
    second_moment,
    gradient,
    factor,
    step_rate,
    fix_first,
    fix_second,
    decay_rate,
):
    clipped = gradient * factor
    new_first = BETA_FIRST * first_moment + (1.0 - BETA_FIRST) * clipped
    new_second = BETA_SECOND * second_moment + (1.0 - BETA_SECOND) * clipped * clipped
    stepped = new_first / fix_first / (jnp.sqrt(new_second / fix_second) + ADAM_EPS)
    return weight - step_rate * (stepped + decay_rate * weight)


def per_device(
    act_in,
    packing,
    enc_weights,
    enc_first,
    enc_second,
    dec_weights,
    dec_first,
    dec_second,
    enc_norms,
    enc_norm_first,
    enc_norm_second,
    dec_norms,
    dec_norm_first,
    dec_norm_second,
    mask_token,
    dec_position,
    learning_rate,
    step_count,
):
    encoder_side = lax.axis_index("section") == 0
    decoder_side = jnp.logical_not(encoder_side)
    mp_rank = lax.axis_index("mp")
    mp_count = lax.axis_size("mp")
    slot_ids = packing[0, 0]
    patch_ids = packing[0, 1]
    pack_allowed = (slot_ids[:, None] == slot_ids[None, :])[None]
    grid_allowed = jnp.ones((1, 1, 1), dtype=jnp.bool_)
    local_images = IMG // mp_count
    grid_cells = local_images * GRID
    local_slot = slot_ids - mp_rank * local_images
    inside = jnp.logical_and(local_slot >= 0, local_slot < local_images)
    target = jnp.where(inside, local_slot * GRID + patch_ids, grid_cells)

    def enc_gather(tokens):
        return lax.all_gather(tokens, "mp", axis=0, tiled=True)

    def enc_sum(partial_rows):
        return lax.psum_scatter(
            partial_rows.astype(jnp.bfloat16), "mp", scatter_dimension=0, tiled=True
        ).astype(jnp.float32)

    def dec_gather(tokens):
        return lax.all_gather(tokens, "mp", axis=0, tiled=True)

    def dec_sum(partial_rows):
        return lax.psum_scatter(
            partial_rows.astype(jnp.bfloat16), "mp", scatter_dimension=0, tiled=True
        ).astype(jnp.float32)

    low_weights = (
        enc_weights.astype(jnp.bfloat16),
        dec_weights.astype(jnp.bfloat16),
        enc_norms.astype(jnp.bfloat16),
        dec_norms.astype(jnp.bfloat16),
    )
    gathered = (
        lax.all_gather(low_weights[0], ("section", "dp"), axis=0, tiled=True),
        lax.all_gather(low_weights[1], ("section", "dp"), axis=0, tiled=True),
        lax.all_gather(low_weights[2], ("section", "dp"), axis=1, tiled=True),
        lax.all_gather(low_weights[3], ("section", "dp"), axis=1, tiled=True),
    )
    enc_mats, enc_projection = split_matrices(gathered[0], FF, mp_count)
    dec_mats, unused_tail = split_matrices(gathered[1], FFD, mp_count)
    enc_gains = gathered[2].astype(jnp.float32)
    dec_gains = gathered[3].astype(jnp.float32)
    stream_in = act_in[0].astype(jnp.float32)
    encoded, enc_saved = block_forward(
        encoder_side, stream_in, enc_mats, enc_gains, 1, pack_allowed, enc_gather, enc_sum
    )
    encoded_all = enc_gather(encoded.astype(jnp.bfloat16))
    projected = on_side(
        encoder_side,
        lambda tokens: jnp.dot(tokens, enc_projection, preferred_element_type=jnp.float32).astype(
            jnp.bfloat16
        ),
        encoded_all,
    )
    arrived = from_behind(projected, "section", 1)
    visible = lax.all_gather(arrived, "mp", axis=1, tiled=True)

    def build(visible_rows):
        grid_rows = (
            jnp.zeros((grid_cells, visible_rows.shape[1]), jnp.float32)
            .at[target]
            .set(visible_rows.astype(jnp.float32), mode="drop")
        )
        seen_mask = jnp.zeros((grid_cells,), jnp.float32).at[target].set(1.0, mode="drop")
        return jnp.where(seen_mask[:, None] > 0, grid_rows, mask_token[None, :]) + jnp.tile(
            dec_position, (local_images, 1)
        )

    dec_stream = on_side(decoder_side, build, visible)
    decoded, dec_saved = block_forward(
        decoder_side, dec_stream, dec_mats, dec_gains, IMG, grid_allowed, dec_gather, dec_sum
    )
    regathered = (
        lax.all_gather(low_weights[0], ("section", "dp"), axis=0, tiled=True),
        lax.all_gather(low_weights[1], ("section", "dp"), axis=0, tiled=True),
        lax.all_gather(low_weights[2], ("section", "dp"), axis=1, tiled=True),
        lax.all_gather(low_weights[3], ("section", "dp"), axis=1, tiled=True),
    )
    enc_mats_back, enc_projection_back = split_matrices(regathered[0], FF, mp_count)
    dec_mats_back, unused_back = split_matrices(regathered[1], FFD, mp_count)
    enc_gains_back = regathered[2].astype(jnp.float32)
    dec_gains_back = regathered[3].astype(jnp.float32)
    cotangent = act_in[0].astype(jnp.float32).reshape(grid_cells, dec_position.shape[1])
    grad_dec_in, dec_matrix_grad, dec_gain_grad = block_backward(
        decoder_side,
        cotangent,
        dec_stream,
        dec_mats_back,
        dec_gains_back,
        dec_saved,
        IMG,
        grid_allowed,
        dec_gather,
        dec_sum,
    )

    def pick(grad_grid):
        clamped = jnp.minimum(target, grid_cells - 1)
        return jnp.where(inside[:, None], grad_grid[clamped], 0.0)

    picked = on_side(decoder_side, pick, grad_dec_in)
    returned = lax.psum_scatter(picked.astype(jnp.bfloat16), "mp", scatter_dimension=1, tiled=True)
    grad_projected = from_behind(returned, "section", -1)

    def project_back(grad_rows):
        return (
            contract_first(encoded_all, grad_rows),
            contract_last(grad_rows, enc_projection_back),
        )

    grad_projection, partial_encoded = on_side(encoder_side, project_back, grad_projected)
    grad_encoded = enc_sum(partial_encoded)
    grad_input, enc_matrix_grad, enc_gain_grad = block_backward(
        encoder_side,
        grad_encoded,
        stream_in,
        enc_mats_back,
        enc_gains_back,
        enc_saved,
        1,
        pack_allowed,
        enc_gather,
        enc_sum,
    )
    enc_grad = jnp.concatenate([enc_matrix_grad, grad_projection], axis=1)[:, None, :]
    dec_grad = dec_matrix_grad[:, None, :]
    reduced = (
        lax.psum_scatter(enc_grad, ("section", "dp"), scatter_dimension=0, tiled=True),
        lax.psum_scatter(dec_grad, ("section", "dp"), scatter_dimension=0, tiled=True),
        lax.psum_scatter(enc_gain_grad, ("section", "dp"), scatter_dimension=1, tiled=True),
        lax.psum_scatter(dec_gain_grad, ("section", "dp"), scatter_dimension=1, tiled=True),
    )
    enc_gain_shard, dec_gain_shard = lax.psum((reduced[2], reduced[3]), "mp")
    local_squares = (
        jnp.sum(reduced[0] * reduced[0])
        + jnp.sum(reduced[1] * reduced[1])
        + (jnp.sum(enc_gain_shard * enc_gain_shard) + jnp.sum(dec_gain_shard * dec_gain_shard))
        / mp_count
    )
    square_total = lax.psum(local_squares, ("section", "dp", "mp"))
    grad_norm = jnp.sqrt(square_total)
    factor = jnp.minimum(1.0, math.sqrt(PARAMS) / (grad_norm + 1e-06))
    step_value = step_count[0].astype(jnp.float32)
    fix_first = 1.0 - jnp.power(BETA_FIRST, step_value)
    fix_second = 1.0 - jnp.power(BETA_SECOND, step_value)
    step_rate = learning_rate[0]
    norm_rate = learning_rate[1]
    enc_new = update(
        enc_weights,
        enc_first,
        enc_second,
        reduced[0],
        factor,
        step_rate,
        fix_first,
        fix_second,
        WEIGHT_DECAY,
    )
    dec_new = update(
        dec_weights,
        dec_first,
        dec_second,
        reduced[1],
        factor,
        step_rate,
        fix_first,
        fix_second,
        WEIGHT_DECAY,
    )
    enc_norm_new = update(
        enc_norms,
        enc_norm_first,
        enc_norm_second,
        enc_gain_shard,
        factor,
        norm_rate,
        fix_first,
        fix_second,
        0.0,
    )
    dec_norm_new = update(
        dec_norms,
        dec_norm_first,
        dec_norm_second,
        dec_gain_shard,
        factor,
        norm_rate,
        fix_first,
        fix_second,
        0.0,
    )
    act_out = jnp.where(encoder_side, grad_input, decoded.reshape(grad_input.shape))[None]
    return (
        act_out,
        enc_new,
        dec_new,
        enc_norm_new,
        dec_norm_new,
        reduced[0] * factor,
        reduced[1] * factor,
        enc_gain_shard * factor,
        dec_gain_shard * factor,
        grad_norm.reshape(1),
    )


def solution(mesh):
    in_specs = (
        P("section", ("dp", "mp"), None),
        P("dp", None, None),
        P(("section", "dp"), "mp", None),
        P(("section", "dp"), "mp", None),
        P(("section", "dp"), "mp", None),
        P(("section", "dp"), "mp", None),
        P(("section", "dp"), "mp", None),
        P(("section", "dp"), "mp", None),
        P(None, ("section", "dp")),
        P(None, ("section", "dp")),
        P(None, ("section", "dp")),
        P(None, ("section", "dp")),
        P(None, ("section", "dp")),
        P(None, ("section", "dp")),
        P(),
        P(),
        P(),
        P(),
    )
    out_specs = (
        P("section", ("dp", "mp"), None),
        P(("section", "dp"), "mp", None),
        P(("section", "dp"), "mp", None),
        P(None, ("section", "dp")),
        P(None, ("section", "dp")),
        P(("section", "dp"), "mp", None),
        P(("section", "dp"), "mp", None),
        P(None, ("section", "dp")),
        P(None, ("section", "dp")),
        P(),
    )
    return jax.shard_map(
        per_device, mesh=mesh, in_specs=in_specs, out_specs=out_specs, check_vma=False
    )
```

profile of v0, /device:TPU:0, one launch (start us, length us, event | category | flops | bytes accessed | tf_op | source)
XLA Modules:
  0.0 2432.7 jit_solution(3088785259745006625)
XLA Ops:
  7.9 42.4 %all-gather = bf16[16,64,4]{1,2,0:T(4,128)(2,1)S(1)} all-gather(bf16[1,64,4]{1,2,0:T(4,128)(2,1)S(1)} %convert_bitcast_fusion.1), channel_id=1, replica_groups=mesh['section'=2,'dp'=8,'mp'=2] {'section','dp'}, dimensions={0}, use_global_device_ids=true | all-gather | bytes 8704 | tf_op jit(solution)/shard_map/all_gather | solution.py:340
  71.4 157.4 %all-gather.20.cloned.1.call-done = bf16[1024,1,6400]{2,0,1:T(8,128)(2,1)} async-done(((bf16[64,1,6400]{2,0,1:T(8,128)(2,1)}), bf16[1024,1,6400]{2,0,1:T(8,128)(2,1)}) %all-gather.20.cloned.1.call-update) | async-done | bytes 13107216 | tf_op jit(solution)/shard_map/all_gather | solution.py:338
  234.8 78.5 %conditional.21 = (bf16[1176,1536]{1,0:T(8,128)(2,1)}, bf16[1176,512]{0,1:T(8,128)(2,1)}, f32[8,1,1176,1]{2,3,1,0:T(1,128)}, bf16[1176,1024]{1,0:T(8,128)(2,1)S(1)}) conditional(s32[]{:T(128)} %convert_element_type.316, () %tuple.159, (bf16[1176,1024]{1,0:T(8,128)(2,1)S(1)}, bf16[1024,1536]{1,0:T(8,128)(2,1)S(1)}, ...), branch_computations={%region_4.5_spmd, %region_5.22_spmd} | conditional | flops 7855743488 | bytes 207742816 | solution.py:37
  351.9 35.2 %conditional.23 = (f32[1176,2048]{1,0:T(8,128)S(1)}, bf16[1176,2048]{1,0:T(8,128)(2,1)}, bf16[1176,1024]{1,0:T(8,128)(2,1)S(1)}) conditional(s32[]{:T(128)} %convert_element_type.316, () %tuple.163, (bf16[1176,1024]{1,0:T(8,128)(2,1)S(1)}, bf16[1024,2048]{1,0:T(8,128)(2,1)}, bf16[1024,2048]{1,0:T(8,128)(2,1)}) %tuple.166), branch_computations={%region_27.28_spmd, %region_28.29_spmd} | conditional | flops 10021552128 | bytes 49250356 | solution.py:37
  351.9 27.3 %fusion.119 = (bf16[1176,2048]{1,0:T(8,128)(2,1)}, f32[1176,2048]{1,0:T(8,128)S(1)}) fusion(bf16[1176,1024]{1,0:T(8,128)(2,1)S(1)} %get-tuple-element.180, bf16[1024,2048]{1,0:T(8,128)(2,1)} %get-tuple-element.181), kind=kOutput, calls=%fused_computation.135 | convolution fusion | flops 5089050624 | bytes 21053440 | tf_op jit(solution)/shard_map/cond/branch_1_fun/dot_general | solution.py:182
  379.2 7.9 fusion.614
  392.2 7.2 fusion.1
  403.2 7.1 concatenate.33
  415.5 9.6 all-gather.38.cloned.1.call-done
  432.9 13.4 collective-permute-done
  448.1 42.0 %all-gather.4 = bf16[16,32,4]{1,2,0:T(4,128)(2,1)S(1)} all-gather(bf16[1,32,4]{1,2,0:T(4,128)(2,1)S(1)} %convert_bitcast_fusion), channel_id=1, replica_groups=mesh['section'=2,'dp'=8,'mp'=2] {'section','dp'}, dimensions={0}, use_global_device_ids=true | all-gather | bytes 4352 | tf_op jit(solution)/shard_map/all_gather | solution.py:341
  492.5 38.9 %all-gather.28.cloned.1.call-done = bf16[512,1,3072]{2,0,1:T(8,128)(2,1)} async-done(((bf16[32,1,3072]{2,0,1:T(8,128)(2,1)}), bf16[512,1,3072]{2,0,1:T(8,128)(2,1)}) %all-gather.28.cloned.1.call-update) | async-done | bytes 3145744 | tf_op jit(solution)/shard_map/all_gather | solution.py:339
  534.5 8.6 all-gather.26.cloned.1.call-done
  543.1 12.1 conditional.27
  555.3 162.9 %reduce-scatter.22.cloned.1.call-done = bf16[1176,512]{1,0:T(8,128)(2,1)} async-done(((bf16[2352,512]{1,0:T(8,128)(2,1)}), bf16[1176,512]{1,0:T(8,128)(2,1)}) %reduce-scatter.22.cloned.1.call-update) | async-done | bytes 1204240 | tf_op jit(solution)/shard_map/reduce_scatter | solution.py:327
  727.3 10.8 all-gather.30.cloned.1.call-done
  738.0 9.4 conditional.29
  756.8 68.8 %reduce-scatter.24.cloned.1.call-done = bf16[1176,512]{1,0:T(8,128)(2,1)} async-done(((bf16[2352,512]{1,0:T(8,128)(2,1)}), bf16[1176,512]{1,0:T(8,128)(2,1)}) %reduce-scatter.24.cloned.1.call-update) | async-done | bytes 1204240 | tf_op jit(solution)/shard_map/reduce_scatter | solution.py:327
  834.9 16.8 all-gather.32.cloned.1.call-done
  851.6 10.1 conditional.32
  862.7 226.7 %reduce-scatter.26.cloned.1.call-done = bf16[1176,512]{1,0:T(8,128)(2,1)} async-done(((bf16[2352,512]{1,0:T(8,128)(2,1)}), bf16[1176,512]{1,0:T(8,128)(2,1)}) %reduce-scatter.26.cloned.1.call-update) | async-done | bytes 1204240 | tf_op jit(solution)/shard_map/reduce_scatter | solution.py:327
  1095.5 24.1 reduce-scatter.28.cloned.1.call-done
  1120.9 16.5 collective-permute-done.1
  1159.2 11.5 all-gather.40.cloned.1.call-done
  1170.8 67.1 %conditional.36 = (f32[1024,2048]{1,0:T(8,128)}, bf16[1176,1024]{1,0:T(8,128)(2,1)}, f32[1024,2048]{1,0:T(8,128)}) conditional(s32[]{:T(128)} %convert_element_type.316, () %tuple.157, (bf16[2,588,1024]{2,1,0:T(8,128)(2,1)}, bf16[1176,2048]{1,0:T(8,128)(2,1)}, f32[1176,2048]{1,0:T(8,128)}, bf16[1024,2048]{1,0:T(8,128)(2,1)}, ...), branch_computations={%region_101.102_spmd, %region_102.103_spmd} | conditional | flops 19903414272 | bytes 130973840 | solution.py:37
  1174.4 29.0 %fusion.339 = bf16[1176,2048]{1,0:T(8,128)(2,1)S(1)} fusion(f32[1176,2048]{1,0:T(8,128)} %get-tuple-element.227, bf16[1176,1024]{1,0:T(8,128)(2,1)S(1)} %reshape.1625, bf16[1024,2048]{1,0:T(8,128)(2,1)} %get-tuple-element.228), kind=kOutput, calls=%fused_computation.511 | convolution fusion | flops 5105909760 | bytes 21053440 | tf_op jit(solution)/shard_map/cond/branch_1_fun/dot_general | solution.py:206
  1209.9 8.0 convolution_bitcast_fusion.2
  1218.0 9.3 copy.914
  1227.3 10.2 fusion.618
  1255.2 11.4 conditional.37
  1282.2 222.2 %conditional.38 = (f32[1024,512]{1,0:T(8,128)}, bf16[1176,1024]{1,0:T(8,128)(2,1)}, f32[1024,1536]{1,0:T(8,128)}) conditional(s32[]{:T(128)} %convert_element_type.316, () %tuple.155, (bf16[2,588,1024]{2,1,0:T(8,128)(2,1)}, bf16[1176,512]{0,1:T(8,128)(2,1)}, bf16[1176,1536]{1,0:T(8,128)(2,1)}, pred[1,1176,1176]{1,2,0:T(8,128)(4,1)S(1)}, ...), branch_computations={%region_112.113_spmd, %region_113.122_spmd} | conditional | flops 17049016320 | bytes 693110144 | solution.py:37
  1337.7 7.7 fusion.399
  1353.1 7.5 fusion.397
  1370.8 7.6 fusion.395
  1378.4 7.3 fusion.405
  1389.0 7.5 fusion.393
  1396.5 7.2 fusion.406
  1407.0 7.8 fusion.391
  1414.9 7.0 fusion.407
  1483.5 8.0 fusion.625
  1522.1 7.9 constant_dynamic-update-slice_fusion.50
  1530.0 8.0 constant_dynamic-update-slice_fusion.49
  1545.8 11.4 conditional.39
  1560.8 21.7 broadcast_in_dim.231
  1600.9 66.3 %reduce-scatter.32.cloned.1.call-done = f32[64,4]{1,0:T(8,128)} async-done(((f32[1024,4]{1,0:T(8,128)}), f32[64,4]{1,0:T(8,128)}) %reduce-scatter.32.cloned.1.call-update) | async-done | bytes 1040
  1673.4 678.1 %all-reduce.16.cloned.1.call-done = f32[1024,1,6400]{2,1,0:T(1,128)} async-done(((f32[1024,1,6400]{2,1,0:T(1,128)}), f32[1024,1,6400]{2,1,0:T(1,128)}) %all-reduce.16.cloned.1.call-update) | async-done | bytes 26214416
  2363.8 39.3 %psum.23 = f32[]{:T(128)} all-reduce(f32[]{:T(128)S(6)} %add.506), channel_id=1, replica_groups=mesh['section'=2,'dp'=8,'mp'=2] {'section','dp','mp'}, use_global_device_ids=true, to_apply=%region_142.143 | all-reduce | flops 1 | bytes 8 | tf_op jit(solution)/shard_map/psum | solution.py:444
  2406.4 13.0 multiply_subtract_fusion
  (488 shorter events, 566.2 us)
Async XLA Ops:
  7.2 60.6 %all-gather.34.cloned.1.call-start = ((), (), s32[]{:S(2)}) async-start(), calls=%async_computation.19 | async-start | bytes 3637248 | tf_op jit(solution)/shard_map/all_gather | solution.py:316
  50.4 281.3 %copy-start.136 = (f32[1024,4]{0,1:T(4,128)}, f32[1024,4]{0,1:T(4,128)S(1)}, u32[]{:S(2)}) copy-start(f32[1024,4]{0,1:T(4,128)S(1)} %reshape.1612) | copy-start | bytes 49156
  60.7 168.0 %all-gather.20.cloned.1.call-start = ((), (), s32[]{:S(2)}) async-start(), calls=%async_computation.7 | async-start | bytes 13926400 | tf_op jit(solution)/shard_map/all_gather | solution.py:338
  61.8 286.5 %all-gather.36.cloned.1.call-start = ((), (), s32[]{:S(2)}) async-start(), calls=%async_computation.20 | async-start | bytes 3637248 | tf_op jit(solution)/shard_map/all_gather | solution.py:316
  64.0 169.1 %copy-start.5 = (pred[1,1176,1176]{1,2,0:T(8,128)(4,1)}, pred[1,1176,1176]{1,2,0:T(8,128)(4,1)S(1)}, u32[]{:S(2)}) copy-start(pred[1,1176,1176]{1,2,0:T(8,128)(4,1)S(1)} %broadcast_compare_fusion.1) | copy-start | bytes 4148932
  321.2 3.5 collective-permute-start.2
  338.9 86.2 %all-gather.38.cloned.1.call-start = ((), (), s32[]{:S(2)}) async-start(), calls=%async_computation.21 | async-start | bytes 3637248 | tf_op jit(solution)/shard_map/all_gather | solution.py:316
  351.9 27.3 %copy-start.41 = (bf16[1024,2048]{1,0:T(8,128)(2,1)S(1)}, bf16[1024,2048]{1,0:T(8,128)(2,1)}, u32[]{:S(2)}) copy-start(bf16[1024,2048]{1,0:T(8,128)(2,1)} %get-tuple-element.182) | copy-start | bytes 12582916 | tf_op jit(solution)/shard_map/cond
  400.2 3.0 collective-permute-start.3
  413.6 77.2 %all-gather.24.cloned.1.call-start = ((), (), s32[]{:S(2)}) async-start(), calls=%async_computation.9 | async-start | bytes 1806336 | tf_op jit(solution)/shard_map/all_gather | solution.py:360
  428.7 61.5 %copy-start.135 = (s32[1176]{0:T(1024)S(1)}, s32[1176]{0:T(1024)}, u32[]{:S(2)}) copy-start(s32[1176]{0:T(1024)} %copy-done.134) | copy-start | bytes 14116
  428.7 61.5 %copy-start.141 = (s32[1176]{0:T(1024)S(1)}, s32[1176]{0:T(1024)}, u32[]{:S(2)}) copy-start(s32[1176]{0:T(1024)} %get-tuple-element.486) | copy-start | bytes 14116
  428.7 62.1 %copy-start.124 = (f32[196,512]{1,0:T(8,128)S(1)}, f32[196,512]{1,0:T(8,128)}, u32[]{:S(2)}) copy-start(f32[196,512]{1,0:T(8,128)} %param.73) | copy-start | bytes 1204228
  428.7 62.1 %copy-start.150 = (f32[512]{0:T(512)S(1)}, f32[512]{0:T(512)}, u32[]{:S(2)}) copy-start(f32[512]{0:T(512)} %param.72) | copy-start | bytes 6148
  431.6 14.8 collective-permute-start
  447.2 84.2 %all-gather.28.cloned.1.call-start = ((), (), s32[]{:S(2)}) async-start(), calls=%async_computation.11 | async-start | bytes 3342336 | tf_op jit(solution)/shard_map/all_gather | solution.py:339
  448.0 95.0 %all-gather.26.cloned.1.call-start = ((), (), s32[]{:S(2)}) async-start(), calls=%async_computation.10 | async-start | bytes 3612672 | tf_op jit(solution)/shard_map/all_gather | solution.py:324
  491.1 227.1 %copy-start = (f32[1176,512]{1,0:T(8,128)}, f32[1176,512]{1,0:T(8,128)S(1)}, u32[]{:S(2)}) copy-start(f32[1176,512]{1,0:T(8,128)S(1)} %get-tuple-element.728) | copy-start | bytes 7225348
  492.4 225.8 %reduce-scatter.22.cloned.1.call-start = ((), (), s32[]{:S(2)}) async-start(), calls=%async_computation.12 | async-start | bytes 3612672 | tf_op jit(solution)/shard_map/reduce_scatter | solution.py:327
  555.2 182.8 %all-gather.30.cloned.1.call-start = ((), (), s32[]{:S(2)}) async-start(), calls=%async_computation.13 | async-start | bytes 3612672 | tf_op jit(solution)/shard_map/all_gather | solution.py:324
  555.3 166.0 %copy-start.140 = (f32[512,4]{0,1:T(4,128)S(1)}, f32[512,4]{0,1:T(4,128)}, u32[]{:S(2)}) copy-start(f32[512,4]{0,1:T(4,128)} %copy-done.139) | copy-start | bytes 24580
  722.4 29.3 %all-gather.22.cloned.1.call-start = ((), (), s32[]{:S(2)}) async-start(), calls=%async_computation.8 | async-start | bytes 3612672 | tf_op jit(solution)/shard_map/all_gather | solution.py:324
  725.7 99.9 %reduce-scatter.24.cloned.1.call-start = ((), (), s32[]{:S(2)}) async-start(), calls=%async_computation.14 | async-start | bytes 3612672 | tf_op jit(solution)/shard_map/reduce_scatter | solution.py:327
  756.7 72.0 %copy-start.2 = (f32[1176,512]{1,0:T(8,128)S(1)}, f32[1176,512]{1,0:T(8,128)}, u32[]{:S(2)}) copy-start(f32[1176,512]{1,0:T(8,128)} %convert_add_fusion.4) | copy-start | bytes 7225348
  756.8 94.9 %all-gather.32.cloned.1.call-start = ((), (), s32[]{:S(2)}) async-start(), calls=%async_computation.15 | async-start | bytes 3612672 | tf_op jit(solution)/shard_map/all_gather | solution.py:324
  834.8 254.6 %reduce-scatter.26.cloned.1.call-start = ((), (), s32[]{:S(2)}) async-start(), calls=%async_computation.16 | async-start | bytes 3612672 | tf_op jit(solution)/shard_map/reduce_scatter | solution.py:327
  861.8 230.8 %copy-start.1 = (f32[1176,512]{1,0:T(8,128)S(1)}, f32[1176,512]{1,0:T(8,128)}, u32[]{:S(2)}) copy-start(f32[1176,512]{1,0:T(8,128)} %copy-done) | copy-start | bytes 7225348
  861.8 257.8 %reduce-scatter.28.cloned.1.call-start = ((), (), s32[]{:S(2)}) async-start(), calls=%async_computation.17 | async-start | bytes 1806336 | tf_op jit(solution)/shard_map/reduce_scatter | solution.py:406
  1095.4 75.4 %all-gather.40.cloned.1.call-start = ((), (), s32[]{:S(2)}) async-start(), calls=%async_computation.22 | async-start | bytes 3637248 | tf_op jit(solution)/shard_map/all_gather | solution.py:316
  1119.6 17.8 collective-permute-start.1
  1149.6 3.1 collective-permute-start.4
  1159.2 122.5 %all-gather.42.cloned.1.call-start = ((), (), s32[]{:S(2)}) async-start(), calls=%async_computation.23 | async-start | bytes 3637248 | tf_op jit(solution)/shard_map/all_gather | solution.py:316
  1174.4 29.0 %copy-start.42 = (bf16[1024,2048]{1,0:T(8,128)(2,1)S(1)}, bf16[1024,2048]{1,0:T(8,128)(2,1)}, u32[]{:S(2)}) copy-start(bf16[1024,2048]{1,0:T(8,128)(2,1)} %get-tuple-element.230) | copy-start | bytes 12582916 | tf_op jit(solution)/shard_map/cond
  1244.3 3.0 collective-permute-start.5
  1270.2 315.7 %reduce-scatter.30.cloned.1.call-start = ((), (), s32[]{:S(2)}) async-start(), calls=%async_computation.18 | async-start | bytes 3612672 | tf_op jit(solution)/shard_map/reduce_scatter | solution.py:327
  1270.8 321.9 %reduce-scatter.34.cloned.1.call-start = ((), (), s32[]{:S(2)}) async-start(), calls=%async_computation.25 | async-start | bytes 278528
  1271.7 321.7 %all-reduce.18.cloned.1.call-start = ((), (), s32[]{:S(2)}) async-start(), calls=%async_computation.27 | async-start | bytes 12582912
  1280.5 386.7 %reduce-scatter.32.cloned.1.call-start = ((), (), s32[]{:S(2)}) async-start(), calls=%async_computation.24 | async-start | bytes 557056
  1510.9 27.0 %collective-permute-start.6 = (bf16[4,1024]{1,0:T(4,128)(2,1)S(1)}, bf16[4,1024]{1,0:T(4,128)(2,1)S(1)}, u32[]{:S(2)}, u32[]{:S(2)}) collective-permute-start(bf16[4,1024]{1,0:T(4,128)(2,1)S(1)} %slice.588), channel_id=1, source_target_pairs={{0,1},{2,3},{4,5},{6,7},{8,9},{10,11},{12,13},{14,15},{16,17},{18,... | collective-permute-start | bytes 24584
  1558.3 793.2 %all-reduce.16.cloned.1.call-start = ((), (), s32[]{:S(2)}) async-start(), calls=%async_computation.26 | async-start | bytes 52428800
  1673.3 730.5 %copy-start.148 = (f32[4,32]{1,0:T(4,128)S(1)}, f32[4,32]{1,0:T(4,128)}, u32[]{:S(2)}) copy-start(f32[4,32]{1,0:T(4,128)} %param.69) | copy-start | bytes 1540
  1673.3 730.5 %copy-start.151 = (f32[4,32]{1,0:T(4,128)S(1)}, f32[4,32]{1,0:T(4,128)}, u32[]{:S(2)}) copy-start(f32[4,32]{1,0:T(4,128)} %param.71) | copy-start | bytes 1540
  1673.3 730.5 %copy-start.152 = (f32[4,32]{1,0:T(4,128)S(1)}, f32[4,32]{1,0:T(4,128)}, u32[]{:S(2)}) copy-start(f32[4,32]{1,0:T(4,128)} %param.70) | copy-start | bytes 1540
  1673.4 731.8 %copy-start.149 = (f32[4,64]{1,0:T(4,128)S(1)}, f32[4,64]{1,0:T(4,128)}, u32[]{:S(2)}) copy-start(f32[4,64]{1,0:T(4,128)} %param.66) | copy-start | bytes 3076
  1673.4 731.8 %copy-start.153 = (f32[4,64]{1,0:T(4,128)S(1)}, f32[4,64]{1,0:T(4,128)}, u32[]{:S(2)}) copy-start(f32[4,64]{1,0:T(4,128)} %param.68) | copy-start | bytes 3076
  1673.4 731.7 %copy-start.154 = (f32[4,64]{1,0:T(4,128)S(1)}, f32[4,64]{1,0:T(4,128)}, u32[]{:S(2)}) copy-start(f32[4,64]{1,0:T(4,128)} %param.67) | copy-start | bytes 3076
  1673.4 733.0 %copy-start.35 = (f32[64,1,6400]{2,1,0:T(1,128)S(1)}, f32[64,1,6400]{2,1,0:T(1,128)}, u32[]{:S(2)}) copy-start(f32[64,1,6400]{2,1,0:T(1,128)} %param.60) | copy-start | bytes 4915204
  1673.4 733.0 %copy-start.64 = (f32[64,1,6400]{2,1,0:T(1,128)S(1)}, f32[64,1,6400]{2,1,0:T(1,128)}, u32[]{:S(2)}) copy-start(f32[64,1,6400]{2,1,0:T(1,128)} %param.62) | copy-start | bytes 4915204
  (73 other events, 453.4 us)
Sparse Core Ops, SparseCore 0:
  60.9 6.9 all-gather.33
  70.5 158.1 all-gather.19
  339.0 9.2 all-gather.35
  413.7 11.3 all-gather.37
  447.3 11.4 all-gather.23
  462.0 69.3 all-gather.27
  533.5 9.5 all-gather.25
  555.3 162.8 reduce-scatter.21
  722.5 15.4 all-gather.29
  739.5 12.1 all-gather.21
  756.9 68.6 reduce-scatter.23
  834.9 16.6 all-gather.31
  861.9 227.4 reduce-scatter.25
  1095.5 24.0 reduce-scatter.27
  1159.3 11.4 all-gather.39
  1270.3 11.3 all-gather.41
  1283.9 11.1 reduce-scatter.29
  1297.7 77.2 reduce-scatter.33
  1382.1 206.6 all-reduce.17
  1591.6 75.6 reduce-scatter.31
  1673.7 677.7 all-reduce.15
where the time goes:
time: 2440 us; the launch traced here: 2430 us
  waiting for transfers between devices  1530 us (63%)
  matrix products  321 us (13%)
  local copies, waits for them, and re-layouts  210 us (9%)
  other arithmetic  164 us (7%)
  blocking collectives  159 us (7%)
    unnamed x30, waiting for transfers between devices  748 us
    reduce_scatter x4, waiting for transfers between devices, dec_sum(): lax.psum_scatter(partial_rows.astype(jnp.bfloat16), 'mp', scatter_dimensi...  458 us
    all_gather x1, waiting for transfers between devices, per_device(): lax.all_gather(low_weights[0], ('section', 'dp'), axis=0, tiled=True)  157 us
    unnamed x145, local copies, waits for them, and re-layouts  95.4 us
    dot_general x8, matrix products, head_backward(): jnp.einsum('gls,gms->glm', queries, key_rows, preferred_element_type=jnp....  53.7 us
  transfers between devices with their start and end apart: 28, of which 22 were waited for; matrix products, arithmetic and copies ran while one was open for 15% of the time, Pallas kernels for 0%

commit v1 on v0

v1 whole, which is shorter than its diff:
```python
import functools
import itertools
import math

import jax
import jax.numpy as jnp
from jax import lax
from jax.experimental import pallas as pl
from jax.experimental.pallas import tpu as pltpu
from jax.sharding import PartitionSpec as P

FF = 4096
FFD = 2048
GRID = 196
IMG = 12
PARAMS = 16259072

BETA_FIRST = 0.9
BETA_SECOND = 0.999
ADAM_EPS = 1e-08
WEIGHT_DECAY = 0.05
ROW_BLOCK = 240
GATHER_ORDERS = ("hlxy", "hlyx", "hlxy", "hlyx", "yxhl")
SCATTER_ORDERS = ("xylh", "yxlh", "xylh", "yxlh", "lhxy")

MESH_ID = pl.DeviceIdType.MESH
EVERY = slice(None)
BOTH = -1
DIMS = "xhly"


class Place:
    def __init__(self):
        s, depth, core = lax.axis_index("section"), lax.axis_index("dp"), lax.axis_index("mp")
        y, low, high = depth % 2, (depth // 2) % 2, depth // 4
        self.at = {"x": s, "h": high, "l": low, "y": y}
        self.s, self.core = s, core
        self.device = {
            "x": (1 - s, depth, core),
            "h": (s, depth + 4 - 8 * high, core),
            "l": (s, depth + 2 - 4 * low, core),
            "y": (s, depth + 1 - 2 * y, core),
        }

    def greet(self):
        barrier = pltpu.get_barrier_semaphore()
        for name in DIMS:
            pl.semaphore_signal(
                barrier, inc=1, device_id=self.device[name], device_id_type=MESH_ID
            )
        pl.semaphore_wait(barrier, len(DIMS))


def run(condition, action):
    if condition is None:
        action()
    else:
        pl.when(condition)(action)


def gather_kernel(chunks, n_in, n_out, ahead, *refs):
    ins, outs = refs[:n_in], refs[n_in : n_in + n_out]
    send, recv, local = refs[n_in + n_out :]
    here = Place()
    count = len(chunks)

    def region(chunk, gathered, sender):
        at = [
            EVERY if d in gathered else 1 - here.at[d] if d == sender else here.at[d] for d in DIMS
        ]
        return outs[chunk[1]].at[(*at, EVERY, pl.ds(chunk[3], chunk[4]))]

    def own(i):
        chunk = chunks[i]
        return pltpu.make_async_copy(
            ins[chunk[0]].at[:, pl.ds(chunk[2], chunk[4])], region(chunk, "", None), local.at[i]
        )

    def copy(i, stage, incoming):
        chunk = chunks[i]
        order = chunk[5]
        axis = order[stage]
        block = region(chunk, order[:stage], axis if incoming else None)
        source = block
        if stage == 0 and not incoming:
            source = ins[chunk[0]].at[:, pl.ds(chunk[2], chunk[4])]
        return pltpu.make_async_remote_copy(
            src_ref=source,
            dst_ref=block,
            send_sem=send.at[i, stage],
            recv_sem=recv.at[i, stage],
            device_id=here.device[axis],
            device_id_type=MESH_ID,
        )

    def roles(i, stage):
        order, owner = chunks[i][5], chunks[i][6]
        if owner == BOTH:
            return None, None
        if order[stage] == "x":
            return here.s != owner, here.s == owner
        if "x" in order[:stage]:
            return here.s == owner, here.s == owner
        return None, None

    def begin(i, stage):
        run(roles(i, stage)[0], lambda: copy(i, stage, False).start())

    def arrive(i, stage):
        run(roles(i, stage)[1], lambda: copy(i, stage, True).wait_recv())
        if stage == 0:
            own(i).wait()

    here.greet()
    for i in range(count):
        own(i).start()
    for i in range(min(ahead, count)):
        begin(i, 0)
    for step in range(count + 2):
        for stage in range(3):
            i = step - stage
            if not 0 <= i < count:
                continue
            arrive(i, stage)
            begin(i, stage + 1)
            if stage == 0 and i + ahead < count:
                begin(i + ahead, 0)
    for i in range(count):
        arrive(i, 3)
    for i in range(count):
        for stage in range(4):
            run(
                roles(i, stage)[0],
                lambda i=i, stage=stage: copy(i, stage, False).wait_send(),
            )


def gather_weights(shards, outputs, chunks, collective_id, ahead=4):
    count = len(chunks)
    call = pl.pallas_call(
        functools.partial(gather_kernel, chunks, len(shards), len(outputs), ahead),
        out_shape=[
            jax.ShapeDtypeStruct((2, 2, 2, 2, rows, width), dtype) for rows, width, dtype in outputs
        ],
        in_specs=[pl.BlockSpec(memory_space=pltpu.VMEM)] * len(shards),
        out_specs=[pl.BlockSpec(memory_space=pl.ANY)] * len(outputs),
        scratch_shapes=[
            pltpu.SemaphoreType.DMA((count, 4)),
            pltpu.SemaphoreType.DMA((count, 4)),
            pltpu.SemaphoreType.DMA((count,)),
        ],
        compiler_params=pltpu.CompilerParams(
            collective_id=collective_id, has_side_effects=True, vmem_limit_bytes=40 * 2**20
        ),
    )
    results = call(*shards)
    return [
        r.reshape(16 * rows, width) for r, (rows, width, _) in zip(results, outputs, strict=True)
    ]


def spread(total, pieces, unit=128):
    units = total // unit
    widths = [units // pieces + (1 if k < units % pieces else 0) for k in range(pieces)]
    return [w * unit for w in widths if w]


def chunk_list(widths, pieces, owner, orders):
    chunks = []
    column = turn = 0
    for index, (width, count) in enumerate(zip(widths, pieces, strict=True)):
        begin = 0
        for piece in spread(width, count):
            chunks.append((index, begin, column, piece, orders[turn % len(orders)], owner))
            begin += piece
            column += piece
            turn += 1
    return chunks


def left_after(order, stage):
    return [d for d in DIMS if d not in order[: stage + 1]]


def scatter_buffers(order, owner):
    shapes = [(2,) * 3]
    for stage in range(4):
        if order[stage] == "x" and owner != BOTH:
            continue
        shapes.append((2,) * (3 - stage))
    return shapes


def scatter_kernel(chunks, n_in, n_out, ahead, lag, *refs):
    ins, outs = refs[:n_in], refs[n_in : n_in + n_out]
    rest = refs[n_in + n_out :]
    send, recv, local = rest[:3]
    here = Place()
    s = here.s
    count = len(chunks)
    own, got = [], []
    position = 3
    for chunk in chunks:
        order, owner = chunk[5], chunk[6]
        own.append(rest[position])
        position += 1
        mine = []
        for stage in range(4):
            if order[stage] == "x" and owner != BOTH:
                mine.append(None)
                continue
            mine.append(rest[position])
            position += 1
        got.append(mine)

    def source(i, axis, keep):
        chunk = chunks[i]
        at = [
            (here.at[d] if keep else 1 - here.at[d]) if d == axis else EVERY for d in DIMS
        ]
        return ins[chunk[0]].at[(*at, EVERY, pl.ds(chunk[2], chunk[4]))]

    def load(i):
        return pltpu.make_async_copy(source(i, chunks[i][5][0], True), own[i], local.at[i])

    def spot(i, stage, flip):
        order = chunks[i][5]
        at = []
        for d in DIMS:
            if d == order[0]:
                continue
            if d in order[:stage]:
                at.append(here.at[d])
            elif d == order[stage]:
                at.append(1 - here.at[d] if flip else here.at[d])
            else:
                at.append(EVERY)
        return tuple(at)

    def copy(i, stage, incoming):
        order = chunks[i][5]
        axis = order[stage]
        moved = got[i][stage] is None
        src = source(i, axis, False) if stage == 0 else own[i].at[spot(i, stage, True)]
        if not moved:
            there = mine = got[i][stage]
        elif stage == 0:
            there = mine = own[i]
        else:
            there, mine = own[i].at[spot(i, stage, True)], own[i].at[spot(i, stage, False)]
        return pltpu.make_async_remote_copy(
            src_ref=mine if incoming else src,
            dst_ref=mine if incoming else there,
            send_sem=send.at[i, stage],
            recv_sem=recv.at[i, stage],
            device_id=here.device[axis],
            device_id_type=MESH_ID,
        )

    def roles(i, stage):
        order, owner = chunks[i][5], chunks[i][6]
        if owner == BOTH:
            return None, None
        if order[stage] == "x":
            return s == owner, s != owner
        if "x" in order[:stage]:
            return None, None
        return s == owner, s == owner

    def begin(i, stage):
        run(roles(i, stage)[0], lambda: copy(i, stage, False).start())

    def arrive(i, stage):
        chunk, a, r = chunks[i], own[i], got[i][stage]
        order, owner = chunk[5], chunk[6]
        run(roles(i, stage)[1], lambda: copy(i, stage, True).wait_recv())
        if stage == 0:
            run(None if owner == BOTH else s == owner, lambda: load(i).wait())
        out = outs[chunk[1]].at[:, pl.ds(chunk[3], chunk[4])]
        place = spot(i, stage, False)
        if stage == 3:
            result = a[place].astype(jnp.float32)
            if r is not None:
                result = result + r[...].astype(jnp.float32)
            out[...] = result
            return
        if r is None:
            return

        def add():
            free = [k for k, p in enumerate(place) if p is EVERY]
            for combo in itertools.product(range(2), repeat=len(free)):
                at = list(place)
                for k, c in zip(free, combo):
                    at[k] = c
                at = tuple(at)
                a[at] = (a[at].astype(jnp.float32) + r[combo].astype(jnp.float32)).astype(a.dtype)

        run(roles(i, stage)[1], add)

    here.greet()
    for i in range(count):
        run(
            None if chunks[i][6] == BOTH else s == chunks[i][6],
            lambda i=i: load(i).start(),
        )
    for i in range(min(ahead, count)):
        begin(i, 0)
    for step in range(count + 3 * lag):
        for stage in range(3, -1, -1):
            i = step - stage * lag
            if not 0 <= i < count:
                continue
            arrive(i, stage)
            if stage < 3:
                begin(i, stage + 1)
            if stage == 0 and i + ahead < count:
                begin(i + ahead, 0)
    for i in range(count):
        for stage in range(4):
            run(
                roles(i, stage)[0],
                lambda i=i, stage=stage: copy(i, stage, False).wait_send(),
            )


def scatter_grads(parts, outputs, chunks, collective_id, ahead=4, lag=1):
    count = len(chunks)
    views = [p.reshape(2, 2, 2, 2, p.shape[0] // 16, p.shape[1]) for p in parts]
    buffers = []
    for chunk in chunks:
        view = views[chunk[0]]
        for lead in scatter_buffers(chunk[5], chunk[6]):
            buffers.append(pltpu.VMEM((*lead, view.shape[4], chunk[4]), view.dtype))
    call = pl.pallas_call(
        functools.partial(scatter_kernel, chunks, len(parts), len(outputs), ahead, lag),
        out_shape=[jax.ShapeDtypeStruct((rows, width), jnp.float32) for rows, width in outputs],
        in_specs=[pl.BlockSpec(memory_space=pl.ANY)] * len(parts),
        out_specs=[pl.BlockSpec(memory_space=pltpu.VMEM)] * len(outputs),
        scratch_shapes=[
            pltpu.SemaphoreType.DMA((count, 4)),
            pltpu.SemaphoreType.DMA((count, 4)),
            pltpu.SemaphoreType.DMA((count,)),
            *buffers,
        ],
        compiler_params=pltpu.CompilerParams(
            collective_id=collective_id, has_side_effects=True, vmem_limit_bytes=56 * 2**20
        ),
    )
    return call(*views)


HEADS = 16
NORM_EPS = 1e-06
MASKED = -1e30
LOW = jnp.bfloat16
WIDE = jnp.float32


def mm(left, right, left_dim=1, right_dim=0):
    return lax.dot_general(
        left, right, (((left_dim,), (right_dim,)), ((), ())), preferred_element_type=WIDE
    )


def centre(tokens):
    average = jnp.mean(tokens, axis=-1, keepdims=True)
    centred = tokens - average
    spread_ = jnp.mean(centred * centred, axis=-1, keepdims=True)
    scale = lax.rsqrt(spread_ + NORM_EPS)
    return centred * scale, scale


def centre_back(unit, scale, gain, grad):
    pulled = grad * gain
    first = jnp.mean(pulled, axis=-1, keepdims=True)
    second = jnp.mean(pulled * unit, axis=-1, keepdims=True)
    return scale * (pulled - first - unit * second)


def gelu_pair(z):
    cdf = 0.5 * (1.0 + lax.erf(z * math.sqrt(0.5)))
    return z * cdf, cdf + z * (jnp.exp(-0.5 * z * z) * (1.0 / math.sqrt(2.0 * math.pi)))


def decoder_kernel(
    grid_cells,
    length,
    target_row,
    target_column,
    visible,
    mask,
    position,
    gains,
    qkv_t,
    qkv_w,
    out_t,
    out_w,
    up_w,
    down_w,
    cotangent,
    decoded,
    grad_visible,
    grad_qkv,
    grad_out,
    grad_up,
    grad_down,
    grad_gains,
    qkv_rows,
    shares,
    mixture,
    hidden,
    slope,
    grad_rows,
):
    image = pl.program_id(0)
    rows, width = decoded.shape[1], decoded.shape[2]
    head = width // HEADS
    units = hidden.shape[1]
    scaling = head ** (-0.5)

    @pl.when(image == 0)
    def _():
        for ref in (grad_visible, grad_qkv, grad_out, grad_up, grad_down, grad_gains):
            ref[...] = jnp.zeros_like(ref)

    packed = target_row.shape[1]
    cell = lax.broadcasted_iota(jnp.int32, (rows, packed), 0)
    wanted = jnp.where(cell < length, cell + image * length, -7)
    chosen = (target_row[...] == wanted).astype(WIDE)
    seen = jnp.max(chosen, axis=1, keepdims=True)
    placed = mm(chosen.astype(LOW), visible[...])
    stream = jnp.where(seen > 0.0, placed, mask[...]) + position[...]

    unit_one, scale_one = centre(stream)
    first = (unit_one * gains[0:1] + gains[1:2]).astype(LOW)
    qkv_rows[...] = mm(qkv_t[...], first, 1, 1).astype(LOW)

    key_index = lax.broadcasted_iota(jnp.int32, (rows, rows), 0)

    def attend(h, carry):
        begin = pl.multiple_of(h * head, head)
        q = qkv_rows[pl.ds(begin, head), :]
        k = qkv_rows[pl.ds(pl.multiple_of(width + begin, head), head), :]
        v = qkv_rows[pl.ds(pl.multiple_of(2 * width + begin, head), head), :]
        scores = mm(k, q, 0, 0) * scaling
        scores = jnp.where(key_index < length, scores, MASKED)
        weights = jnp.exp(scores - jnp.max(scores, axis=0, keepdims=True))
        share = weights * (1.0 / jnp.sum(weights, axis=0, keepdims=True))
        shares[h] = share
        mixture[pl.ds(begin, head), :] = mm(v, share.astype(LOW)).astype(LOW)
        return carry

    lax.fori_loop(0, HEADS, attend, 0, unroll=4)
    mixed = mixture[...]
    after = stream + mm(jnp.transpose(mixed), out_w[...], 1, 1)
    unit_two, scale_two = centre(after)
    second = (unit_two * gains[2:3] + gains[3:4]).astype(LOW)
    piece = 256
    result = after
    for c in range(0, units, piece):
        z = mm(second, up_w[:, c : c + piece])
        h, g = gelu_pair(z)
        hidden[:, c : c + piece] = h.astype(LOW)
        slope[:, c : c + piece] = g
    decoded[0] = after + mm(hidden[...], down_w[...], 1, 1)

    grad_low = cotangent[0]
    grad_result = grad_low.astype(WIDE)
    turned = jnp.transpose(grad_low)
    second_turned = jnp.transpose(second)
    for c in range(0, units, piece):
        cut = slice(c, c + piece)
        grad_down[:, cut] += mm(turned, hidden[:, cut])
        grad_z = (mm(grad_low, down_w[:, cut]) * slope[:, cut]).astype(LOW)
        hidden[:, cut] = grad_z
        grad_up[:, cut] += mm(second_turned, grad_z)
    grad_second = mm(hidden[...], up_w[...], 1, 1)
    grad_after = grad_result + centre_back(unit_two, scale_two, gains[2:3], grad_second)
    grad_gains[2:3] += jnp.sum(grad_second * unit_two, axis=0, keepdims=True)
    grad_gains[3:4] += jnp.sum(grad_second, axis=0, keepdims=True)

    after_low = grad_after.astype(LOW)
    grad_out[...] += mm(mixed, after_low)
    grad_rows[...] = mm(out_t[...], after_low, 1, 1).astype(LOW)

    def attend_back(h, carry):
        begin = pl.multiple_of(h * head, head)
        key_at = pl.multiple_of(width + begin, head)
        value_at = pl.multiple_of(2 * width + begin, head)
        q = qkv_rows[pl.ds(begin, head), :]
        k = qkv_rows[pl.ds(key_at, head), :]
        v = qkv_rows[pl.ds(value_at, head), :]
        grad_mixture = grad_rows[pl.ds(begin, head), :]
        share = shares[h]
        grad_share = mm(v, grad_mixture, 0, 0)
        grad_value = mm(grad_mixture, share.astype(LOW), 1, 1)
        inner = jnp.sum(share * grad_share, axis=0, keepdims=True)
        grad_score = (share * (grad_share - inner)).astype(LOW)
        grad_query = mm(k, grad_score) * scaling
        grad_key = mm(q, grad_score, 1, 1) * scaling
        qkv_rows[pl.ds(begin, head), :] = grad_query.astype(LOW)
        qkv_rows[pl.ds(key_at, head), :] = grad_key.astype(LOW)
        qkv_rows[pl.ds(value_at, head), :] = grad_value.astype(LOW)
        return carry

    lax.fori_loop(0, HEADS, attend_back, 0, unroll=4)
    grads = qkv_rows[...]
    grad_qkv[...] += mm(grads, first)
    grad_first = jnp.transpose(mm(qkv_w[...], grads))
    grad_stream = grad_after + centre_back(unit_one, scale_one, gains[0:1], grad_first)
    grad_gains[0:1] += jnp.sum(grad_first * unit_one, axis=0, keepdims=True)
    grad_gains[1:2] += jnp.sum(grad_first, axis=0, keepdims=True)

    cell_lane = lax.broadcasted_iota(jnp.int32, (packed, rows), 1)
    wanted_lane = jnp.where(cell_lane < length, cell_lane + image * length, -7)
    chosen_back = (target_column[...] == wanted_lane).astype(WIDE).astype(LOW)
    grad_visible[...] += mm(chosen_back, grad_stream.astype(LOW))


def decoder_step(
    visible, target, mask, position, gains, qkv_w, out_w, up_w, down_w, cotangent, images
):
    length, width = position.shape
    rows = -(-length // 16) * 16
    packed = -(-visible.shape[0] // 128) * 128
    spare = packed - visible.shape[0]
    units = up_w.shape[1]
    visible = jnp.pad(visible, ((0, spare), (0, 0)))
    target = jnp.pad(target, (0, spare), constant_values=-1)
    longer = ((0, 0), (0, rows - length), (0, 0))
    cotangent = jnp.pad(cotangent.reshape(images, length, width), longer)
    position = jnp.pad(position, ((0, rows - length), (0, 0)))

    def fixed(shape):
        return pl.BlockSpec(shape, lambda i: (0,) * len(shape), pipeline_mode=pl.Buffered(1))

    per_image = pl.BlockSpec((1, rows, width), lambda i: (i, 0, 0))
    grads = [
        ((packed, width), WIDE),
        ((3 * width, width), WIDE),
        ((width, width), WIDE),
        ((width, units), WIDE),
        ((width, units), WIDE),
        ((8, width), WIDE),
    ]
    results = pl.pallas_call(
        functools.partial(decoder_kernel, images * length, length),
        grid=(images,),
        out_shape=[jax.ShapeDtypeStruct((images, rows, width), WIDE)]
        + [jax.ShapeDtypeStruct(s, d) for s, d in grads],
        in_specs=[
            fixed((1, packed)),
            fixed((packed, 1)),
            fixed((packed, width)),
            fixed((1, width)),
            fixed((rows, width)),
            fixed((4, width)),
            fixed((3 * width, width)),
            fixed((width, 3 * width)),
            fixed((width, width)),
            fixed((width, width)),
            fixed((width, units)),
            fixed((width, units)),
            per_image,
        ],
        out_specs=[per_image] + [fixed(s) for s, _ in grads],
        scratch_shapes=[
            pltpu.VMEM((3 * width, rows), LOW),
            pltpu.VMEM((HEADS, rows, rows), WIDE),
            pltpu.VMEM((width, rows), LOW),
            pltpu.VMEM((rows, units), LOW),
            pltpu.VMEM((rows, units), WIDE),
            pltpu.VMEM((width, rows), LOW),
        ],
        compiler_params=pltpu.CompilerParams(
            dimension_semantics=("arbitrary",), vmem_limit_bytes=60 * 2**20
        ),
    )(
        target[None, :],
        target[:, None],
        visible,
        mask[None, :],
        position,
        gains,
        qkv_w.T,
        qkv_w,
        out_w.T,
        out_w,
        up_w,
        down_w,
        cotangent,
    )
    decoded, grad_visible, grad_qkv, grad_out, grad_up, grad_down, grad_gains = results
    return (
        decoded[:, :length].reshape(images * length, width),
        grad_visible[: packed - spare],
        grad_qkv,
        grad_out,
        grad_up,
        grad_down,
        grad_gains[:4],
    )


TILE = 256
GROUP = 4


def fixed(shape):
    return pl.BlockSpec(shape, lambda i: (0,) * len(shape), pipeline_mode=pl.Buffered(1))


def down_rows(rows, width):
    return pl.BlockSpec((rows, width), lambda i: (i, 0))


def params(megabytes=60):
    return pltpu.CompilerParams(
        dimension_semantics=("arbitrary",), vmem_limit_bytes=megabytes * 2**20
    )


def attend_kernel(
    head, bounds, stream, slots_row, slots_column, gains, qkv_w, out_w, first, turned, mixture, log_sum, partial
):
    rows, width = stream.shape
    part, lanes = mixture.shape
    tiles = lanes // TILE
    scaling = head ** (-0.5)
    unit, _ = centre(stream[...].astype(WIDE))
    first[...] = (unit * gains[0:1] + gains[1:2]).astype(LOW)
    turned[:, rows:] = jnp.zeros((3 * part, lanes - rows), LOW)
    for c in range(0, 3 * part, TILE):
        weight = jnp.transpose(qkv_w[:, c : c + TILE])
        turned[c : c + TILE, :rows] = mm(weight, first[...], 1, 1).astype(LOW)

    def at(which, h, tile):
        return (
            pl.ds(pl.multiple_of(which * part + h * head, head), head),
            pl.ds(pl.multiple_of(tile * TILE, TILE), TILE),
        )

    def step(n, carry):
        group, i = n // tiles, n % tiles
        heads = [group * GROUP + g for g in range(GROUP)]
        lane_i = pl.ds(pl.multiple_of(i * TILE, TILE), TILE)
        queries = [turned[at(0, h, i)] for h in heads]
        slot_i = slots_row[:, lane_i]

        def inner(j, state):
            same = slots_column[pl.ds(pl.multiple_of(j * TILE, TILE), TILE), :] == slot_i
            result = []
            for g, h in enumerate(heads):
                high, total, mixed = state[g]
                scores = mm(turned[at(1, h, j)], queries[g], 0, 0) * scaling
                scores = jnp.where(same, scores, MASKED)
                higher = jnp.maximum(high, jnp.max(scores, axis=0, keepdims=True))
                weights = jnp.exp(scores - higher)
                fix = jnp.exp(high - higher)
                total = total * fix + jnp.sum(weights, axis=0, keepdims=True)
                mixed = mixed * fix + mm(turned[at(2, h, j)], weights.astype(LOW))
                result.append((higher, total, mixed))
            return tuple(result)

        begin = (
            jnp.full((1, TILE), MASKED, WIDE),
            jnp.zeros((1, TILE), WIDE),
            jnp.zeros((head, TILE), WIDE),
        )
        state = lax.fori_loop(bounds[i, 0], bounds[i, 1], inner, (begin,) * GROUP)
        for g, h in enumerate(heads):
            high, total, mixed = state[g]
            mixture[at(0, h, i)] = (mixed / total).astype(LOW)
            log_sum[pl.ds(h, 1), lane_i] = high + jnp.log(total)
        return carry

    lax.fori_loop(0, part // head // GROUP * tiles, step, 0)
    mixed = jnp.transpose(mixture[...])[:rows]
    for c in range(0, width, TILE):
        partial[:, c : c + TILE] = mm(mixed, out_w[c : c + TILE, :], 1, 1).astype(LOW)


def encoder_attend(stream, slots, bounds, gains, qkv_w, out_w, head):
    rows, width = stream.shape
    lanes = slots.shape[0]
    part = out_w.shape[1]
    return pl.pallas_call(
        functools.partial(attend_kernel, head),
        in_specs=[pl.BlockSpec(memory_space=pltpu.SMEM)]
        + [pl.BlockSpec(memory_space=pltpu.VMEM)] * 6,
        out_specs=[pl.BlockSpec(memory_space=pltpu.VMEM)] * 5,
        out_shape=[
            jax.ShapeDtypeStruct((rows, width), LOW),
            jax.ShapeDtypeStruct((3 * part, lanes), LOW),
            jax.ShapeDtypeStruct((part, lanes), LOW),
            jax.ShapeDtypeStruct((part // head, lanes), WIDE),
            jax.ShapeDtypeStruct((rows, width), LOW),
        ],
        compiler_params=pltpu.CompilerParams(vmem_limit_bytes=60 * 2**20),
    )(bounds, stream, slots[None, :], slots[:, None], gains, qkv_w, out_w)


def attend_back_kernel(
    head,
    bounds,
    slots_row,
    slots_column,
    first,
    turned,
    mixture,
    log_sum,
    grad_low,
    qkv_w,
    out_w,
    grad_qkv_w,
    grad_out_w,
    partial,
    grad_mixture,
    grad_turned,
    inner_sum,
    key_sum,
    value_sum,
):
    rows, width = grad_low.shape
    part, lanes = mixture.shape
    tiles = lanes // TILE
    scaling = head ** (-0.5)
    grad_mixture[:, rows:] = jnp.zeros((part, lanes - rows), LOW)
    for c in range(0, width, TILE):
        grad_out_w[c : c + TILE, :] = jnp.transpose(
            mm(mixture[:, :rows], grad_low[:, c : c + TILE]).astype(LOW)
        )
    for c in range(0, part, TILE):
        weight = jnp.transpose(out_w[:, c : c + TILE])
        grad_mixture[c : c + TILE, :rows] = mm(weight, grad_low[...], 1, 1).astype(LOW)
    for h in range(part // head):
        cut = slice(h * head, (h + 1) * head)
        inner_sum[h : h + 1, :] = jnp.sum(
            grad_mixture[cut, :].astype(WIDE) * mixture[cut, :].astype(WIDE), axis=0, keepdims=True
        )

    def at(which, h, tile):
        return (
            pl.ds(pl.multiple_of(which * part + h * head, head), head),
            pl.ds(pl.multiple_of(tile * TILE, TILE), TILE),
        )

    def over_group(group, carry):
        heads = [group * GROUP + g for g in range(GROUP)]
        key_sum[...] = jnp.zeros_like(key_sum)
        value_sum[...] = jnp.zeros_like(value_sum)

        def over_queries(i, carry):
            lane_i = pl.ds(pl.multiple_of(i * TILE, TILE), TILE)
            slot_i = slots_row[:, lane_i]
            queries = [turned[at(0, h, i)] for h in heads]
            grads = [grad_mixture[at(0, h, i)] for h in heads]
            logs = [log_sum[pl.ds(h, 1), lane_i] for h in heads]
            sums = [inner_sum[pl.ds(h, 1), lane_i] for h in heads]

            def inner(j, state):
                lane_j = pl.ds(pl.multiple_of(j * TILE, TILE), TILE)
                same = slots_column[lane_j, :] == slot_i
                result = []
                for g, h in enumerate(heads):
                    cut = slice(g * head, (g + 1) * head)
                    keys, values = turned[at(1, h, j)], turned[at(2, h, j)]
                    scores = jnp.where(same, mm(keys, queries[g], 0, 0) * scaling, MASKED)
                    share = jnp.exp(scores - logs[g])
                    grad_share = mm(values, grads[g], 0, 0)
                    grad_score = (share * (grad_share - sums[g])).astype(LOW)
                    value_sum[cut, lane_j] += mm(grads[g], share.astype(LOW), 1, 1)
                    key_sum[cut, lane_j] += mm(queries[g], grad_score, 1, 1)
                    result.append(state[g] + mm(keys, grad_score))
                return tuple(result)

            begin = (jnp.zeros((head, TILE), WIDE),) * GROUP
            state = lax.fori_loop(bounds[i, 0], bounds[i, 1], inner, begin)
            for g, h in enumerate(heads):
                grad_turned[at(0, h, i)] = (state[g] * scaling).astype(LOW)
            return carry

        lax.fori_loop(0, tiles, over_queries, 0)
        size = GROUP * head
        key_at = pl.ds(pl.multiple_of(part + group * size, size), size)
        value_at = pl.ds(pl.multiple_of(2 * part + group * size, size), size)
        grad_turned[key_at, :] = (key_sum[...] * scaling).astype(LOW)
        grad_turned[value_at, :] = value_sum[...].astype(LOW)
        return carry

    lax.fori_loop(0, part // head // GROUP, over_group, 0)
    for c in range(0, 3 * part, TILE):
        grad_qkv_w[:, c : c + TILE] = jnp.transpose(
            mm(grad_turned[c : c + TILE, :rows], first[...]).astype(LOW)
        )
    for c in range(0, width, TILE):
        partial[:, c : c + TILE] = jnp.transpose(
            mm(qkv_w[c : c + TILE, :], grad_turned[:, :rows]).astype(LOW)
        )


def encoder_attend_back(
    slots, bounds, first, turned, mixture, log_sum, grad_low, qkv_w, out_w, head
):
    rows, width = first.shape
    part, lanes = mixture.shape
    return pl.pallas_call(
        functools.partial(attend_back_kernel, head),
        in_specs=[pl.BlockSpec(memory_space=pltpu.SMEM)]
        + [pl.BlockSpec(memory_space=pltpu.VMEM)] * 9,
        out_specs=[pl.BlockSpec(memory_space=pltpu.VMEM)] * 3,
        out_shape=[
            jax.ShapeDtypeStruct((width, 3 * part), LOW),
            jax.ShapeDtypeStruct((width, part), LOW),
            jax.ShapeDtypeStruct((rows, width), LOW),
        ],
        scratch_shapes=[
            pltpu.VMEM((part, lanes), LOW),
            pltpu.VMEM((3 * part, lanes), LOW),
            pltpu.VMEM((part // head, lanes), WIDE),
            pltpu.VMEM((GROUP * head, lanes), WIDE),
            pltpu.VMEM((GROUP * head, lanes), WIDE),
        ],
        compiler_params=pltpu.CompilerParams(vmem_limit_bytes=60 * 2**20),
    )(
        bounds,
        slots[None, :],
        slots[:, None],
        first,
        turned,
        mixture,
        log_sum,
        grad_low,
        qkv_w,
        out_w,
    )


def feed_kernel(stream, own, other, gains, up_w, down_w, after, second, hidden, slope, partial):
    summed = stream[...].astype(WIDE) + (own[...].astype(WIDE) + other[...].astype(WIDE))
    after[...] = summed
    unit, _ = centre(summed)
    second[...] = (unit * gains[2:3] + gains[3:4]).astype(LOW)
    units = up_w.shape[1]
    for c in range(0, units, TILE):
        cut = slice(c, c + TILE)
        h, g = gelu_pair(mm(second[...], up_w[:, cut]))
        hidden[:, cut] = h.astype(LOW)
        slope[:, cut] = g.astype(LOW)
    partial[...] = mm(hidden[...], down_w[...], 1, 1).astype(LOW)


def encoder_feed(stream, own, other, gains, up_w, down_w, block):
    rows, width = stream.shape
    units = up_w.shape[1]
    wide, tall = down_rows(block, width), down_rows(block, units)
    return pl.pallas_call(
        feed_kernel,
        grid=(rows // block,),
        in_specs=[wide, wide, wide, fixed((4, width)), fixed(up_w.shape), fixed(down_w.shape)],
        out_specs=[wide, wide, tall, tall, wide],
        out_shape=[
            jax.ShapeDtypeStruct((rows, width), WIDE),
            jax.ShapeDtypeStruct((rows, width), LOW),
            jax.ShapeDtypeStruct((rows, units), LOW),
            jax.ShapeDtypeStruct((rows, units), LOW),
            jax.ShapeDtypeStruct((rows, width), LOW),
        ],
        compiler_params=params(),
    )(stream, own, other, gains, up_w, down_w)


def feed_back_kernel(
    own,
    other,
    second,
    hidden,
    slope,
    up_w,
    down_w,
    grad_up,
    grad_down,
    partial,
    grad_low,
    grad_turned,
    second_turned,
    total,
):
    @pl.when(pl.program_id(0) == 0)
    def _():
        grad_low[...] = (own[...].astype(WIDE) + other[...].astype(WIDE)).astype(LOW)
        grad_turned[...] = jnp.transpose(grad_low[...])
        second_turned[...] = jnp.transpose(second[...])
        total[...] = jnp.zeros_like(total)

    grad_down[...] = mm(grad_turned[...], hidden[...]).astype(LOW)
    grad_z = (mm(grad_low[...], down_w[...]) * slope[...].astype(WIDE)).astype(LOW)
    grad_up[...] = mm(second_turned[...], grad_z).astype(LOW)
    total[...] += mm(grad_z, up_w[...], 1, 1)

    @pl.when(pl.program_id(0) == pl.num_programs(0) - 1)
    def _():
        partial[...] = total[...].astype(LOW)


def encoder_feed_back(own, other, second, hidden, slope, up_w, down_w):
    rows, width = own.shape
    units = up_w.shape[1]
    piece = 256
    whole = fixed((rows, width))
    tall = pl.BlockSpec((rows, piece), lambda i: (0, i))
    weight = pl.BlockSpec((width, piece), lambda i: (0, i))
    return pl.pallas_call(
        feed_back_kernel,
        grid=(units // piece,),
        in_specs=[whole, whole, whole, tall, tall, weight, weight],
        out_specs=[weight, weight, whole],
        out_shape=[
            jax.ShapeDtypeStruct((width, units), LOW),
            jax.ShapeDtypeStruct((width, units), LOW),
            jax.ShapeDtypeStruct((rows, width), LOW),
        ],
        scratch_shapes=[
            pltpu.VMEM((rows, width), LOW),
            pltpu.VMEM((width, rows), LOW),
            pltpu.VMEM((width, rows), LOW),
            pltpu.VMEM((rows, width), WIDE),
        ],
        compiler_params=params(),
    )(own, other, second, hidden, slope, up_w, down_w)


def norm_back_kernel(tokens, own, other, skip_own, skip_other, gains, grad, grad_low, grad_gains, *, at):
    @pl.when(pl.program_id(0) == 0)
    def _():
        grad_gains[...] = jnp.zeros_like(grad_gains)

    pulled = own[...].astype(WIDE) + other[...].astype(WIDE)
    unit, scale = centre(tokens[...].astype(WIDE))
    result = skip_own[...].astype(WIDE)
    if skip_other is not None:
        result = result + skip_other[...].astype(WIDE)
    result = result + centre_back(unit, scale, gains[at : at + 1], pulled)
    grad[...] = result
    if grad_low is not None:
        grad_low[...] = result.astype(LOW)
    grad_gains[0:1] += jnp.sum(pulled * unit, axis=0, keepdims=True)
    grad_gains[1:2] += jnp.sum(pulled, axis=0, keepdims=True)


def encoder_norm_back(tokens, own, other, skip, gains, at, block, low):
    rows, width = tokens.shape
    wide = down_rows(block, width)
    two = len(skip) == 2

    def kernel(*refs):
        refs = list(refs)
        if not two:
            refs.insert(4, None)
        if not low:
            refs.insert(7, None)
        norm_back_kernel(*refs, at=at)

    shapes = [jax.ShapeDtypeStruct((rows, width), WIDE)]
    if low:
        shapes.append(jax.ShapeDtypeStruct((rows, width), LOW))
    shapes.append(jax.ShapeDtypeStruct((8, width), WIDE))
    return pl.pallas_call(
        kernel,
        grid=(rows // block,),
        in_specs=[wide, wide, wide] + [wide] * len(skip) + [fixed((4, width))],
        out_specs=[wide] * (2 if low else 1) + [fixed((8, width))],
        out_shape=shapes,
        compiler_params=params(),
    )(tokens, own, other, *skip, gains)


def from_behind(value, axis, by):
    length = lax.axis_size(axis)
    pairs = [(i, i + by) for i in range(length) if 0 <= i + by < length]
    return lax.ppermute(value, axis, pairs)


def partner(value):
    length = lax.axis_size("mp")
    return lax.ppermute(value, "mp", [(i, (i + 1) % length) for i in range(length)])


def on_side(active, action, *operands):
    def skipped(*values):
        return jax.tree.map(
            lambda leaf: jnp.zeros(leaf.shape, leaf.dtype), jax.eval_shape(action, *values)
        )

    return lax.cond(active, action, skipped, *operands)


def is_fast():
    return lax.axis_size("section") == 2 and lax.axis_size("dp") == 8


def plan(widths, pieces, dec_width, dec_pieces, orders):
    enc = chunk_list(widths, pieces, 0, orders)
    dec = [
        (len(widths), b, c, w, o, k)
        for _, b, c, w, o, k in chunk_list((dec_width,), (dec_pieces,), 1, orders)
    ]
    return enc[:8] + dec + enc[8:]


def gather_all(low_enc, low_dec, norms, widths):
    count = len(widths)
    if not is_fast():
        both = ("section", "dp")
        enc = lax.all_gather(low_enc, both, axis=0, tiled=True)
        dec = lax.all_gather(low_dec, both, axis=0, tiled=True)
        rows = lax.all_gather(norms, both, axis=0, tiled=True)
        parts, column = [], 0
        for w in widths:
            parts.append(enc[:, column : column + w])
            column += w
        return parts, dec, rows
    chunks = plan(widths, (4, 1, 4, 4, 2), low_dec.shape[1], 4, GATHER_ORDERS)
    outputs = [(low_enc.shape[0], w, LOW) for w in widths]
    outputs += [(low_dec.shape[0], low_dec.shape[1], LOW), (8, 128, WIDE)]
    described = [(k // count, k, c, b, w, o, own) for k, b, c, w, o, own in chunks]
    described.append((2, count + 1, 0, 0, 128, "hlyx", BOTH))
    results = gather_weights([low_enc, low_dec, norms], outputs, described, 1, 8)
    return results[:count], results[count], results[count + 1]


def scatter_all(enc_parts, dec, norms, encoder_side):
    widths = [p.shape[1] for p in enc_parts]
    count = len(widths)
    if not is_fast():
        both = ("section", "dp")
        enc = jnp.concatenate(enc_parts, axis=1).astype(WIDE)
        enc = jnp.where(encoder_side, enc, 0.0)
        dec = jnp.where(encoder_side, 0.0, dec.astype(WIDE))
        return [
            lax.psum_scatter(v, both, scatter_dimension=0, tiled=True) for v in (enc, dec, norms)
        ]
    chunks = plan(widths, (4, 1, 4, 4, 2), dec.shape[1], 4, SCATTER_ORDERS)
    described = [(k, k // count, b, c, w, o, own) for k, b, c, w, o, own in chunks]
    described.append((count + 1, 2, 0, 0, 128, "xylh", BOTH))
    rows = enc_parts[0].shape[0] // 16
    outputs = [(rows, sum(widths)), (dec.shape[0] // 16, dec.shape[1]), (8, 128)]
    return scatter_grads([*enc_parts, dec, norms], outputs, described, 2, 8, 2)


def pack_norms(enc_rows, dec_rows, blocks):
    both = [rows.reshape(4, blocks, -1).transpose(1, 0, 2) for rows in (enc_rows, dec_rows)]
    joined = jnp.concatenate(both, axis=2)
    joined = jnp.pad(joined, ((0, 0), (0, 4), (0, 128 - joined.shape[2])))
    return joined.reshape(blocks * 8, 128)


def unpack_norms(packed, blocks, enc_width, dec_width):
    split = packed.reshape(blocks, 8, 128)[:, :4].transpose(1, 0, 2)
    return (
        split[:, :, :enc_width].reshape(4, -1),
        split[:, :, enc_width : enc_width + dec_width].reshape(4, -1),
    )


def key_ranges(slots):
    tiles = slots.reshape(-1, TILE)
    low, high = jnp.min(tiles, axis=1), jnp.max(tiles, axis=1)
    meet = jnp.logical_and(low[:, None] <= high[None, :], high[:, None] >= low[None, :])
    index = jnp.arange(tiles.shape[0], dtype=jnp.int32)[None, :]
    first = jnp.min(jnp.where(meet, index, tiles.shape[0]), axis=1)
    last = jnp.max(jnp.where(meet, index + 1, 0), axis=1)
    return jnp.stack([first, last], axis=1)


def cut_columns(matrix, widths):
    parts, column = [], 0
    for w in widths:
        parts.append(matrix[:, column : column + w])
        column += w
    return parts


def update(
    weight,
    first_moment,
    second_moment,
    gradient,
    factor,
    step_rate,
    fix_first,
    fix_second,
    decay_rate,
):
    clipped = gradient * factor
    new_first = BETA_FIRST * first_moment + (1.0 - BETA_FIRST) * clipped
    new_second = BETA_SECOND * second_moment + (1.0 - BETA_SECOND) * clipped * clipped
    stepped = new_first / fix_first / (jnp.sqrt(new_second / fix_second) + ADAM_EPS)
    return weight - step_rate * (stepped + decay_rate * weight)


def per_device(
    act_in,
    packing,
    enc_weights,
    enc_first,
    enc_second,
    dec_weights,
    dec_first,
    dec_second,
    enc_norms,
    enc_norm_first,
    enc_norm_second,
    dec_norms,
    dec_norm_first,
    dec_norm_second,
    mask_token,
    dec_position,
    learning_rate,
    step_count,
):
    encoder_side = lax.axis_index("section") == 0
    decoder_side = jnp.logical_not(encoder_side)
    mp_rank = lax.axis_index("mp")
    mp_count = lax.axis_size("mp")
    first_half = mp_rank == 0
    slot_ids = packing[0, 0]
    patch_ids = packing[0, 1]
    local_images = IMG // mp_count
    grid_cells = local_images * GRID
    local_slot = slot_ids - mp_rank * local_images
    inside = jnp.logical_and(local_slot >= 0, local_slot < local_images)
    target = jnp.where(inside, local_slot * GRID + patch_ids, grid_cells)

    local_rows, width = act_in.shape[1], act_in.shape[2]
    real_rows = local_rows * mp_count
    rows = -(-real_rows // ROW_BLOCK) * ROW_BLOCK
    lanes = -(-rows // TILE) * TILE
    part = width // mp_count
    units = FF // mp_count
    head = width // HEADS
    dec_width = dec_position.shape[1]
    dec_part = dec_width // mp_count
    dec_units = FFD // mp_count
    widths = (3 * part, part, units, units, dec_part)
    dec_widths = (dec_part,) * 4 + (dec_units,) * 2
    slots = jnp.pad(slot_ids, (0, lanes - real_rows), constant_values=IMG + 1)
    ranges = key_ranges(slots)

    def halves(own, other, axis):
        return jnp.where(
            first_half,
            jnp.concatenate([own, other], axis=axis),
            jnp.concatenate([other, own], axis=axis),
        )

    (qkv_w, out_w, up_w, down_w, projection), dec_own, norm_rows = gather_all(
        enc_weights[:, 0, :].astype(LOW),
        dec_weights[:, 0, :].astype(LOW),
        pack_norms(enc_norms, dec_norms, 1),
        widths,
    )
    enc_gains, dec_gains = (
        v.astype(LOW).astype(WIDE)
        for v in unpack_norms(
            norm_rows, norm_rows.shape[0] // 8, enc_norms.shape[1], dec_norms.shape[1]
        )
    )
    stream = halves(act_in[0], partner(act_in[0]), 0)
    stream = jnp.pad(stream, ((0, rows - real_rows), (0, 0)))
    first, turned, mixture, log_sum, mix_own = encoder_attend(
        stream, slots, ranges, enc_gains, qkv_w, out_w, head
    )
    after, second, hidden, slope, feed_own = encoder_feed(
        stream, mix_own, partner(mix_own), enc_gains, up_w, down_w, ROW_BLOCK
    )
    encoded = (after + (feed_own.astype(WIDE) + partner(feed_own).astype(WIDE))).astype(LOW)
    projected = mm(encoded, projection)[:real_rows].astype(LOW)
    arrived = from_behind(projected, "section", 1)
    visible = halves(arrived, partner(arrived), 1)

    def join(own, other):
        pieces = list(zip(cut_columns(own, dec_widths), cut_columns(other, dec_widths)))
        qkv = jnp.concatenate([p for pair in pieces[:3] for p in pair], axis=1)
        return (qkv, *(jnp.concatenate(pair, axis=1) for pair in pieces[3:]))

    dec_mats = on_side(decoder_side, join, dec_own, partner(dec_own))
    decoded, grad_visible, grad_qkv, grad_out, grad_up, grad_down, dec_gain_grad = decoder_step(
        visible, target, mask_token, dec_position, dec_gains, *dec_mats, act_in[0], local_images
    )

    seen = grad_visible.astype(LOW)
    left, right = seen[:, :dec_part], seen[:, dec_part:]
    returned = jnp.where(first_half, left, right).astype(WIDE) + partner(
        jnp.where(first_half, right, left)
    ).astype(WIDE)
    grad_projected = from_behind(returned.astype(LOW), "section", -1)
    grad_projected = jnp.pad(grad_projected, ((0, rows - real_rows), (0, 0)))

    def dec_packs(grad_qkv, grad_out, grad_up, grad_down):
        pieces = [grad_qkv.T[:, k * dec_part : (k + 1) * dec_part] for k in range(6)]
        pieces += [grad_out.T[:, :dec_part], grad_out.T[:, dec_part:]]
        for matrix in (grad_up, grad_down):
            pieces += [matrix[:, :dec_units], matrix[:, dec_units:]]
        return tuple(
            jnp.concatenate(pieces[k::2], axis=1).astype(kind) for k, kind in ((0, WIDE), (1, LOW))
        )

    pack_own, pack_other = on_side(
        decoder_side, dec_packs, grad_qkv, grad_out, grad_up, grad_down
    )
    dec_grad = (pack_own + partner(pack_other).astype(WIDE)).astype(LOW)
    dec_gain_grad = dec_gain_grad + partner(dec_gain_grad)

    grad_projection = mm(encoded, grad_projected, 0, 0).astype(LOW)
    end_own = mm(grad_projected, projection, 1, 1).astype(LOW)
    end_other = partner(end_own)
    grad_up_w, grad_down_w, back_own = encoder_feed_back(
        end_own, end_other, second, hidden, slope, up_w, down_w
    )
    grad_after, grad_low, gains_two = encoder_norm_back(
        after, back_own, partner(back_own), (end_own, end_other), enc_gains, 2, ROW_BLOCK, True
    )
    grad_qkv_w, grad_out_w, start_own = encoder_attend_back(
        slots, ranges, first, turned, mixture, log_sum, grad_low, qkv_w, out_w, head
    )
    grad_stream, gains_one = encoder_norm_back(
        stream, start_own, partner(start_own), (grad_after,), enc_gains, 0, ROW_BLOCK, False
    )
    enc_gain_grad = jnp.concatenate([gains_one[:2], gains_two[:2]], axis=0)
    norm_grads = pack_norms(
        jnp.where(encoder_side, enc_gain_grad, 0.0),
        jnp.where(decoder_side, dec_gain_grad, 0.0),
        norm_rows.shape[0] // 8,
    )
    enc_shard, dec_shard, norm_shard = scatter_all(
        (grad_qkv_w, grad_out_w, grad_up_w, grad_down_w, grad_projection),
        dec_grad,
        norm_grads,
        encoder_side,
    )
    enc_gain_shard, dec_gain_shard = unpack_norms(
        norm_shard, 1, enc_norms.shape[1], dec_norms.shape[1]
    )
    local_squares = (
        jnp.sum(enc_shard * enc_shard)
        + jnp.sum(dec_shard * dec_shard)
        + (jnp.sum(enc_gain_shard * enc_gain_shard) + jnp.sum(dec_gain_shard * dec_gain_shard))
        / mp_count
    )
    square_total = lax.psum(local_squares, ("section", "dp", "mp"))
    grad_norm = jnp.sqrt(square_total)
    factor = jnp.minimum(1.0, math.sqrt(PARAMS) / (grad_norm + 1e-06))
    step_value = step_count[0].astype(jnp.float32)
    fix_first = 1.0 - jnp.power(BETA_FIRST, step_value)
    fix_second = 1.0 - jnp.power(BETA_SECOND, step_value)

    def renew(weight, first_moment, second_moment, gradient, rate, decay):
        return update(
            weight, first_moment, second_moment, gradient, factor, rate, fix_first, fix_second, decay
        )

    enc_shard, dec_shard = enc_shard[:, None, :], dec_shard[:, None, :]
    step_rate, norm_rate = learning_rate[0], learning_rate[1]
    own_grad = lax.dynamic_slice_in_dim(grad_stream, mp_rank * local_rows, local_rows, axis=0)
    act_out = jnp.where(encoder_side, own_grad, decoded.reshape(local_rows, width))[None]
    return (
        act_out,
        renew(enc_weights, enc_first, enc_second, enc_shard, step_rate, WEIGHT_DECAY),
        renew(dec_weights, dec_first, dec_second, dec_shard, step_rate, WEIGHT_DECAY),
        renew(enc_norms, enc_norm_first, enc_norm_second, enc_gain_shard, norm_rate, 0.0),
        renew(dec_norms, dec_norm_first, dec_norm_second, dec_gain_shard, norm_rate, 0.0),
        enc_shard * factor,
        dec_shard * factor,
        enc_gain_shard * factor,
        dec_gain_shard * factor,
        grad_norm.reshape(1),
    )


def solution(mesh):
    in_specs = (
        P("section", ("dp", "mp"), None),
        P("dp", None, None),
        P(("section", "dp"), "mp", None),
        P(("section", "dp"), "mp", None),
        P(("section", "dp"), "mp", None),
        P(("section", "dp"), "mp", None),
        P(("section", "dp"), "mp", None),
        P(("section", "dp"), "mp", None),
        P(None, ("section", "dp")),
        P(None, ("section", "dp")),
        P(None, ("section", "dp")),
        P(None, ("section", "dp")),
        P(None, ("section", "dp")),
        P(None, ("section", "dp")),
        P(),
        P(),
        P(),
        P(),
    )
    out_specs = (
        P("section", ("dp", "mp"), None),
        P(("section", "dp"), "mp", None),
        P(("section", "dp"), "mp", None),
        P(None, ("section", "dp")),
        P(None, ("section", "dp")),
        P(("section", "dp"), "mp", None),
        P(("section", "dp"), "mp", None),
        P(None, ("section", "dp")),
        P(None, ("section", "dp")),
        P(),
    )
    return jax.shard_map(
        per_device, mesh=mesh, in_specs=in_specs, out_specs=out_specs, check_vma=False
    )
```

time: 2440 us -> 831 us (0.34)
  waiting for transfers between devices: 1530 us -> 53 us
  Pallas kernels: 0 us -> 628 us
  matrix products: 321 us -> 5.14 us
  local copies, waits for them, and re-layouts: 210 us -> 60.5 us
  other arithmetic: 164 us -> 30.3 us
  blocking collectives: 159 us -> 38.1 us
    unnamed x30 -> x0, waiting for transfers between devices: 748 us -> none
    pallas_call x0 -> x9, Pallas kernels: none -> 628 us  [the longest x1 171 us: scatter_grads(): return call(*views)]
    reduce_scatter x5 -> x0, waiting for transfers between devices: 483 us -> none  [the longest x4 458 us: dec_sum(): lax.psum_scatter(partial_rows.astype(jnp.bfloat16), 'mp', scatter_dimensi...]
    dot_general x71 -> x3, matrix products: 321 us -> 5.14 us  [mm(): lax.dot_general(left, right, (((left_dim,), (right_dim,)), ((), ())), pre...]
    all_gather x12 -> x0, waiting for transfers between devices: 266 us -> none  [the longest x1 157 us: per_device(): lax.all_gather(low_weights[0], ('section', 'dp'), axis=0, tiled=True)]
    all_gather x2 -> x0, blocking collectives: 84.4 us -> none  [the longest x1 42.4 us: per_device(): lax.all_gather(low_weights[2], ('section', 'dp'), axis=1, tiled=True)]
    unnamed x145 -> x70, local copies, waits for them, and re-layouts: 95.4 us -> 23.8 us
    another operation x10 -> x2, other arithmetic: 45.7 us -> 1.92 us
  transfers between devices with their start and end apart: 28 -> 13, of which waited for: 22 -> 6; matrix products, arithmetic and copies ran while one was open for 15% -> 5% of each run, Pallas kernels for 0% -> 25%
where the time goes in v1:
time: 831 us; the launch traced here: 828 us
  Pallas kernels  628 us (76%)
  local copies, waits for them, and re-layouts  60.5 us (7%)
  waiting for transfers between devices  53 us (6%)
  blocking collectives  38.1 us (5%)
  other arithmetic  30.3 us (4%)
    pallas_call x1, Pallas kernels, scatter_grads(): return call(*views)  171 us
    pallas_call x1, Pallas kernels, gather_weights(): results = call(*shards)  142 us
    pallas_call x1, Pallas kernels, decoder_step(): pl.pallas_call(functools.partial(decoder_kernel, images * length, length)...  135 us
    pallas_call x1, Pallas kernels, encoder_attend_back(): pl.pallas_call(functools.partial(attend_back_kernel, head), in_specs=[pl....  55.1 us
    pallas_call x1, Pallas kernels, encoder_attend(): pl.pallas_call(functools.partial(attend_kernel, head), in_specs=[pl.Block...  52.2 us
    psum x1, blocking collectives, per_device(): square_total = lax.psum(local_squares, ('section', 'dp', 'mp'))  38.1 us
    ppermute x2, waiting for transfers between devices, from_behind(): return lax.ppermute(value, axis, pairs)  34.8 us
    pallas_call x1, Pallas kernels, encoder_feed_back(): pl.pallas_call(feed_back_kernel, grid=(units // piece,), in_specs=[whole,...  30.7 us
  transfers between devices with their start and end apart: 13, of which 6 were waited for; matrix products, arithmetic and copies ran while one was open for 5% of the time, Pallas kernels for 25%

profile of v1, /device:TPU:0, one launch (start us, length us, event | category | flops | bytes accessed | tf_op | source)
XLA Modules:
  0.0 828.4 jit_solution(16306455163593034835)
XLA Ops:
  4.8 1.5 copy.170
  6.5 141.6 %shard_map.249 = (bf16[2,2,2,2,64,1536]{5,4,3,2,1,0:T(8,128)(2,1)S(1)}, bf16[2,2,2,2,64,512]{5,4,3,2,1,0:T(8,128)(2,1)S(1)}, bf16[2,2,2,2,64,2048]{5,4,3,2,1,0:T...) custom-call(bf16[64,6400]{1,0:T(8,128)(2,1)S(1)} %bitcast.117, ...), custom_call_target="tpu_custom_call" | custom-call | tf_op jit(solution)/shard_map/pallas_call | solution.py:156
  148.2 2.0 copy-done
  150.1 2.0 copy-done.1
  152.1 1.7 copy-done.2
  156.8 1.7 pad.35.stream.refs_0_
  158.4 52.2 %shard_map.250 = (bf16[1200,1024]{1,0:T(8,128)(2,1)}, bf16[1536,1280]{1,0:T(8,128)(2,1)}, bf16[512,1280]{1,0:T(8,128)(2,1)}, f32[8,1280]{1,0:T(8,128)}, bf16[1200,1024]{1,0:T(8,128)(2,1)}) custom-call(s32[5,2]{1,0:T(8,128)} %copy.119.bounds, bf16[1200,1024]{1,0:T(8,128)(2,1)} %pad.35.stream.refs_0_, s32[1,1280]{1,0:T(1,128)} %broadcast_in_dim.63.slots_row, ...), custom_call_target="tpu_custom_call" | custom-call | tf_op jit(solution)/shard_map/pallas_call | solution.py:688
  210.6 5.0 collective-permute-done.1.other
  215.7 20.7 %shard_map.251 = (f32[1200,1024]{1,0:T(8,128)}, bf16[1200,1024]{1,0:T(8,128)(2,1)}, bf16[1200,2048]{1,0:T(8,128)(2,1)}, bf16[1200,2048]{1,0:T(8,128)(2,1)}, bf16[1200,1024]{1,0:T(8,128)(2,1)}) custom-call(bf16[1200,1024]{1,0:T(8,128)(2,1)} %pad.35.stream.refs_0_, bf16[1200,1024]{1,0:T(8,128)(2,1)} %get-tuple-element.79.own, ...), custom_call_target="tpu_custom_call" | custom-call | tf_op jit(solution)/shard_map/pallas_call | solution.py:858
  236.9 6.9 collective-permute-done.2
  243.7 4.5 add_convert_fusion.1
  249.8 3.1 collective-permute-start.3
  252.9 12.2 %collective-permute-done.3 = bf16[1176,256]{1,0:T(8,128)(2,1)} collective-permute-done((bf16[1176,256]{1,0:T(8,128)(2,1)S(1)}, bf16[1176,256]{1,0:T(8,128)(2,1)}, u32[]{:S(2)}, u32[]{:S(2)}) %collective-permute-start.3) | collective-permute-done | bytes 602144 | tf_op jit(solution)/shard_map/ppermute | solution.py:982
  269.4 2.0 pad.40.position
  271.3 3.4 conditional.2
  271.5 1.6 broadcast.35
  273.1 1.6 broadcast.35.clone
  274.7 2.0 copy.116
  277.7 2.0 maximum_select_fusion.1
  280.8 135.1 %shard_map.252 = (f32[6,208,512]{2,1,0:T(8,128)}, f32[1280,512]{1,0:T(8,128)}, f32[1536,512]{1,0:T(8,128)}, f32[512,512]{1,0:T(8,128)}, f32[512,2048]{1,0:T(8,12...) custom-call(s32[1,1280]{1,0:T(1,128)} %broadcast_in_dim.66.target_row, s32[1280,1]{1,0:T(8,128)} %broadcast_in_dim.72.target_column, ...), custom_call_target="tpu_custom_call" | custom-call | tf_op jit(solution)/shard_map/pallas_call | solution.py:547
  415.9 1.9 convert.34
  418.4 1.6 collective-permute-done.6
  420.3 1.5 collective-permute-start.7
  421.8 22.6 %collective-permute-done.7 = bf16[1176,256]{1,0:T(8,128)(2,1)S(1)} collective-permute-done((bf16[1176,256]{1,0:T(8,128)(2,1)S(1)}, bf16[1176,256]{1,0:T(8,128)(2,1)S(1)}, u32[]{:S(2)}, u32[]{:S(2)}) %collective-permute-start.7) | collective-permute-done | bytes 602144 | tf_op jit(solution)/shard_map/ppermute | solution.py:982
  445.3 4.7 collective-permute-done.8.other.refs_4_
  450.0 1.5 copy-done.8
  451.4 30.7 %shard_map.253 = (bf16[1024,2048]{1,0:T(8,128)(2,1)}, bf16[1024,2048]{1,0:T(8,128)(2,1)}, bf16[1200,1024]{1,0:T(8,128)(2,1)}) custom-call(bf16[1200,1024]{1,0:T(8,128)(2,1)} %copy-done.4, bf16[1200,1024]{1,0:T(8,128)(2,1)} %copy-done.8, bf16[1200,1024]{1,0:T(8,128)(2,1)} %get-tuple-element.91.second, bf16[1200,2048]{1,0:T(8,128)(2,1)} %get-tuple-element.92.hidden, ...), custom_call_target="tpu_custom_call" | custom-call | tf_op jit(solution)/shard_map/pallas_call | solution.py:914
  482.3 5.5 conditional.3
  482.3 3.5 broadcast.36
  485.8 2.0 broadcast.37
  488.2 11.3 %shard_map.254 = (f32[1200,1024]{1,0:T(8,128)}, bf16[1200,1024]{1,0:T(8,128)(2,1)}, f32[8,1024]{1,0:T(8,128)}) custom-call(f32[1200,1024]{1,0:T(8,128)} %get-tuple-element.82.refs_0_, bf16[1200,1024]{1,0:T(8,128)(2,1)} %get-tuple-element.94.refs_1_, bf16[1200,1024]{1,0:T(8,128)(2,1)} %collective-permute-done.9.refs_2_, bf16[1200,1024]{1,0:T(8,128)(2,1)} %copy-done.4, ...), custom_call_target="tpu_custom_call" | custom-call | tf_op jit(solution)/shard_map/pallas_call | solution.py:969
  499.6 55.1 %shard_map.255 = (bf16[1024,1536]{1,0:T(8,128)(2,1)}, bf16[1024,512]{1,0:T(8,128)(2,1)}, bf16[1200,1024]{1,0:T(8,128)(2,1)}) custom-call(s32[5,2]{1,0:T(8,128)} %copy.119.bounds, s32[1,1280]{1,0:T(1,128)} %broadcast_in_dim.63.slots_row, s32[1280,1]{1,0:T(8,128)} %broadcast_in_dim.73.slots_column, bf16[1200,1024]{1,0:T(8,128)(2,1)} %get-tuple-element.75.first, ...), custom_call_target="tpu_custom_call" | custom-call | tf_op jit(solution)/shard_map/pallas_call | solution.py:808
  556.6 3.4 slice.144
  560.7 1.4 copy.172
  562.1 3.5 convolution_convert_fusion.1
  565.6 5.4 add_convert_fusion
  571.9 9.9 %shard_map.256 = (f32[1200,1024]{1,0:T(8,128)}, f32[8,1024]{1,0:T(8,128)}) custom-call(bf16[1200,1024]{1,0:T(8,128)(2,1)} %pad.35.stream.refs_0_, bf16[1200,1024]{1,0:T(8,128)(2,1)} %get-tuple-element.96.refs_1_, bf16[1200,1024]{1,0:T(8,128)(2,1)} %collective-permute-done.10.refs_2_, f32[1200,1024]{1,0:T(8,128)} %get-tuple-element.97.refs_3_, ...), custom_call_target="tpu_custom_call" | custom-call | tf_op jit(solution)/shard_map/pallas_call | solution.py:969
  583.5 170.8 %shard_map.257 = (f32[64,6400]{1,0:T(8,128)}, f32[32,3072]{1,0:T(8,128)}, f32[8,128]{1,0:T(8,128)}) custom-call(bf16[2,2,2,2,64,1536]{5,4,3,2,1,0:T(8,128)(2,1)} %bitcast.135, bf16[2,2,2,2,64,512]{5,4,3,2,1,0:T(8,128)(2,1)} %bitcast.137, bf16[2,2,2,2,64,2048]{5,4,3,2,1,0:T(8,128)(2,1)} %bitcast.129, bf16[2,2,2,2,64,2048]{5,4,3,2,1,0:T(8,128)(2,1)} %bitcast.130, ...), custom_call_target="tpu_custom_call" | custom-call | tf_op jit(solution)/shard_map/pallas_call | solution.py:350
  756.2 2.5 multiply_reduce_fusion
  758.7 1.7 multiply_reduce_fusion.1
  763.0 3.5 reshape_reshape.10
  766.5 38.1 %psum.7 = f32[]{:T(128)} all-reduce(f32[]{:T(128)S(6)} %add.131), channel_id=1, replica_groups=mesh['section'=2,'dp'=8,'mp'=2] {'section','dp','mp'}, use_global_device_ids=true, to_apply=%region_12.13 | all-reduce | flops 1 | bytes 8 | tf_op jit(solution)/shard_map/psum | solution.py:1252
  805.5 1.5 copy-done.9
  807.1 2.4 select_bitcast_fusion
  809.5 3.9 copy.132
  813.4 1.9 multiply_subtract_fusion
  815.3 2.8 copy.133
  820.4 2.8 copy.135
  (131 shorter events, 30.5 us)
Async XLA Ops:
  0.6 5.7 copy-start.18
  0.7 5.7 copy-start.27
  0.7 5.7 copy-start.25
  0.7 154.8 %collective-permute-start = (bf16[588,1024]{1,0:T(8,128)(2,1)}, bf16[588,1024]{1,0:T(8,128)(2,1)S(1)}, u32[]{:S(2)}, u32[]{:S(2)}) collective-permute-start(bf16[588,1024]{1,0:T(8,128)(2,1)} %bitcast.127), channel_id=1, source_target_pairs={{0,1},{1,0},{2,3},{3,2},{4,5},{5,4},{6,7},{7,6},{8,9},{9,8},{10,11... | collective-permute-start | bytes 3612680 | tf_op jit(solution)/shard_map/ppermute | solution.py:987
  2.6 152.8 %copy-start.11 = (bf16[1,588,1024]{2,1,0:T(8,128)(2,1)S(1)}, bf16[1,588,1024]{2,1,0:T(8,128)(2,1)}, u32[]{:S(2)}) copy-start(bf16[1,588,1024]{2,1,0:T(8,128)(2,1)} %param.22) | copy-start | bytes 3612676
  148.1 2.0 copy-start
  150.1 2.0 copy-start.1
  152.1 1.7 copy-start.2
  153.8 1.0 copy-start.3
  210.6 5.0 collective-permute-start.1
  236.4 7.4 collective-permute-start.2
  236.5 34.9 %collective-permute-start.5 = (bf16[512,3072]{1,0:T(8,128)(2,1)}, bf16[512,3072]{1,0:T(8,128)(2,1)}, u32[]{:S(2)}, u32[]{:S(2)}) collective-permute-start(bf16[512,3072]{1,0:T(8,128)(2,1)} %bitcast.133), channel_id=1, source_target_pairs={{0,1},{1,0},{2,3},{3,2},{4,5},{5,4},{6,7},{7,6},{8,9},{9,8},{10,11... | collective-permute-start | bytes 9437192 | tf_op jit(solution)/shard_map/ppermute | solution.py:987
  248.3 1.4 copy-start.14
  249.8 15.4 %collective-permute-start.3 = (bf16[1176,256]{1,0:T(8,128)(2,1)S(1)}, bf16[1176,256]{1,0:T(8,128)(2,1)}, u32[]{:S(2)}, u32[]{:S(2)}) collective-permute-start(bf16[1176,256]{1,0:T(8,128)(2,1)S(1)} %slice.208), channel_id=1, source_target_pairs={{0,16},{1,17},{2,18},{3,19},{4,20},{5,21},{6,22},{7,23},{8,24},{9,... | collective-permute-start | bytes 1806344 | tf_op jit(solution)/shard_map/ppermute | solution.py:982
  265.1 12.5 %collective-permute-start.4 = (bf16[1176,256]{1,0:T(8,128)(2,1)}, bf16[1176,256]{1,0:T(8,128)(2,1)}, u32[]{:S(2)}, u32[]{:S(2)}) collective-permute-start(bf16[1176,256]{1,0:T(8,128)(2,1)} %collective-permute-done.3), channel_id=1, source_target_pairs={{0,1},{1,0},{2,3},{3,2},{4,5},{5,4},{6,7},{7,6},{8,9},{9,8},{10,11... | collective-permute-start | bytes 1806344 | tf_op jit(solution)/shard_map/ppermute | solution.py:987
  268.1 3.2 copy-start.13
  417.9 2.2 collective-permute-start.6
  420.3 24.1 %collective-permute-start.7 = (bf16[1176,256]{1,0:T(8,128)(2,1)S(1)}, bf16[1176,256]{1,0:T(8,128)(2,1)S(1)}, u32[]{:S(2)}, u32[]{:S(2)}) collective-permute-start(bf16[1176,256]{1,0:T(8,128)(2,1)S(1)} %add_convert_fusion.2), channel_id=1, source_target_pairs={{16,0},{17,1},{18,2},{19,3},{20,4},{21,5},{22,6},{23,7},{24,8},{25... | collective-permute-start | bytes 1806344 | tf_op jit(solution)/shard_map/ppermute | solution.py:982
  444.4 7.1 copy-start.19
  445.2 6.2 copy-start.4
  445.2 4.7 collective-permute-start.8
  450.0 1.5 copy-start.8
  482.1 6.1 collective-permute-start.9
  487.8 77.8 %collective-permute-start.11 = (bf16[512,3072]{1,0:T(8,128)(2,1)}, bf16[512,3072]{1,0:T(8,128)(2,1)S(1)}, u32[]{:S(2)}, u32[]{:S(2)}) collective-permute-start(bf16[512,3072]{1,0:T(8,128)(2,1)} %get-tuple-element.109), channel_id=1, source_target_pairs={{0,1},{1,0},{2,3},{3,2},{4,5},{5,4},{6,7},{7,6},{8,9},{9,8},{10,11... | collective-permute-start | bytes 9437192 | tf_op jit(solution)/shard_map/ppermute | solution.py:987
  499.6 55.3 %copy-start.23 = (f32[8,512]{1,0:T(8,128)S(1)}, f32[8,512]{1,0:T(8,128)}, u32[]{:S(2)}) copy-start(f32[8,512]{1,0:T(8,128)} %get-tuple-element.112) | copy-start | bytes 49156
  499.6 55.6 %copy-start.33 = (f32[2]{0:T(128)S(1)}, f32[2]{0:T(128)}, u32[]{:S(2)}) copy-start(f32[2]{0:T(128)} %param.38) | copy-start | bytes 28
  554.7 17.3 %collective-permute-start.10 = (bf16[1200,1024]{1,0:T(8,128)(2,1)}, bf16[1200,1024]{1,0:T(8,128)(2,1)}, u32[]{:S(2)}, u32[]{:S(2)}) collective-permute-start(bf16[1200,1024]{1,0:T(8,128)(2,1)} %get-tuple-element.96.refs_1_), channel_id=1, source_target_pairs={{0,1},{1,0},{2,3},{3,2},{4,5},{5,4},{6,7},{7,6},{8,9},{9,8},{10,11... | collective-permute-start | bytes 7372808 | tf_op jit(solution)/shard_map/ppermute | solution.py:987
  554.8 5.2 collective-permute-start.12
  556.6 3.5 copy-start.24
  571.9 10.8 %copy-start.22 = (f32[4,16,32]{2,0,1:T(4,128)S(1)}, f32[4,16,32]{2,0,1:T(4,128)}, u32[]{:S(2)}) copy-start(f32[4,16,32]{2,0,1:T(4,128)} %copy.172) | copy-start | bytes 24580
  763.0 42.4 %copy-start.5 = (f32[64,6400]{1,0:T(8,128)S(1)}, f32[64,6400]{1,0:T(8,128)}, u32[]{:S(2)}) copy-start(f32[64,6400]{1,0:T(8,128)} %get-tuple-element.113) | copy-start | bytes 4915204
  766.5 39.0 %copy-start.12 = (f32[32,3072]{1,0:T(8,128)S(1)}, f32[32,3072]{1,0:T(8,128)}, u32[]{:S(2)}) copy-start(f32[32,3072]{1,0:T(8,128)} %get-tuple-element.114) | copy-start | bytes 1179652
  805.4 1.7 copy-start.9
  807.1 6.3 copy-start.17
  809.5 3.9 copy-start.10
  809.5 3.9 copy-start.16
  815.3 2.9 copy-start.20
  815.3 2.9 copy-start.21
  819.2 5.2 copy-start.26
  819.2 5.2 copy-start.29
  819.2 5.2 copy-start.30
  819.3 6.5 copy-start.28
  819.3 6.5 copy-start.31
  819.3 6.5 copy-start.32

commit v2 on v1

--- a/solution.py
+++ b/solution.py
@@ -40,15 +40,16 @@
             "h": (s, depth + 4 - 8 * high, core),
             "l": (s, depth + 2 - 4 * low, core),
             "y": (s, depth + 1 - 2 * y, core),
+            "c": (s, depth, 1 - core),
         }
 
     def greet(self):
         barrier = pltpu.get_barrier_semaphore()
-        for name in DIMS:
+        for name in self.device:
             pl.semaphore_signal(
                 barrier, inc=1, device_id=self.device[name], device_id_type=MESH_ID
             )
-        pl.semaphore_wait(barrier, len(DIMS))
+        pl.semaphore_wait(barrier, len(self.device))
 
 
 def run(condition, action):
@@ -58,7 +59,7 @@
         pl.when(condition)(action)
 
 
-def gather_kernel(chunks, n_in, n_out, ahead, *refs):
+def gather_kernel(chunks, n_in, n_out, ahead, lag, *refs):
     ins, outs = refs[:n_in], refs[n_in : n_in + n_out]
     send, recv, local = refs[n_in + n_out :]
     here = Place()
@@ -116,9 +117,9 @@
         own(i).start()
     for i in range(min(ahead, count)):
         begin(i, 0)
-    for step in range(count + 2):
+    for step in range(count + sum(lag)):
         for stage in range(3):
-            i = step - stage
+            i = step - sum(lag[:stage])
             if not 0 <= i < count:
                 continue
             arrive(i, stage)
@@ -135,10 +136,10 @@
             )
 
 
-def gather_weights(shards, outputs, chunks, collective_id, ahead=4):
+def gather_weights(shards, outputs, chunks, collective_id, ahead=4, lag=(1, 1)):
     count = len(chunks)
     call = pl.pallas_call(
-        functools.partial(gather_kernel, chunks, len(shards), len(outputs), ahead),
+        functools.partial(gather_kernel, chunks, len(shards), len(outputs), ahead, lag),
         out_shape=[
             jax.ShapeDtypeStruct((2, 2, 2, 2, rows, width), dtype) for rows, width, dtype in outputs
         ],
@@ -191,15 +192,27 @@
     return shapes
 
 
-def scatter_kernel(chunks, n_in, n_out, ahead, lag, *refs):
-    ins, outs = refs[:n_in], refs[n_in : n_in + n_out]
-    rest = refs[n_in + n_out :]
-    send, recv, local = rest[:3]
+def squares(ref):
+    def step(k, total):
+        block = ref[:, pl.ds(pl.multiple_of(k * 128, 128), 128)].astype(jnp.float32)
+        block = block * block
+        for r in range(0, block.shape[0], 8):
+            total = total + block[r : r + 8]
+        return total
+
+    return lax.fori_loop(0, ref.shape[1] // 128, step, jnp.zeros((8, 128), jnp.float32))
+
+
+def scatter_kernel(chunks, n_in, n_out, ahead, lag, cores, *refs):
+    ins, summed, outs = refs[:n_in], refs[n_in], refs[n_in + 1 : n_in + 1 + n_out]
+    square_total = refs[n_in + 1 + n_out]
+    rest = refs[n_in + n_out + 2 :]
+    send, recv, local, square_send, square_recv, square_mine, square_there = rest[:7]
     here = Place()
     s = here.s
     count = len(chunks)
     own, got = [], []
-    position = 3
+    position = 7
     for chunk in chunks:
         order, owner = chunk[5], chunk[6]
         own.append(rest[position])
@@ -306,9 +319,9 @@
         )
     for i in range(min(ahead, count)):
         begin(i, 0)
-    for step in range(count + 3 * lag):
+    for step in range(count + sum(lag)):
         for stage in range(3, -1, -1):
-            i = step - stage * lag
+            i = step - sum(lag[:stage])
             if not 0 <= i < count:
                 continue
             arrive(i, stage)
@@ -323,8 +336,27 @@
                 lambda i=i, stage=stage: copy(i, stage, False).wait_send(),
             )
 
-
-def scatter_grads(parts, outputs, chunks, collective_id, ahead=4, lag=1):
+    value = squares(summed)
+    for k, out in enumerate(outs):
+        value = value + squares(out) * (1.0 / cores if k == n_out - 1 else 1.0)
+    value = jnp.broadcast_to(jnp.sum(value, keepdims=True), (8, 128))
+    for k, axis in enumerate("cyxlh"):
+        square_mine[k] = value
+        move = pltpu.make_async_remote_copy(
+            src_ref=square_mine.at[k],
+            dst_ref=square_there.at[k],
+            send_sem=square_send.at[k],
+            recv_sem=square_recv.at[k],
+            device_id=here.device[axis],
+            device_id_type=MESH_ID,
+        )
+        move.start()
+        move.wait()
+        value = value + square_there[k]
+    square_total[...] = value
+
+
+def scatter_grads(parts, summed, outputs, chunks, collective_id, ahead=4, lag=(1, 1, 1)):
     count = len(chunks)
     views = [p.reshape(2, 2, 2, 2, p.shape[0] // 16, p.shape[1]) for p in parts]
     buffers = []
@@ -333,21 +365,28 @@
         for lead in scatter_buffers(chunk[5], chunk[6]):
             buffers.append(pltpu.VMEM((*lead, view.shape[4], chunk[4]), view.dtype))
     call = pl.pallas_call(
-        functools.partial(scatter_kernel, chunks, len(parts), len(outputs), ahead, lag),
-        out_shape=[jax.ShapeDtypeStruct((rows, width), jnp.float32) for rows, width in outputs],
-        in_specs=[pl.BlockSpec(memory_space=pl.ANY)] * len(parts),
-        out_specs=[pl.BlockSpec(memory_space=pltpu.VMEM)] * len(outputs),
+        functools.partial(scatter_kernel, chunks, len(parts), len(outputs), ahead, lag, lax.axis_size("mp")),
+        out_shape=[
+            jax.ShapeDtypeStruct((rows, width), jnp.float32) for rows, width in [*outputs, (8, 128)]
+        ],
+        in_specs=[pl.BlockSpec(memory_space=pl.ANY)] * len(parts)
+        + [pl.BlockSpec(memory_space=pltpu.VMEM)],
+        out_specs=[pl.BlockSpec(memory_space=pltpu.VMEM)] * (len(outputs) + 1),
         scratch_shapes=[
             pltpu.SemaphoreType.DMA((count, 4)),
             pltpu.SemaphoreType.DMA((count, 4)),
             pltpu.SemaphoreType.DMA((count,)),
+            pltpu.SemaphoreType.DMA((5,)),
+            pltpu.SemaphoreType.DMA((5,)),
+            pltpu.VMEM((5, 8, 128), jnp.float32),
+            pltpu.VMEM((5, 8, 128), jnp.float32),
             *buffers,
         ],
         compiler_params=pltpu.CompilerParams(
             collective_id=collective_id, has_side_effects=True, vmem_limit_bytes=56 * 2**20
         ),
     )
-    return call(*views)
+    return call(*views, summed)
 
 
 HEADS = 16
@@ -872,6 +911,7 @@
 
 
 def feed_back_kernel(
+    counts,
     own,
     other,
     second,
@@ -894,7 +934,8 @@
         second_turned[...] = jnp.transpose(second[...])
         total[...] = jnp.zeros_like(total)
 
-    grad_down[...] = mm(grad_turned[...], hidden[...]).astype(LOW)
+    down = mm(grad_turned[...], hidden[...])
+    grad_down[...] = jnp.where(counts[0] > 0, down, jnp.zeros_like(down)).astype(LOW)
     grad_z = (mm(grad_low[...], down_w[...]) * slope[...].astype(WIDE)).astype(LOW)
     grad_up[...] = mm(second_turned[...], grad_z).astype(LOW)
     total[...] += mm(grad_z, up_w[...], 1, 1)
@@ -904,7 +945,7 @@
         partial[...] = total[...].astype(LOW)
 
 
-def encoder_feed_back(own, other, second, hidden, slope, up_w, down_w):
+def encoder_feed_back(counts, own, other, second, hidden, slope, up_w, down_w):
     rows, width = own.shape
     units = up_w.shape[1]
     piece = 256
@@ -914,7 +955,8 @@
     return pl.pallas_call(
         feed_back_kernel,
         grid=(units // piece,),
-        in_specs=[whole, whole, whole, tall, tall, weight, weight],
+        in_specs=[pl.BlockSpec(memory_space=pltpu.SMEM)]
+        + [whole, whole, whole, tall, tall, weight, weight],
         out_specs=[weight, weight, whole],
         out_shape=[
             jax.ShapeDtypeStruct((width, units), LOW),
@@ -928,7 +970,7 @@
             pltpu.VMEM((rows, width), WIDE),
         ],
         compiler_params=params(),
-    )(own, other, second, hidden, slope, up_w, down_w)
+    )(counts, own, other, second, hidden, slope, up_w, down_w)
 
 
 def norm_back_kernel(tokens, own, other, skip_own, skip_other, gains, grad, grad_low, grad_gains, *, at):
@@ -1021,32 +1063,51 @@
             parts.append(enc[:, column : column + w])
             column += w
         return parts, dec, rows
-    chunks = plan(widths, (4, 1, 4, 4, 2), low_dec.shape[1], 4, GATHER_ORDERS)
-    outputs = [(low_enc.shape[0], w, LOW) for w in widths]
+    columns = [sum(widths[:k]) for k in range(count + 1)]
+    ahead = [low_enc[:, : columns[3]], low_enc[:, columns[4] :]]
+    near = (*widths[:3], widths[4])
+    chunks = plan(near, (4, 1, 4, 2), low_dec.shape[1], 4, GATHER_ORDERS)
+    outputs = [(low_enc.shape[0], w, LOW) for w in near]
     outputs += [(low_dec.shape[0], low_dec.shape[1], LOW), (8, 128, WIDE)]
-    described = [(k // count, k, c, b, w, o, own) for k, b, c, w, o, own in chunks]
-    described.append((2, count + 1, 0, 0, 128, "hlyx", BOTH))
-    results = gather_weights([low_enc, low_dec, norms], outputs, described, 1, 8)
-    return results[:count], results[count], results[count + 1]
+    described = [(k // 4, k, c, b, w, o, own) for k, b, c, w, o, own in chunks]
+    described.append((2, 5, 0, 0, 128, "hlyx", BOTH))
+    shards = [jnp.concatenate(ahead, axis=1), low_dec, norms]
+    results = gather_weights(shards, outputs, described, 1, 4, (1, 3))
+    low_down, norm_rows = lax.optimization_barrier(
+        (low_enc[:, columns[3] : columns[4]], results[5])
+    )
+    down = lax.all_gather(low_down, ("section", "dp"), axis=0, tiled=True)
+    return [*results[:3], down, results[3]], results[4], norm_rows
 
 
 def scatter_all(enc_parts, dec, norms, encoder_side):
     widths = [p.shape[1] for p in enc_parts]
-    count = len(widths)
+    both = ("section", "dp")
+
+    def scattered(v):
+        return lax.psum_scatter(v, both, scatter_dimension=0, tiled=True)
+
     if not is_fast():
-        both = ("section", "dp")
-        enc = jnp.concatenate(enc_parts, axis=1).astype(WIDE)
-        enc = jnp.where(encoder_side, enc, 0.0)
-        dec = jnp.where(encoder_side, 0.0, dec.astype(WIDE))
-        return [
-            lax.psum_scatter(v, both, scatter_dimension=0, tiled=True) for v in (enc, dec, norms)
-        ]
-    chunks = plan(widths, (4, 1, 4, 4, 2), dec.shape[1], 4, SCATTER_ORDERS)
-    described = [(k, k // count, b, c, w, o, own) for k, b, c, w, o, own in chunks]
-    described.append((count + 1, 2, 0, 0, 128, "xylh", BOTH))
-    rows = enc_parts[0].shape[0] // 16
-    outputs = [(rows, sum(widths)), (dec.shape[0] // 16, dec.shape[1]), (8, 128)]
-    return scatter_grads([*enc_parts, dec, norms], outputs, described, 2, 8, 2)
+        parts = [scattered(jnp.where(encoder_side, p.astype(WIDE), 0.0)) for p in enc_parts]
+        dec = scattered(jnp.where(encoder_side, 0.0, dec.astype(WIDE)))
+        norms = scattered(norms)
+        local = sum(jnp.sum(v * v) for v in (*parts, dec))
+        local = local + jnp.sum(norms * norms) / lax.axis_size("mp")
+        return jnp.concatenate(parts, axis=1), dec, norms, lax.psum(local, (*both, "mp"))
+    down = scattered(enc_parts[3])
+    near = (*enc_parts[:3], enc_parts[4])
+    near_widths = (*widths[:3], widths[4])
+    chunks = plan(near_widths, (4, 1, 4, 2), dec.shape[1], 4, SCATTER_ORDERS)
+    described = [(k, k // 4, b, c, w, o, own) for k, b, c, w, o, own in chunks]
+    described.append((5, 2, 0, 0, 128, "xylh", BOTH))
+    rows = near[0].shape[0] // 16
+    outputs = [(rows, sum(near_widths)), (dec.shape[0] // 16, dec.shape[1]), (8, 128)]
+    enc, dec, norms, total = scatter_grads(
+        [*near, dec, norms], down, outputs, described, 2, 4, (2, 2, 2)
+    )
+    cut = sum(widths[:3])
+    enc = jnp.concatenate([enc[:, :cut], down.astype(WIDE), enc[:, cut:]], axis=1)
+    return enc, dec, norms, total[0, 0]
 
 
 def pack_norms(enc_rows, dec_rows, blocks):
@@ -1217,7 +1278,14 @@
     end_own = mm(grad_projected, projection, 1, 1).astype(LOW)
     end_other = partner(end_own)
     grad_up_w, grad_down_w, back_own = encoder_feed_back(
-        end_own, end_other, second, hidden, slope, up_w, down_w
+        jnp.where(encoder_side, 1, 0).astype(jnp.int32).reshape(1),
+        end_own,
+        end_other,
+        second,
+        hidden,
+        slope,
+        up_w,
+        down_w,
     )
     grad_after, grad_low, gains_two = encoder_norm_back(
         after, back_own, partner(back_own), (end_own, end_other), enc_gains, 2, ROW_BLOCK, True
@@ -1234,7 +1302,7 @@
         jnp.where(decoder_side, dec_gain_grad, 0.0),
         norm_rows.shape[0] // 8,
     )
-    enc_shard, dec_shard, norm_shard = scatter_all(
+    enc_shard, dec_shard, norm_shard, square_total = scatter_all(
         (grad_qkv_w, grad_out_w, grad_up_w, grad_down_w, grad_projection),
         dec_grad,
         norm_grads,
@@ -1243,13 +1311,6 @@
     enc_gain_shard, dec_gain_shard = unpack_norms(
         norm_shard, 1, enc_norms.shape[1], dec_norms.shape[1]
     )
-    local_squares = (
-        jnp.sum(enc_shard * enc_shard)
-        + jnp.sum(dec_shard * dec_shard)
-        + (jnp.sum(enc_gain_shard * enc_gain_shard) + jnp.sum(dec_gain_shard * dec_gain_shard))
-        / mp_count
-    )
-    square_total = lax.psum(local_squares, ("section", "dp", "mp"))
     grad_norm = jnp.sqrt(square_total)
     factor = jnp.minimum(1.0, math.sqrt(PARAMS) / (grad_norm + 1e-06))
     step_value = step_count[0].astype(jnp.float32)
@@ -1257,24 +1318,46 @@
     fix_second = 1.0 - jnp.power(BETA_SECOND, step_value)
 
     def renew(weight, first_moment, second_moment, gradient, rate, decay):
-        return update(
-            weight, first_moment, second_moment, gradient, factor, rate, fix_first, fix_second, decay
-        )
-
-    enc_shard, dec_shard = enc_shard[:, None, :], dec_shard[:, None, :]
+        flat = (-1, 128) if gradient.size % 1024 == 0 else gradient.shape
+        gradient = gradient.reshape(flat)
+        renewed = update(
+            weight.reshape(flat),
+            first_moment.reshape(flat),
+            second_moment.reshape(flat),
+            gradient,
+            factor,
+            rate,
+            fix_first,
+            fix_second,
+            decay,
+        )
+        return renewed.reshape(weight.shape), (gradient * factor).reshape(weight.shape)
+
     step_rate, norm_rate = learning_rate[0], learning_rate[1]
+    new_enc, enc_clipped = renew(
+        enc_weights, enc_first, enc_second, enc_shard, step_rate, WEIGHT_DECAY
+    )
+    new_dec, dec_clipped = renew(
+        dec_weights, dec_first, dec_second, dec_shard, step_rate, WEIGHT_DECAY
+    )
+    new_enc_norms, enc_norm_clipped = renew(
+        enc_norms, enc_norm_first, enc_norm_second, enc_gain_shard, norm_rate, 0.0
+    )
+    new_dec_norms, dec_norm_clipped = renew(
+        dec_norms, dec_norm_first, dec_norm_second, dec_gain_shard, norm_rate, 0.0
+    )
     own_grad = lax.dynamic_slice_in_dim(grad_stream, mp_rank * local_rows, local_rows, axis=0)
     act_out = jnp.where(encoder_side, own_grad, decoded.reshape(local_rows, width))[None]
     return (
         act_out,
-        renew(enc_weights, enc_first, enc_second, enc_shard, step_rate, WEIGHT_DECAY),
-        renew(dec_weights, dec_first, dec_second, dec_shard, step_rate, WEIGHT_DECAY),
-        renew(enc_norms, enc_norm_first, enc_norm_second, enc_gain_shard, norm_rate, 0.0),
-        renew(dec_norms, dec_norm_first, dec_norm_second, dec_gain_shard, norm_rate, 0.0),
-        enc_shard * factor,
-        dec_shard * factor,
-        enc_gain_shard * factor,
-        dec_gain_shard * factor,
+        new_enc,
+        new_dec,
+        new_enc_norms,
+        new_dec_norms,
+        enc_clipped,
+        dec_clipped,
+        enc_norm_clipped,
+        dec_norm_clipped,
         grad_norm.reshape(1),
     )
 

time: 831 us -> 740 us (0.89); the launches traced: 828 us -> 728 us
  Pallas kernels: 628 us -> 555 us
  blocking collectives: 38.1 us -> 0 us
  between operations: 6.49 us -> 17.4 us
  waiting for transfers between devices: 53 us -> 63.2 us
    pallas_call x1, Pallas kernels: 142 us -> 98.1 us  [gather_weights(): results = call(*shards)]
    psum x1 -> x0, blocking collectives: 38.1 us -> none  [per_device(): square_total = lax.psum(local_squares, ('section', 'dp', 'mp'))]
    pallas_call x2, Pallas kernels: 201 us -> 171 us  [the longest x1 141 us: scatter_grads(): return call(*views, summed)]
    all_gather x0 -> x1, waiting for transfers between devices: none -> 10 us  [gather_all(): down = lax.all_gather(low_down, ('section', 'dp'), axis=0, tiled=True)]
    unnamed x70 -> x64, local copies, waits for them, and re-layouts: 23.8 us -> 18.9 us
  transfers between devices with their start and end apart: 13 -> 15, of which waited for: 6 -> 7; matrix products, arithmetic and copies ran while one was open for 5% -> 7% of each run, Pallas kernels for 25% -> 18%
where the time goes in v2:
time: 740 us; the launch traced here: 728 us
  Pallas kernels  555 us (75%)
  waiting for transfers between devices  63.2 us (9%)
  local copies, waits for them, and re-layouts  53.2 us (7%)
  other arithmetic  26 us (4%)
  between operations  17.4 us (2%)
  starting transfers between devices  8.54 us (1%)
    pallas_call x1, Pallas kernels, scatter_grads(): return call(*views, summed)  141 us
    pallas_call x1, Pallas kernels, decoder_step(): pl.pallas_call(functools.partial(decoder_kernel, images * length, length)...  135 us
    pallas_call x1, Pallas kernels, gather_weights(): results = call(*shards)  98.1 us
    pallas_call x1, Pallas kernels, encoder_attend_back(): pl.pallas_call(functools.partial(attend_back_kernel, head), in_specs=[pl....  55.2 us
    pallas_call x1, Pallas kernels, encoder_attend(): pl.pallas_call(functools.partial(attend_kernel, head), in_specs=[pl.Block...  52.3 us
    ppermute x2, waiting for transfers between devices, from_behind(): return lax.ppermute(value, axis, pairs)  34.9 us
    pallas_call x1, Pallas kernels, encoder_feed_back(): pl.pallas_call(feed_back_kernel, grid=(units // piece,), in_specs=[pl.Blo...  30.7 us
    pallas_call x2, Pallas kernels, encoder_norm_back(): pl.pallas_call(kernel, grid=(rows // block,), in_specs=[wide, wide, wide]...  21.9 us
  transfers between devices with their start and end apart: 15, of which 7 were waited for; matrix products, arithmetic and copies ran while one was open for 7% of the time, Pallas kernels for 18%

profile of v2, /device:TPU:0, one launch (start us, length us, event | category | flops | bytes accessed | tf_op | source)
XLA Modules:
  0.0 728.0 jit_solution(14007382443687184146)
XLA Ops:
  7.3 1.6 copy.202
  9.8 98.1 %shard_map.249 = (bf16[2,2,2,2,64,1536]{5,4,3,2,1,0:T(8,128)(2,1)S(1)}, bf16[2,2,2,2,64,512]{5,4,3,2,1,0:T(8,128)(2,1)S(1)}, bf16[2,2,2,2,64,2048]{5,4,3,2,1,0:T...) custom-call(bf16[64,4352]{1,0:T(8,128)(2,1)S(1)} %pad_maximum_fusion, ...), custom_call_target="tpu_custom_call" | custom-call | tf_op jit(solution)/shard_map/pallas_call | solution.py:157
  108.0 2.0 copy-done
  109.9 1.7 copy-done.1
  116.3 1.3 maximum_select_fusion
  117.7 1.6 pad.35.stream.refs_0_
  119.3 52.3 %shard_map.250 = (bf16[1200,1024]{1,0:T(8,128)(2,1)}, bf16[1536,1280]{1,0:T(8,128)(2,1)}, bf16[512,1280]{1,0:T(8,128)(2,1)}, f32[8,1280]{1,0:T(8,128)}, bf16[1200,1024]{1,0:T(8,128)(2,1)}) custom-call(s32[5,2]{1,0:T(8,128)} %copy.149.bounds, bf16[1200,1024]{1,0:T(8,128)(2,1)} %pad.35.stream.refs_0_, s32[1,1280]{1,0:T(1,128)} %broadcast_in_dim.61.slots_row, ...), custom_call_target="tpu_custom_call" | custom-call | tf_op jit(solution)/shard_map/pallas_call | solution.py:727
  172.0 4.6 collective-permute-done.1.other
  176.7 10.0 %all-gather.2.cloned.1.call-done.down_w = bf16[1024,2048]{1,0:T(8,128)(2,1)} async-done(((bf16[64,2048]{1,0:T(8,128)(2,1)}), bf16[1024,2048]{1,0:T(8,128)(2,1)}) %all-gather.2.cloned.1.call-update) | async-done | bytes 4194320 | tf_op jit(solution)/shard_map/all_gather | solution.py:1079
  186.7 20.8 %shard_map.251 = (f32[1200,1024]{1,0:T(8,128)}, bf16[1200,1024]{1,0:T(8,128)(2,1)}, bf16[1200,2048]{1,0:T(8,128)(2,1)}, bf16[1200,2048]{1,0:T(8,128)(2,1)}, bf16[1200,1024]{1,0:T(8,128)(2,1)}) custom-call(bf16[1200,1024]{1,0:T(8,128)(2,1)} %pad.35.stream.refs_0_, bf16[1200,1024]{1,0:T(8,128)(2,1)} %get-tuple-element.82.own, ...), custom_call_target="tpu_custom_call" | custom-call | tf_op jit(solution)/shard_map/pallas_call | solution.py:897
  208.1 7.1 collective-permute-done.2
  215.2 4.5 add_convert_fusion.1
  221.2 4.2 collective-permute-start.3
  225.4 12.3 %collective-permute-done.3 = bf16[1176,256]{1,0:T(8,128)(2,1)} collective-permute-done((bf16[1176,256]{1,0:T(8,128)(2,1)S(1)}, bf16[1176,256]{1,0:T(8,128)(2,1)}, u32[]{:S(2)}, u32[]{:S(2)}) %collective-permute-start.3) | collective-permute-done | bytes 602144 | tf_op jit(solution)/shard_map/ppermute | solution.py:1024
  240.7 1.3 pad.41.cotangent
  242.0 1.9 pad.40.position
  243.9 3.3 conditional.2
  244.1 1.6 broadcast.78
  245.6 1.6 broadcast.78.clone
  247.2 1.6 copy.146
  249.8 1.9 maximum_select_fusion.1
  252.9 135.2 %shard_map.252 = (f32[6,208,512]{2,1,0:T(8,128)}, f32[1280,512]{1,0:T(8,128)}, f32[1536,512]{1,0:T(8,128)}, f32[512,512]{1,0:T(8,128)}, f32[512,2048]{1,0:T(8,12...) custom-call(s32[1,1280]{1,0:T(1,128)} %broadcast_in_dim.64.target_row, s32[1280,1]{1,0:T(8,128)} %broadcast_in_dim.70.target_column, ...), custom_call_target="tpu_custom_call" | custom-call | tf_op jit(solution)/shard_map/pallas_call | solution.py:586
  388.1 1.9 convert.35
  390.6 1.6 collective-permute-done.6
  392.5 1.5 collective-permute-start.7
  394.0 22.6 %collective-permute-done.7 = bf16[1176,256]{1,0:T(8,128)(2,1)S(1)} collective-permute-done((bf16[1176,256]{1,0:T(8,128)(2,1)S(1)}, bf16[1176,256]{1,0:T(8,128)(2,1)S(1)}, u32[]{:S(2)}, u32[]{:S(2)}) %collective-permute-start.7) | collective-permute-done | bytes 602144 | tf_op jit(solution)/shard_map/ppermute | solution.py:1024
  417.5 4.8 collective-permute-done.8.other.refs_4_
  422.3 30.7 %shard_map.253 = (bf16[1024,2048]{1,0:T(8,128)(2,1)}, bf16[1024,2048]{1,0:T(8,128)(2,1)}, bf16[1200,1024]{1,0:T(8,128)(2,1)}) custom-call(s32[1]{0:T(128)} %bitcast.16.counts, bf16[1200,1024]{1,0:T(8,128)(2,1)} %copy-done.3, bf16[1200,1024]{1,0:T(8,128)(2,1)} %collective-permute-done.8.other.refs_4_, bf16[1200,1024]{1,0:T(8,128)(2,1)} %get-tuple-element.94.second, ...), custom_call_target="tpu_custom_call" | custom-call | tf_op jit(solution)/shard_map/pallas_call | solution.py:955
  453.2 5.5 conditional.3
  453.2 3.4 broadcast.79
  456.6 2.1 broadcast.80
  459.1 11.4 %shard_map.254 = (f32[1200,1024]{1,0:T(8,128)}, bf16[1200,1024]{1,0:T(8,128)(2,1)}, f32[8,1024]{1,0:T(8,128)}) custom-call(f32[1200,1024]{1,0:T(8,128)} %get-tuple-element.85.refs_0_, bf16[1200,1024]{1,0:T(8,128)(2,1)} %get-tuple-element.97.refs_1_, bf16[1200,1024]{1,0:T(8,128)(2,1)} %collective-permute-done.9.refs_2_, bf16[1200,1024]{1,0:T(8,128)(2,1)} %copy-done.3, ...), custom_call_target="tpu_custom_call" | custom-call | tf_op jit(solution)/shard_map/pallas_call | solution.py:1011
  470.5 55.2 %shard_map.255 = (bf16[1024,1536]{1,0:T(8,128)(2,1)}, bf16[1024,512]{1,0:T(8,128)(2,1)}, bf16[1200,1024]{1,0:T(8,128)(2,1)}) custom-call(s32[5,2]{1,0:T(8,128)} %copy.149.bounds, s32[1,1280]{1,0:T(1,128)} %broadcast_in_dim.61.slots_row, s32[1280,1]{1,0:T(8,128)} %broadcast_in_dim.71.slots_column, bf16[1200,1024]{1,0:T(8,128)(2,1)} %get-tuple-element.78.first, ...), custom_call_target="tpu_custom_call" | custom-call | tf_op jit(solution)/shard_map/pallas_call | solution.py:847
  527.6 1.9 slice.165
  529.5 2.2 reshape_reshape.6
  531.9 3.4 convolution_convert_fusion.1
  535.3 6.5 add_convert_fusion
  542.6 10.5 %shard_map.256 = (f32[1200,1024]{1,0:T(8,128)}, f32[8,1024]{1,0:T(8,128)}) custom-call(bf16[1200,1024]{1,0:T(8,128)(2,1)} %pad.35.stream.refs_0_, bf16[1200,1024]{1,0:T(8,128)(2,1)} %get-tuple-element.99.refs_1_, bf16[1200,1024]{1,0:T(8,128)(2,1)} %collective-permute-done.10.refs_2_, f32[1200,1024]{1,0:T(8,128)} %get-tuple-element.100.refs_3_, ...), custom_call_target="tpu_custom_call" | custom-call | tf_op jit(solution)/shard_map/pallas_call | solution.py:1011
  553.2 2.5 select_bitcast_fusion
  555.6 3.9 copy.162
  561.2 140.6 %shard_map.257 = (f32[64,4352]{1,0:T(8,128)}, f32[32,3072]{1,0:T(8,128)}, f32[8,128]{1,0:T(8,128)}, f32[8,128]{1,0:T(8,128)}) custom-call(bf16[2,2,2,2,64,1536]{5,4,3,2,1,0:T(8,128)(2,1)} %bitcast.118, bf16[2,2,2,2,64,512]{5,4,3,2,1,0:T(8,128)(2,1)} %bitcast.120, bf16[2,2,2,2,64,2048]{5,4,3,2,1,0:T(8,128)(2,1)} %bitcast.110, ...), custom_call_target="tpu_custom_call" | custom-call | tf_op jit(solution)/shard_map/pallas_call | solution.py:389
  702.8 1.3 slice_bitcast_fusion
  704.1 1.2 slice.172
  706.1 1.9 multiply_subtract_fusion
  708.1 2.8 copy.163
  713.2 2.8 copy.165
  717.2 1.3 multiply_subtract_fusion.3
  718.5 1.4 multiply_subtract_fusion.2
  (133 shorter events, 24.0 us)
Async XLA Ops:
  7.2 2.4 copy-start.14
  7.2 2.6 copy-start.24
  7.2 2.6 copy-start.23
  7.2 179.5 %all-gather.2.cloned.1.call-start = ((), (), s32[]{:S(2)}) async-start(), calls=%async_computation.1 | async-start | bytes 4456448 | tf_op jit(solution)/shard_map/all_gather | solution.py:1079
  8.8 103.9 %copy-start.8 = (bf16[1,588,1024]{2,1,0:T(8,128)(2,1)S(1)}, bf16[1,588,1024]{2,1,0:T(8,128)(2,1)}, u32[]{:S(2)}) copy-start(bf16[1,588,1024]{2,1,0:T(8,128)(2,1)} %param.22) | copy-start | bytes 3612676
  8.8 104.0 %copy-start.22 = (s32[1,2,1176]{2,1,0:T(2,128)S(1)}, s32[1,2,1176]{2,1,0:T(2,128)}, u32[]{:S(2)}) copy-start(s32[1,2,1176]{2,1,0:T(2,128)} %param.23) | copy-start | bytes 28228
  107.9 2.0 copy-start
  109.9 1.7 copy-start.1
  111.6 1.0 copy-start.2
  112.6 448.5 %reduce-scatter.2.cloned.1.call-start = ((), (), s32[]{:S(2)}) async-start(), calls=%async_computation.2 | async-start | bytes 4456448 | tf_op jit(solution)/shard_map/reduce_scatter | solution.py:1088
  112.7 3.6 collective-permute-start
  171.6 5.1 collective-permute-start.1
  207.6 7.7 %collective-permute-start.2 = (bf16[1200,1024]{1,0:T(8,128)(2,1)}, bf16[1200,1024]{1,0:T(8,128)(2,1)S(1)}, u32[]{:S(2)}, u32[]{:S(2)}) collective-permute-start(bf16[1200,1024]{1,0:T(8,128)(2,1)} %get-tuple-element.86), channel_id=1, source_target_pairs={{0,1},{1,0},{2,3},{3,2},{4,5},{5,4},{6,7},{7,6},{8,9},{9,8},{10,11... | collective-permute-start | bytes 7372808 | tf_op jit(solution)/shard_map/ppermute | solution.py:1029
  207.6 36.3 %collective-permute-start.5 = (bf16[512,3072]{1,0:T(8,128)(2,1)}, bf16[512,3072]{1,0:T(8,128)(2,1)}, u32[]{:S(2)}, u32[]{:S(2)}) collective-permute-start(bf16[512,3072]{1,0:T(8,128)(2,1)} %bitcast.116), channel_id=1, source_target_pairs={{0,1},{1,0},{2,3},{3,2},{4,5},{5,4},{6,7},{7,6},{8,9},{9,8},{10,11... | collective-permute-start | bytes 9437192 | tf_op jit(solution)/shard_map/ppermute | solution.py:1029
  219.8 1.4 copy-start.10
  221.2 16.4 %collective-permute-start.3 = (bf16[1176,256]{1,0:T(8,128)(2,1)S(1)}, bf16[1176,256]{1,0:T(8,128)(2,1)}, u32[]{:S(2)}, u32[]{:S(2)}) collective-permute-start(bf16[1176,256]{1,0:T(8,128)(2,1)S(1)} %slice.235), channel_id=1, source_target_pairs={{0,16},{1,17},{2,18},{3,19},{4,20},{5,21},{6,22},{7,23},{8,24},{9,... | collective-permute-start | bytes 1806344 | tf_op jit(solution)/shard_map/ppermute | solution.py:1024
  237.7 12.1 %collective-permute-start.4 = (bf16[1176,256]{1,0:T(8,128)(2,1)}, bf16[1176,256]{1,0:T(8,128)(2,1)}, u32[]{:S(2)}, u32[]{:S(2)}) collective-permute-start(bf16[1176,256]{1,0:T(8,128)(2,1)} %collective-permute-done.3), channel_id=1, source_target_pairs={{0,1},{1,0},{2,3},{3,2},{4,5},{5,4},{6,7},{7,6},{8,9},{9,8},{10,11... | collective-permute-start | bytes 1806344 | tf_op jit(solution)/shard_map/ppermute | solution.py:1029
  240.7 3.2 copy-start.9
  390.1 2.2 collective-permute-start.6
  392.5 24.1 %collective-permute-start.7 = (bf16[1176,256]{1,0:T(8,128)(2,1)S(1)}, bf16[1176,256]{1,0:T(8,128)(2,1)S(1)}, u32[]{:S(2)}, u32[]{:S(2)}) collective-permute-start(bf16[1176,256]{1,0:T(8,128)(2,1)S(1)} %add_convert_fusion.2), channel_id=1, source_target_pairs={{16,0},{17,1},{18,2},{19,3},{20,4},{21,5},{22,6},{23,7},{24,8},{25... | collective-permute-start | bytes 1806344 | tf_op jit(solution)/shard_map/ppermute | solution.py:1024
  416.6 0.8 copy-start.17
  417.5 4.9 copy-start.3
  417.5 4.9 collective-permute-start.8
  453.0 6.1 collective-permute-start.9
  458.7 76.6 %collective-permute-start.11 = (bf16[512,3072]{1,0:T(8,128)(2,1)}, bf16[512,3072]{1,0:T(8,128)(2,1)}, u32[]{:S(2)}, u32[]{:S(2)}) collective-permute-start(bf16[512,3072]{1,0:T(8,128)(2,1)} %get-tuple-element.111), channel_id=1, source_target_pairs={{0,1},{1,0},{2,3},{3,2},{4,5},{5,4},{6,7},{7,6},{8,9},{9,8},{10,11... | collective-permute-start | bytes 9437192 | tf_op jit(solution)/shard_map/ppermute | solution.py:1029
  470.5 55.3 %copy-start.21 = (f32[8,512]{1,0:T(8,128)S(1)}, f32[8,512]{1,0:T(8,128)}, u32[]{:S(2)}) copy-start(f32[8,512]{1,0:T(8,128)} %get-tuple-element.114) | copy-start | bytes 49156
  470.5 55.7 %copy-start.29 = (f32[2]{0:T(128)S(1)}, f32[2]{0:T(128)}, u32[]{:S(2)}) copy-start(f32[2]{0:T(128)} %param.38) | copy-start | bytes 28
  525.7 16.9 %collective-permute-start.10 = (bf16[1200,1024]{1,0:T(8,128)(2,1)}, bf16[1200,1024]{1,0:T(8,128)(2,1)}, u32[]{:S(2)}, u32[]{:S(2)}) collective-permute-start(bf16[1200,1024]{1,0:T(8,128)(2,1)} %get-tuple-element.99.refs_1_), channel_id=1, source_target_pairs={{0,1},{1,0},{2,3},{3,2},{4,5},{5,4},{6,7},{7,6},{8,9},{9,8},{10,11... | collective-permute-start | bytes 7372808 | tf_op jit(solution)/shard_map/ppermute | solution.py:1029
  525.8 6.0 collective-permute-start.12
  529.5 2.3 copy-start.18
  542.6 10.5 %copy-start.6 = (f32[588,1024]{1,0:T(8,128)S(1)}, f32[588,1024]{1,0:T(8,128)}, u32[]{:S(2)}) copy-start(f32[588,1024]{1,0:T(8,128)} %reshape_reshape.6) | copy-start | bytes 7225348
  561.2 144.8 %copy-start.16 = (bf16[64,2048]{1,0:T(8,128)(2,1)S(1)}, bf16[64,2048]{1,0:T(8,128)(2,1)}, u32[]{:S(2)}) copy-start(bf16[64,2048]{1,0:T(8,128)(2,1)} %reduce-scatter.2.cloned.1.call-done.refs_6_) | copy-start | bytes 786436
  561.2 144.9 %copy-start.12 = (f32[64,1,6400]{2,1,0:T(1,128)S(1)}, f32[64,1,6400]{2,1,0:T(1,128)}, u32[]{:S(2)}) copy-start(f32[64,1,6400]{2,1,0:T(1,128)} %param.26) | copy-start | bytes 4915204
  561.2 144.9 %copy-start.13 = (f32[64,1,6400]{2,1,0:T(1,128)S(1)}, f32[64,1,6400]{2,1,0:T(1,128)}, u32[]{:S(2)}) copy-start(f32[64,1,6400]{2,1,0:T(1,128)} %param.25) | copy-start | bytes 4915204
  701.8 4.3 copy-start.7
  708.0 2.9 copy-start.15
  708.0 2.9 copy-start.19
  708.0 2.9 copy-start.20
  710.9 2.3 copy-start.30
  712.0 5.2 copy-start.25
  712.0 5.2 copy-start.26
  712.0 6.5 copy-start.27
  712.0 6.5 copy-start.28
Sparse Core Ops, SparseCore 0:
  112.8 73.9 all-gather.1
  453.2 92.9 reduce-scatter.1

commit v3 on v2

--- a/solution.py
+++ b/solution.py
@@ -10,7 +10,6 @@
 from jax.sharding import PartitionSpec as P
 
 FF = 4096
-FFD = 2048
 GRID = 196
 IMG = 12
 PARAMS = 16259072
@@ -20,6 +19,7 @@
 ADAM_EPS = 1e-08
 WEIGHT_DECAY = 0.05
 ROW_BLOCK = 240
+MOST_VISIBLE = 73
 GATHER_ORDERS = ("hlxy", "hlyx", "hlxy", "hlyx", "yxhl")
 SCATTER_ORDERS = ("xylh", "yxlh", "xylh", "yxlh", "lhxy")
 
@@ -390,6 +390,7 @@
 
 
 HEADS = 16
+TOGETHER = 4
 NORM_EPS = 1e-06
 MASKED = -1e30
 LOW = jnp.bfloat16
@@ -423,52 +424,76 @@
 
 
 def decoder_kernel(
-    grid_cells,
     length,
+    flag,
     target_row,
     target_column,
-    visible,
+    visible_own,
+    visible_other,
     mask,
     position,
     gains,
-    qkv_t,
-    qkv_w,
-    out_t,
-    out_w,
-    up_w,
-    down_w,
+    pack_own,
+    pack_other,
     cotangent,
     decoded,
-    grad_visible,
-    grad_qkv,
-    grad_out,
-    grad_up,
-    grad_down,
+    grad_keep,
+    grad_send,
+    grad_own,
+    grad_other,
     grad_gains,
+    qkv_t,
+    out_t,
     qkv_rows,
     shares,
     mixture,
     hidden,
     slope,
     grad_rows,
+    grad_visible,
+    grad_qkv,
+    grad_out,
+    grad_up,
+    grad_down,
 ):
     image = pl.program_id(0)
     rows, width = decoded.shape[1], decoded.shape[2]
     head = width // HEADS
     units = hidden.shape[1]
+    part, half = width // 2, units // 2
+    up_at, down_at = 4 * part, 4 * part + half
     scaling = head ** (-0.5)
+    packs = (pack_own, pack_other)
+    halves = ((slice(0, half), pack_own), (slice(half, units), pack_other))
 
     @pl.when(image == 0)
     def _():
         for ref in (grad_visible, grad_qkv, grad_out, grad_up, grad_down, grad_gains):
             ref[...] = jnp.zeros_like(ref)
+        for which in range(4):
+            for k, pack in enumerate(packs):
+                at = (2 * which + k) * part
+                piece = jnp.transpose(pack[:, which * part : (which + 1) * part])
+                if which < 3:
+                    qkv_t[at : at + part, :] = piece
+                else:
+                    out_t[k * part : (k + 1) * part, :] = piece
 
     packed = target_row.shape[1]
     cell = lax.broadcasted_iota(jnp.int32, (rows, packed), 0)
     wanted = jnp.where(cell < length, cell + image * length, -7)
     chosen = (target_row[...] == wanted).astype(WIDE)
     seen = jnp.max(chosen, axis=1, keepdims=True)
-    placed = mm(chosen.astype(LOW), visible[...])
+    chosen = chosen.astype(LOW)
+    placed_own, placed_other = mm(chosen, visible_own[...]), mm(chosen, visible_other[...])
+    left = flag[0] > 0
+    placed = jnp.concatenate(
+        [
+            jnp.where(left, placed_own, placed_other),
+            jnp.where(left, placed_other, placed_own),
+        ],
+        axis=1,
+    )
     stream = jnp.where(seen > 0.0, placed, mask[...]) + position[...]
 
     unit_one, scale_one = centre(stream)
@@ -477,32 +502,31 @@
 
     key_index = lax.broadcasted_iota(jnp.int32, (rows, rows), 0)
 
-    def attend(h, carry):
-        begin = pl.multiple_of(h * head, head)
-        q = qkv_rows[pl.ds(begin, head), :]
-        k = qkv_rows[pl.ds(pl.multiple_of(width + begin, head), head), :]
-        v = qkv_rows[pl.ds(pl.multiple_of(2 * width + begin, head), head), :]
-        scores = mm(k, q, 0, 0) * scaling
-        scores = jnp.where(key_index < length, scores, MASKED)
-        weights = jnp.exp(scores - jnp.max(scores, axis=0, keepdims=True))
-        share = weights * (1.0 / jnp.sum(weights, axis=0, keepdims=True))
-        shares[h] = share
-        mixture[pl.ds(begin, head), :] = mm(v, share.astype(LOW)).astype(LOW)
-        return carry
-
-    lax.fori_loop(0, HEADS, attend, 0, unroll=4)
+    def lines(which, h):
+        return slice(which * width + h * head, which * width + (h + 1) * head)
+
+    for begin in range(0, HEADS, TOGETHER):
+        group = range(begin, begin + TOGETHER)
+        scores = [mm(qkv_rows[lines(1, h), :], qkv_rows[lines(0, h), :], 0, 0) * scaling for h in group]
+        scores = [jnp.where(key_index < length, s, MASKED) for s in scores]
+        weights = [jnp.exp(s - jnp.max(s, axis=0, keepdims=True)) for s in scores]
+        group_shares = [w * (1.0 / jnp.sum(w, axis=0, keepdims=True)) for w in weights]
+        for h, share in zip(group, group_shares):
+            shares[h] = share
+            mixture[lines(0, h), :] = mm(qkv_rows[lines(2, h), :], share.astype(LOW)).astype(LOW)
     mixed = mixture[...]
-    after = stream + mm(jnp.transpose(mixed), out_w[...], 1, 1)
+    after = stream + mm(mixed, out_t[...], 0, 0)
     unit_two, scale_two = centre(after)
     second = (unit_two * gains[2:3] + gains[3:4]).astype(LOW)
     piece = 256
-    result = after
     for c in range(0, units, piece):
-        z = mm(second, up_w[:, c : c + piece])
+        pack, at = packs[c // half], up_at + c % half
+        z = mm(second, pack[:, at : at + piece])
         h, g = gelu_pair(z)
         hidden[:, c : c + piece] = h.astype(LOW)
         slope[:, c : c + piece] = g
-    decoded[0] = after + mm(hidden[...], down_w[...], 1, 1)
+    fed = [mm(hidden[:, cut], pack[:, down_at : down_at + half], 1, 1) for cut, pack in halves]
+    decoded[0] = after + (fed[0] + fed[1])
 
     grad_low = cotangent[0]
     grad_result = grad_low.astype(WIDE)
@@ -511,10 +535,12 @@
     for c in range(0, units, piece):
         cut = slice(c, c + piece)
         grad_down[:, cut] += mm(turned, hidden[:, cut])
-        grad_z = (mm(grad_low, down_w[:, cut]) * slope[:, cut]).astype(LOW)
+        pack, at = packs[c // half], down_at + c % half
+        grad_z = (mm(grad_low, pack[:, at : at + piece]) * slope[:, cut]).astype(LOW)
         hidden[:, cut] = grad_z
         grad_up[:, cut] += mm(second_turned, grad_z)
-    grad_second = mm(hidden[...], up_w[...], 1, 1)
+    pulled = [mm(hidden[:, cut], pack[:, up_at : up_at + half], 1, 1) for cut, pack in halves]
+    grad_second = pulled[0] + pulled[1]
     grad_after = grad_result + centre_back(unit_two, scale_two, gains[2:3], grad_second)
     grad_gains[2:3] += jnp.sum(grad_second * unit_two, axis=0, keepdims=True)
     grad_gains[3:4] += jnp.sum(grad_second, axis=0, keepdims=True)
@@ -523,30 +549,26 @@
     grad_out[...] += mm(mixed, after_low)
     grad_rows[...] = mm(out_t[...], after_low, 1, 1).astype(LOW)
 
-    def attend_back(h, carry):
-        begin = pl.multiple_of(h * head, head)
-        key_at = pl.multiple_of(width + begin, head)
-        value_at = pl.multiple_of(2 * width + begin, head)
-        q = qkv_rows[pl.ds(begin, head), :]
-        k = qkv_rows[pl.ds(key_at, head), :]
-        v = qkv_rows[pl.ds(value_at, head), :]
-        grad_mixture = grad_rows[pl.ds(begin, head), :]
-        share = shares[h]
-        grad_share = mm(v, grad_mixture, 0, 0)
-        grad_value = mm(grad_mixture, share.astype(LOW), 1, 1)
-        inner = jnp.sum(share * grad_share, axis=0, keepdims=True)
-        grad_score = (share * (grad_share - inner)).astype(LOW)
-        grad_query = mm(k, grad_score) * scaling
-        grad_key = mm(q, grad_score, 1, 1) * scaling
-        qkv_rows[pl.ds(begin, head), :] = grad_query.astype(LOW)
-        qkv_rows[pl.ds(key_at, head), :] = grad_key.astype(LOW)
-        qkv_rows[pl.ds(value_at, head), :] = grad_value.astype(LOW)
-        return carry
-
-    lax.fori_loop(0, HEADS, attend_back, 0, unroll=4)
+    for begin in range(0, HEADS, TOGETHER):
+        group = range(begin, begin + TOGETHER)
+        queries = [qkv_rows[lines(0, h), :] for h in group]
+        keys = [qkv_rows[lines(1, h), :] for h in group]
+        values = [qkv_rows[lines(2, h), :] for h in group]
+        grads_in = [grad_rows[lines(0, h), :] for h in group]
+        grad_shares = [mm(v, g, 0, 0) for v, g in zip(values, grads_in)]
+        grad_values = [mm(g, shares[h].astype(LOW), 1, 1) for g, h in zip(grads_in, group)]
+        grad_scores = []
+        for h, g in zip(group, grad_shares):
+            share = shares[h]
+            inner = jnp.sum(share * g, axis=0, keepdims=True)
+            grad_scores.append((share * (g - inner)).astype(LOW))
+        for k, h in enumerate(group):
+            qkv_rows[lines(0, h), :] = (mm(keys[k], grad_scores[k]) * scaling).astype(LOW)
+            qkv_rows[lines(1, h), :] = (mm(queries[k], grad_scores[k], 1, 1) * scaling).astype(LOW)
+            qkv_rows[lines(2, h), :] = grad_values[k].astype(LOW)
     grads = qkv_rows[...]
     grad_qkv[...] += mm(grads, first)
-    grad_first = jnp.transpose(mm(qkv_w[...], grads))
+    grad_first = mm(grads, qkv_t[...], 0, 0)
     grad_stream = grad_after + centre_back(unit_one, scale_one, gains[0:1], grad_first)
     grad_gains[0:1] += jnp.sum(grad_first * unit_one, axis=0, keepdims=True)
     grad_gains[1:2] += jnp.sum(grad_first, axis=0, keepdims=True)
@@ -556,19 +578,33 @@
     chosen_back = (target_column[...] == wanted_lane).astype(WIDE).astype(LOW)
     grad_visible[...] += mm(chosen_back, grad_stream.astype(LOW))
 
+    @pl.when(image == pl.num_programs(0) - 1)
+    def _():
+        gathered = grad_visible[...].astype(LOW)
+        one, two = gathered[:, :part], gathered[:, part:]
+        grad_keep[...] = jnp.where(left, one, two)
+        grad_send[...] = jnp.where(left, two, one)
+        for k, ref in enumerate((grad_own, grad_other)):
+            for which in range(4):
+                at = (2 * which + k) * part
+                piece = grad_qkv[at : at + part, :] if which < 3 else grad_out[k * part : (k + 1) * part, :]
+                ref[:, which * part : (which + 1) * part] = jnp.transpose(piece.astype(LOW))
+            cut = slice(k * half, (k + 1) * half)
+            ref[:, up_at:down_at] = grad_up[:, cut].astype(LOW)
+            ref[:, down_at:] = grad_down[:, cut].astype(LOW)
+
 
 def decoder_step(
-    visible, target, mask, position, gains, qkv_w, out_w, up_w, down_w, cotangent, images
+    left, visible_own, visible_other, target, mask, position, gains, pack_own, pack_other, cotangent, images
 ):
     length, width = position.shape
     rows = -(-length // 16) * 16
-    packed = -(-visible.shape[0] // 128) * 128
-    spare = packed - visible.shape[0]
-    units = up_w.shape[1]
-    visible = jnp.pad(visible, ((0, spare), (0, 0)))
-    target = jnp.pad(target, (0, spare), constant_values=-1)
-    longer = ((0, 0), (0, rows - length), (0, 0))
-    cotangent = jnp.pad(cotangent.reshape(images, length, width), longer)
+    packed = visible_own.shape[0]
+    columns = pack_own.shape[1]
+    units = columns - 2 * width
+    cotangent = jnp.pad(
+        cotangent.reshape(images, length, width), ((0, 0), (0, rows - length), (0, 0))
+    )
     position = jnp.pad(position, ((0, rows - length), (0, 0)))
 
     def fixed(shape):
@@ -576,70 +612,64 @@
 
     per_image = pl.BlockSpec((1, rows, width), lambda i: (i, 0, 0))
     grads = [
-        ((packed, width), WIDE),
-        ((3 * width, width), WIDE),
-        ((width, width), WIDE),
-        ((width, units), WIDE),
-        ((width, units), WIDE),
+        ((packed, width // 2), LOW),
+        ((packed, width // 2), LOW),
+        ((width, columns), LOW),
+        ((width, columns), LOW),
         ((8, width), WIDE),
     ]
-    results = pl.pallas_call(
-        functools.partial(decoder_kernel, images * length, length),
+    decoded, keep, send, grad_own, grad_other, grad_gains = pl.pallas_call(
+        functools.partial(decoder_kernel, length),
         grid=(images,),
         out_shape=[jax.ShapeDtypeStruct((images, rows, width), WIDE)]
         + [jax.ShapeDtypeStruct(s, d) for s, d in grads],
         in_specs=[
+            pl.BlockSpec(memory_space=pltpu.SMEM),
             fixed((1, packed)),
             fixed((packed, 1)),
-            fixed((packed, width)),
+            fixed((packed, width // 2)),
+            fixed((packed, width // 2)),
             fixed((1, width)),
             fixed((rows, width)),
             fixed((4, width)),
-            fixed((3 * width, width)),
-            fixed((width, 3 * width)),
-            fixed((width, width)),
-            fixed((width, width)),
-            fixed((width, units)),
-            fixed((width, units)),
+            fixed((width, columns)),
+            fixed((width, columns)),
             per_image,
         ],
         out_specs=[per_image] + [fixed(s) for s, _ in grads],
         scratch_shapes=[
+            pltpu.VMEM((3 * width, width), LOW),
+            pltpu.VMEM((width, width), LOW),
             pltpu.VMEM((3 * width, rows), LOW),
             pltpu.VMEM((HEADS, rows, rows), WIDE),
             pltpu.VMEM((width, rows), LOW),
             pltpu.VMEM((rows, units), LOW),
             pltpu.VMEM((rows, units), WIDE),
             pltpu.VMEM((width, rows), LOW),
+            pltpu.VMEM((packed, width), WIDE),
+            pltpu.VMEM((3 * width, width), WIDE),
+            pltpu.VMEM((width, width), WIDE),
+            pltpu.VMEM((width, units), WIDE),
+            pltpu.VMEM((width, units), WIDE),
         ],
         compiler_params=pltpu.CompilerParams(
             dimension_semantics=("arbitrary",), vmem_limit_bytes=60 * 2**20
         ),
     )(
+        left.astype(jnp.int32).reshape(1),
         target[None, :],
         target[:, None],
-        visible,
+        visible_own,
+        visible_other,
         mask[None, :],
         position,
         gains,
-        qkv_w.T,
-        qkv_w,
-        out_w.T,
-        out_w,
-        up_w,
-        down_w,
+        pack_own,
+        pack_other,
         cotangent,
     )
-    decoded, grad_visible, grad_qkv, grad_out, grad_up, grad_down, grad_gains = results
-    return (
-        decoded[:, :length].reshape(images * length, width),
-        grad_visible[: packed - spare],
-        grad_qkv,
-        grad_out,
-        grad_up,
-        grad_down,
-        grad_gains[:4],
-    )
+    decoded = decoded[:, :length].reshape(images * length, width)
+    return decoded, keep, send, grad_own, grad_other, grad_gains[:4]
 
 
 TILE = 256
@@ -689,18 +719,20 @@
 
         def inner(j, state):
             same = slots_column[pl.ds(pl.multiple_of(j * TILE, TILE), TILE), :] == slot_i
-            result = []
-            for g, h in enumerate(heads):
-                high, total, mixed = state[g]
-                scores = mm(turned[at(1, h, j)], queries[g], 0, 0) * scaling
-                scores = jnp.where(same, scores, MASKED)
-                higher = jnp.maximum(high, jnp.max(scores, axis=0, keepdims=True))
-                weights = jnp.exp(scores - higher)
-                fix = jnp.exp(high - higher)
-                total = total * fix + jnp.sum(weights, axis=0, keepdims=True)
-                mixed = mixed * fix + mm(turned[at(2, h, j)], weights.astype(LOW))
-                result.append((higher, total, mixed))
-            return tuple(result)
+            scores = [mm(turned[at(1, h, j)], q, 0, 0) * scaling for h, q in zip(heads, queries)]
+            scores = [jnp.where(same, s, MASKED) for s in scores]
+            highs = [
+                jnp.maximum(state[g][0], jnp.max(s, axis=0, keepdims=True))
+                for g, s in enumerate(scores)
+            ]
+            weights = [jnp.exp(s - high) for s, high in zip(scores, highs)]
+            fixes = [jnp.exp(state[g][0] - high) for g, high in enumerate(highs)]
+            sums = [jnp.sum(w, axis=0, keepdims=True) for w in weights]
+            mixes = [mm(turned[at(2, h, j)], w.astype(LOW)) for h, w in zip(heads, weights)]
+            return tuple(
+                (highs[g], state[g][1] * fixes[g] + sums[g], state[g][2] * fixes[g] + mixes[g])
+                for g in range(GROUP)
+            )
 
         begin = (
             jnp.full((1, TILE), MASKED, WIDE),
@@ -801,18 +833,24 @@
             def inner(j, state):
                 lane_j = pl.ds(pl.multiple_of(j * TILE, TILE), TILE)
                 same = slots_column[lane_j, :] == slot_i
-                result = []
-                for g, h in enumerate(heads):
-                    cut = slice(g * head, (g + 1) * head)
-                    keys, values = turned[at(1, h, j)], turned[at(2, h, j)]
-                    scores = jnp.where(same, mm(keys, queries[g], 0, 0) * scaling, MASKED)
-                    share = jnp.exp(scores - logs[g])
-                    grad_share = mm(values, grads[g], 0, 0)
-                    grad_score = (share * (grad_share - sums[g])).astype(LOW)
-                    value_sum[cut, lane_j] += mm(grads[g], share.astype(LOW), 1, 1)
-                    key_sum[cut, lane_j] += mm(queries[g], grad_score, 1, 1)
-                    result.append(state[g] + mm(keys, grad_score))
-                return tuple(result)
+                cuts = [slice(g * head, (g + 1) * head) for g in range(GROUP)]
+                keys = [turned[at(1, h, j)] for h in heads]
+                values = [turned[at(2, h, j)] for h in heads]
+                scores = [mm(k, q, 0, 0) * scaling for k, q in zip(keys, queries)]
+                grad_shares = [mm(v, g, 0, 0) for v, g in zip(values, grads)]
+                shares = [
+                    jnp.exp(jnp.where(same, s, MASKED) - log) for s, log in zip(scores, logs)
+                ]
+                grad_scores = [
+                    (s * (g - total)).astype(LOW) for s, g, total in zip(shares, grad_shares, sums)
+                ]
+                for g, cut in enumerate(cuts):
+                    value_sum[cut, lane_j] += mm(grads[g], shares[g].astype(LOW), 1, 1)
+                for g, cut in enumerate(cuts):
+                    key_sum[cut, lane_j] += mm(queries[g], grad_scores[g], 1, 1)
+                return tuple(
+                    state[g] + mm(keys[g], grad_scores[g]) for g in range(GROUP)
+                )
 
             begin = (jnp.zeros((head, TILE), WIDE),) * GROUP
             state = lax.fori_loop(bounds[i, 0], bounds[i, 1], inner, begin)
@@ -1029,15 +1067,6 @@
     return lax.ppermute(value, "mp", [(i, (i + 1) % length) for i in range(length)])
 
 
-def on_side(active, action, *operands):
-    def skipped(*values):
-        return jax.tree.map(
-            lambda leaf: jnp.zeros(leaf.shape, leaf.dtype), jax.eval_shape(action, *values)
-        )
-
-    return lax.cond(active, action, skipped, *operands)
-
-
 def is_fast():
     return lax.axis_size("section") == 2 and lax.axis_size("dp") == 8
 
@@ -1133,14 +1162,6 @@
     first = jnp.min(jnp.where(meet, index, tiles.shape[0]), axis=1)
     last = jnp.max(jnp.where(meet, index + 1, 0), axis=1)
     return jnp.stack([first, last], axis=1)
-
-
-def cut_columns(matrix, widths):
-    parts, column = [], 0
-    for w in widths:
-        parts.append(matrix[:, column : column + w])
-        column += w
-    return parts
 
 
 def update(
@@ -1203,9 +1224,7 @@
     head = width // HEADS
     dec_width = dec_position.shape[1]
     dec_part = dec_width // mp_count
-    dec_units = FFD // mp_count
     widths = (3 * part, part, units, units, dec_part)
-    dec_widths = (dec_part,) * 4 + (dec_units,) * 2
     slots = jnp.pad(slot_ids, (0, lanes - real_rows), constant_values=IMG + 1)
     ranges = key_ranges(slots)
 
@@ -1237,41 +1256,30 @@
         stream, mix_own, partner(mix_own), enc_gains, up_w, down_w, ROW_BLOCK
     )
     encoded = (after + (feed_own.astype(WIDE) + partner(feed_own).astype(WIDE))).astype(LOW)
-    projected = mm(encoded, projection)[:real_rows].astype(LOW)
+    shown = min(real_rows, -(-IMG * MOST_VISIBLE // 16) * 16)
+    packed = -(-shown // 128) * 128
+    projected = mm(encoded[:shown], projection).astype(LOW)
     arrived = from_behind(projected, "section", 1)
-    visible = halves(arrived, partner(arrived), 1)
-
-    def join(own, other):
-        pieces = list(zip(cut_columns(own, dec_widths), cut_columns(other, dec_widths)))
-        qkv = jnp.concatenate([p for pair in pieces[:3] for p in pair], axis=1)
-        return (qkv, *(jnp.concatenate(pair, axis=1) for pair in pieces[3:]))
-
-    dec_mats = on_side(decoder_side, join, dec_own, partner(dec_own))
-    decoded, grad_visible, grad_qkv, grad_out, grad_up, grad_down, dec_gain_grad = decoder_step(
-        visible, target, mask_token, dec_position, dec_gains, *dec_mats, act_in[0], local_images
-    )
-
-    seen = grad_visible.astype(LOW)
-    left, right = seen[:, :dec_part], seen[:, dec_part:]
-    returned = jnp.where(first_half, left, right).astype(WIDE) + partner(
-        jnp.where(first_half, right, left)
-    ).astype(WIDE)
-    grad_projected = from_behind(returned.astype(LOW), "section", -1)
-    grad_projected = jnp.pad(grad_projected, ((0, rows - real_rows), (0, 0)))
-
-    def dec_packs(grad_qkv, grad_out, grad_up, grad_down):
-        pieces = [grad_qkv.T[:, k * dec_part : (k + 1) * dec_part] for k in range(6)]
-        pieces += [grad_out.T[:, :dec_part], grad_out.T[:, dec_part:]]
-        for matrix in (grad_up, grad_down):
-            pieces += [matrix[:, :dec_units], matrix[:, dec_units:]]
-        return tuple(
-            jnp.concatenate(pieces[k::2], axis=1).astype(kind) for k, kind in ((0, WIDE), (1, LOW))
-        )
-
-    pack_own, pack_other = on_side(
-        decoder_side, dec_packs, grad_qkv, grad_out, grad_up, grad_down
-    )
-    dec_grad = (pack_own + partner(pack_other).astype(WIDE)).astype(LOW)
+    arrived = jnp.pad(arrived, ((0, packed - shown), (0, 0)))
+    seen_target = jnp.pad(target[:shown], (0, packed - shown), constant_values=-1)
+    decoded, grad_keep, grad_send, dec_grad_own, dec_grad_other, dec_gain_grad = decoder_step(
+        first_half,
+        arrived,
+        partner(arrived),
+        seen_target,
+        mask_token,
+        dec_position,
+        dec_gains,
+        dec_own,
+        partner(dec_own),
+        act_in[0],
+        local_images,
+    )
+    returned = grad_keep[:shown] + partner(grad_send[:shown])
+    grad_projected = from_behind(returned, "section", -1)
+    grad_projected = jnp.pad(grad_projected, ((0, rows - shown), (0, 0)))
+    dec_grad = dec_grad_own.astype(WIDE) + partner(dec_grad_other).astype(WIDE)
+    dec_grad = dec_grad.astype(LOW)
     dec_gain_grad = dec_gain_grad + partner(dec_gain_grad)
 
     grad_projection = mm(encoded, grad_projected, 0, 0).astype(LOW)

time: 740 us -> 650 us (0.88)
  Pallas kernels: 555 us -> 465 us
  waiting for transfers between devices: 63.2 us -> 72.6 us
    pallas_call x1, Pallas kernels: 135 us -> 84.3 us  [decoder_step(): pl.pallas_call(functools.partial(decoder_kernel, length), grid=(images,),...]
    pallas_call x1, Pallas kernels: 52.3 us -> 35 us  [encoder_attend(): pl.pallas_call(functools.partial(attend_kernel, head), in_specs=[pl.Block...]
    pallas_call x1, Pallas kernels: 141 us -> 125 us  [scatter_grads(): return call(*views, summed)]
    all_gather x1, waiting for transfers between devices: 10 us -> 25 us  [gather_all(): down = lax.all_gather(low_down, ('section', 'dp'), axis=0, tiled=True)]
    ppermute x2, waiting for transfers between devices: 34.9 us -> 23.2 us  [from_behind(): return lax.ppermute(value, axis, pairs)]
    unnamed x64 -> x80, local copies, waits for them, and re-layouts: 18.9 us -> 21.3 us
  transfers between devices with their start and end apart: 15 -> 15, of which waited for: 7 -> 8; matrix products, arithmetic and copies ran while one was open for 7% -> 7% of each run, Pallas kernels for 18% -> 17%
where the time goes in v3:
time: 650 us; the launch traced here: 640 us
  Pallas kernels  465 us (72%)
  waiting for transfers between devices  72.6 us (11%)
  local copies, waits for them, and re-layouts  48.6 us (7%)
  other arithmetic  23.5 us (4%)
  between operations  17.8 us (3%)
  starting transfers between devices  7.27 us (1%)
    pallas_call x1, Pallas kernels, scatter_grads(): return call(*views, summed)  125 us
    pallas_call x1, Pallas kernels, gather_weights(): results = call(*shards)  98.2 us
    pallas_call x1, Pallas kernels, decoder_step(): pl.pallas_call(functools.partial(decoder_kernel, length), grid=(images,),...  84.3 us
    pallas_call x1, Pallas kernels, encoder_attend_back(): pl.pallas_call(functools.partial(attend_back_kernel, head), in_specs=[pl....  48.9 us
    pallas_call x1, Pallas kernels, encoder_attend(): pl.pallas_call(functools.partial(attend_kernel, head), in_specs=[pl.Block...  35 us
    pallas_call x1, Pallas kernels, encoder_feed_back(): pl.pallas_call(feed_back_kernel, grid=(units // piece,), in_specs=[pl.Blo...  30.7 us
    all_gather x1, waiting for transfers between devices, gather_all(): down = lax.all_gather(low_down, ('section', 'dp'), axis=0, tiled=True)  25 us
    ppermute x11, waiting for transfers between devices, partner(): lax.ppermute(value, 'mp', [(i, (i + 1) % length) for i in range(length)])  24.4 us
  transfers between devices with their start and end apart: 15, of which 8 were waited for; matrix products, arithmetic and copies ran while one was open for 7% of the time, Pallas kernels for 17%

profile of v3, /device:TPU:0, one launch (start us, length us, event | category | flops | bytes accessed | tf_op | source)
XLA Modules:
  0.0 639.7 jit_solution(14419695318064099564)
XLA Ops:
  7.3 1.6 copy.182
  9.9 98.2 %shard_map.249 = (bf16[2,2,2,2,64,1536]{5,4,3,2,1,0:T(8,128)(2,1)S(1)}, bf16[2,2,2,2,64,512]{5,4,3,2,1,0:T(8,128)(2,1)S(1)}, bf16[2,2,2,2,64,2048]{5,4,3,2,1,0:T...) custom-call(bf16[64,4352]{1,0:T(8,128)(2,1)S(1)} %pad_maximum_fusion, ...), custom_call_target="tpu_custom_call" | custom-call | tf_op jit(solution)/shard_map/pallas_call | solution.py:157
  108.1 2.0 copy-done
  110.1 1.6 copy-done.1
  114.5 1.1 broadcast_in_dim.71.slots_column
  118.0 3.0 maximum_select_fusion
  121.0 1.7 pad.36.stream.refs_0_
  122.7 35.0 %shard_map.250 = (bf16[1200,1024]{1,0:T(8,128)(2,1)}, bf16[1536,1280]{1,0:T(8,128)(2,1)}, bf16[512,1280]{1,0:T(8,128)(2,1)}, f32[8,1280]{1,0:T(8,128)}, bf16[1200,1024]{1,0:T(8,128)(2,1)}) custom-call(s32[5,2]{1,0:T(8,128)} %copy.129.bounds, bf16[1200,1024]{1,0:T(8,128)(2,1)} %pad.36.stream.refs_0_, s32[1,1280]{1,0:T(1,128)} %broadcast_in_dim.61.slots_row, ...), custom_call_target="tpu_custom_call" | custom-call | tf_op jit(solution)/shard_map/pallas_call | solution.py:759
  157.9 4.8 collective-permute-done.1.other
  162.7 25.0 %all-gather.2.cloned.1.call-done.down_w = bf16[1024,2048]{1,0:T(8,128)(2,1)} async-done(((bf16[64,2048]{1,0:T(8,128)(2,1)}), bf16[1024,2048]{1,0:T(8,128)(2,1)}) %all-gather.2.cloned.1.call-update) | async-done | bytes 4194320 | tf_op jit(solution)/shard_map/all_gather | solution.py:1108
  187.7 20.8 %shard_map.251 = (f32[1200,1024]{1,0:T(8,128)}, bf16[1200,1024]{1,0:T(8,128)(2,1)}, bf16[1200,2048]{1,0:T(8,128)(2,1)}, bf16[1200,2048]{1,0:T(8,128)(2,1)}, bf16[1200,1024]{1,0:T(8,128)(2,1)}) custom-call(bf16[1200,1024]{1,0:T(8,128)(2,1)} %pad.36.stream.refs_0_, bf16[1200,1024]{1,0:T(8,128)(2,1)} %get-tuple-element.57.own, ...), custom_call_target="tpu_custom_call" | custom-call | tf_op jit(solution)/shard_map/pallas_call | solution.py:935
  209.1 7.0 %collective-permute-done.2 = bf16[1200,1024]{1,0:T(8,128)(2,1)S(1)} collective-permute-done((bf16[1200,1024]{1,0:T(8,128)(2,1)}, bf16[1200,1024]{1,0:T(8,128)(2,1)S(1)}, u32[]{:S(2)}, u32[]{:S(2)}) %collective-permute-start.2) | collective-permute-done | bytes 2457632 | tf_op jit(solution)/shard_map/ppermute | solution.py:1067
  216.1 4.6 add_convert_fusion.1
  221.4 3.4 collective-permute-start.3
  224.8 9.9 %collective-permute-done.3 = bf16[880,256]{1,0:T(8,128)(2,1)S(1)} collective-permute-done((bf16[880,256]{1,0:T(8,128)(2,1)S(1)}, bf16[880,256]{1,0:T(8,128)(2,1)S(1)}, u32[]{:S(2)}, u32[]{:S(2)}) %collective-permute-start.3) | collective-permute-done | bytes 450592 | tf_op jit(solution)/shard_map/ppermute | solution.py:1062
  237.0 2.5 reshape_squeeze.3
  239.6 2.5 pad.42.cotangent
  242.7 1.4 reshape.225.gains
  245.0 84.3 %shard_map.252 = (f32[6,208,512]{2,1,0:T(8,128)}, bf16[896,256]{1,0:T(8,128)(2,1)}, bf16[896,256]{1,0:T(8,128)(2,1)}, bf16[512,3072]{1,0:T(8,128)(2,1)}, bf16[512,3072]{1,0:T(8,128)(2,1)}, /*index=5*/f32[8,512]{1,0:T(8,128)}) custom-call(s32[1]{0:T(128)} %bitcast.15.flag, s32[1,896]{1,0:T(1,128)} %broadcast_in_dim.64.target_row, ...), custom_call_target="tpu_custom_call" | custom-call | tf_op jit(solution)/shard_map/pallas_call | solution.py:621
  329.4 1.1 slice.86
  331.0 1.4 collective-permute-done.6
  332.4 1.1 slice_add_fusion
  333.5 1.3 collective-permute-start.7
  334.8 13.3 %collective-permute-done.7 = bf16[880,256]{1,0:T(8,128)(2,1)S(1)} collective-permute-done((bf16[880,256]{1,0:T(8,128)(2,1)S(1)}, bf16[880,256]{1,0:T(8,128)(2,1)S(1)}, u32[]{:S(2)}, u32[]{:S(2)}) %collective-permute-start.7) | collective-permute-done | bytes 450592 | tf_op jit(solution)/shard_map/ppermute | solution.py:1062
  349.1 4.8 collective-permute-done.8.other.refs_4_
  353.9 30.7 %shard_map.253 = (bf16[1024,2048]{1,0:T(8,128)(2,1)}, bf16[1024,2048]{1,0:T(8,128)(2,1)}, bf16[1200,1024]{1,0:T(8,128)(2,1)}) custom-call(s32[1]{0:T(128)} %bitcast.14.counts, bf16[1200,1024]{1,0:T(8,128)(2,1)} %copy-done.7, bf16[1200,1024]{1,0:T(8,128)(2,1)} %collective-permute-done.8.other.refs_4_, bf16[1200,1024]{1,0:T(8,128)(2,1)} %get-tuple-element.66.second, ...), custom_call_target="tpu_custom_call" | custom-call | tf_op jit(solution)/shard_map/pallas_call | solution.py:993
  384.6 1.7 copy-done.12
  386.8 6.4 %collective-permute-done.9.refs_2_ = bf16[1200,1024]{1,0:T(8,128)(2,1)} collective-permute-done((bf16[1200,1024]{1,0:T(8,128)(2,1)S(1)}, bf16[1200,1024]{1,0:T(8,128)(2,1)}, u32[]{:S(2)}, u32[]{:S(2)}) %collective-permute-start.9) | collective-permute-done | bytes 2457632 | tf_op jit(solution)/shard_map/ppermute | solution.py:1067
  393.2 11.4 %shard_map.254 = (f32[1200,1024]{1,0:T(8,128)}, bf16[1200,1024]{1,0:T(8,128)(2,1)}, f32[8,1024]{1,0:T(8,128)}) custom-call(f32[1200,1024]{1,0:T(8,128)} %get-tuple-element.60.refs_0_, bf16[1200,1024]{1,0:T(8,128)(2,1)} %get-tuple-element.69.refs_1_, bf16[1200,1024]{1,0:T(8,128)(2,1)} %collective-permute-done.9.refs_2_, bf16[1200,1024]{1,0:T(8,128)(2,1)} %copy-done.7, ...), custom_call_target="tpu_custom_call" | custom-call | tf_op jit(solution)/shard_map/pallas_call | solution.py:1049
  404.6 48.9 %shard_map.255 = (bf16[1024,1536]{1,0:T(8,128)(2,1)}, bf16[1024,512]{1,0:T(8,128)(2,1)}, bf16[1200,1024]{1,0:T(8,128)(2,1)}) custom-call(s32[5,2]{1,0:T(8,128)} %copy.129.bounds, s32[1,1280]{1,0:T(1,128)} %broadcast_in_dim.61.slots_row, s32[1280,1]{1,0:T(8,128)} %broadcast_in_dim.71.slots_column, bf16[1200,1024]{1,0:T(8,128)(2,1)} %get-tuple-element.53.first, ...), custom_call_target="tpu_custom_call" | custom-call | tf_op jit(solution)/shard_map/pallas_call | solution.py:885
  455.4 1.9 slice.87
  457.4 2.2 reshape_reshape.6
  459.7 3.6 convolution_convert_fusion.1
  463.3 4.7 add_convert_fusion
  468.9 10.4 %shard_map.256 = (f32[1200,1024]{1,0:T(8,128)}, f32[8,1024]{1,0:T(8,128)}) custom-call(bf16[1200,1024]{1,0:T(8,128)(2,1)} %pad.36.stream.refs_0_, bf16[1200,1024]{1,0:T(8,128)(2,1)} %get-tuple-element.71.refs_1_, bf16[1200,1024]{1,0:T(8,128)(2,1)} %collective-permute-done.10.refs_2_, f32[1200,1024]{1,0:T(8,128)} %get-tuple-element.72.refs_3_, ...), custom_call_target="tpu_custom_call" | custom-call | tf_op jit(solution)/shard_map/pallas_call | solution.py:1049
  479.3 2.5 select_bitcast_fusion
  481.8 3.9 copy.142
  487.3 125.1 %shard_map.257 = (f32[64,4352]{1,0:T(8,128)}, f32[32,3072]{1,0:T(8,128)}, f32[8,128]{1,0:T(8,128)}, f32[8,128]{1,0:T(8,128)}) custom-call(bf16[2,2,2,2,64,1536]{5,4,3,2,1,0:T(8,128)(2,1)} %bitcast.107, bf16[2,2,2,2,64,512]{5,4,3,2,1,0:T(8,128)(2,1)} %bitcast.108, bf16[2,2,2,2,64,2048]{5,4,3,2,1,0:T(8,128)(2,1)} %bitcast.103, ...), custom_call_target="tpu_custom_call" | custom-call | tf_op jit(solution)/shard_map/pallas_call | solution.py:389
  613.4 1.3 slice_bitcast_fusion
  614.8 1.2 slice.94
  617.5 1.2 multiply_subtract_fusion.1
  618.7 1.2 copy.144
  619.8 1.1 copy.146
  621.0 1.9 multiply_subtract_fusion
  623.0 2.8 copy.143
  625.9 2.8 copy.145
  628.7 1.3 multiply_subtract_fusion.2
  630.0 1.2 multiply_subtract_fusion.3
  (135 shorter events, 19.0 us)
Async XLA Ops:
  7.2 2.5 copy-start.15
  7.2 2.5 copy-start.28
  7.2 2.5 copy-start.26
  7.2 180.5 %all-gather.2.cloned.1.call-start = ((), (), s32[]{:S(2)}) async-start(), calls=%async_computation.1 | async-start | bytes 4456448 | tf_op jit(solution)/shard_map/all_gather | solution.py:1108
  8.9 104.8 %copy-start.25 = (s32[1,2,1176]{2,1,0:T(2,128)S(1)}, s32[1,2,1176]{2,1,0:T(2,128)}, u32[]{:S(2)}) copy-start(s32[1,2,1176]{2,1,0:T(2,128)} %param.19) | copy-start | bytes 28228
  108.1 2.0 copy-start
  110.1 1.6 copy-start.1
  113.5 95.1 %copy-start.3 = (bf16[2,2,2,2,32,3072]{5,4,3,2,1,0:T(8,128)(2,1)}, bf16[2,2,2,2,32,3072]{5,4,3,2,1,0:T(8,128)(2,1)S(1)}, u32[]{:S(2)}) copy-start(bf16[2,2,2,2,32,3072]{5,4,3,2,1,0:T(8,128)(2,1)S(1)} %get-tuple-element.63) | copy-start | bytes 9437188
  113.5 373.8 %reduce-scatter.2.cloned.1.call-start = ((), (), s32[]{:S(2)}) async-start(), calls=%async_computation.2 | async-start | bytes 4456448 | tf_op jit(solution)/shard_map/reduce_scatter | solution.py:1117
  113.6 4.4 collective-permute-start
  157.7 5.0 collective-permute-start.1
  208.5 7.6 %collective-permute-start.2 = (bf16[1200,1024]{1,0:T(8,128)(2,1)}, bf16[1200,1024]{1,0:T(8,128)(2,1)S(1)}, u32[]{:S(2)}, u32[]{:S(2)}) collective-permute-start(bf16[1200,1024]{1,0:T(8,128)(2,1)} %get-tuple-element.61), channel_id=1, source_target_pairs={{0,1},{1,0},{2,3},{3,2},{4,5},{5,4},{6,7},{7,6},{8,9},{9,8},{10,11... | collective-permute-start | bytes 7372808 | tf_op jit(solution)/shard_map/ppermute | solution.py:1067
  208.6 36.4 %collective-permute-start.5 = (bf16[512,3072]{1,0:T(8,128)(2,1)S(1)}, bf16[512,3072]{1,0:T(8,128)(2,1)}, u32[]{:S(2)}, u32[]{:S(2)}) collective-permute-start(bf16[512,3072]{1,0:T(8,128)(2,1)S(1)} %bitcast.94), channel_id=1, source_target_pairs={{0,1},{1,0},{2,3},{3,2},{4,5},{5,4},{6,7},{7,6},{8,9},{9,8},{10,11... | collective-permute-start | bytes 9437192 | tf_op jit(solution)/shard_map/ppermute | solution.py:1067
  216.1 4.6 copy-start.5
  220.7 14.7 %copy-start.11 = (bf16[1200,1024]{1,0:T(8,128)(2,1)}, bf16[1200,1024]{1,0:T(8,128)(2,1)S(1)}, u32[]{:S(2)}) copy-start(bf16[1200,1024]{1,0:T(8,128)(2,1)S(1)} %add_convert_fusion.1) | copy-start | bytes 7372804
  220.7 14.7 %copy-start.35 = (pred[896]{0:T(1024)(128)(4,1)S(1)}, pred[896]{0:T(1024)(128)(4,1)}, u32[]{:S(2)}) copy-start(pred[896]{0:T(1024)(128)(4,1)} %constant.39.clone.1) | copy-start | bytes 2692
  221.4 13.2 %collective-permute-start.3 = (bf16[880,256]{1,0:T(8,128)(2,1)S(1)}, bf16[880,256]{1,0:T(8,128)(2,1)S(1)}, u32[]{:S(2)}, u32[]{:S(2)}) collective-permute-start(bf16[880,256]{1,0:T(8,128)(2,1)S(1)} %fusion.9), channel_id=1, source_target_pairs={{0,16},{1,17},{2,18},{3,19},{4,20},{5,21},{6,22},{7,23},{8,24},{9,... | collective-permute-start | bytes 1351688 | tf_op jit(solution)/shard_map/ppermute | solution.py:1062
  235.4 9.6 %collective-permute-start.4 = (bf16[896,256]{1,0:T(8,128)(2,1)}, bf16[896,256]{1,0:T(8,128)(2,1)}, u32[]{:S(2)}, u32[]{:S(2)}) collective-permute-start(bf16[896,256]{1,0:T(8,128)(2,1)} %pad.40.visible_own), channel_id=1, source_target_pairs={{0,1},{1,0},{2,3},{3,2},{4,5},{5,4},{6,7},{7,6},{8,9},{9,8},{10,11... | collective-permute-start | bytes 1376264 | tf_op jit(solution)/shard_map/ppermute | solution.py:1067
  237.0 7.1 %copy-start.19 = (f32[196,512]{1,0:T(8,128)S(1)}, f32[196,512]{1,0:T(8,128)}, u32[]{:S(2)}) copy-start(f32[196,512]{1,0:T(8,128)} %param.33) | copy-start | bytes 1204228
  239.6 2.5 copy-start.23
  329.3 18.8 %copy-start.6 = (bf16[2,2,2,2,64,256]{5,4,3,2,1,0:T(8,128)(2,1)S(1)}, bf16[2,2,2,2,64,256]{5,4,3,2,1,0:T(8,128)(2,1)}, u32[]{:S(2)}) copy-start(bf16[2,2,2,2,64,256]{5,4,3,2,1,0:T(8,128)(2,1)} %copy-done.4) | copy-start | bytes 1572868
  330.5 2.0 collective-permute-start.6
  333.5 14.6 %collective-permute-start.7 = (bf16[880,256]{1,0:T(8,128)(2,1)S(1)}, bf16[880,256]{1,0:T(8,128)(2,1)S(1)}, u32[]{:S(2)}, u32[]{:S(2)}) collective-permute-start(bf16[880,256]{1,0:T(8,128)(2,1)S(1)} %slice_add_fusion), channel_id=1, source_target_pairs={{16,0},{17,1},{18,2},{19,3},{20,4},{21,5},{22,6},{23,7},{24,8},{25... | collective-permute-start | bytes 1351688 | tf_op jit(solution)/shard_map/ppermute | solution.py:1062
  349.0 4.9 copy-start.7
  349.0 4.9 collective-permute-start.8
  384.6 1.7 copy-start.12
  386.3 6.9 %collective-permute-start.9 = (bf16[1200,1024]{1,0:T(8,128)(2,1)S(1)}, bf16[1200,1024]{1,0:T(8,128)(2,1)}, u32[]{:S(2)}, u32[]{:S(2)}) collective-permute-start(bf16[1200,1024]{1,0:T(8,128)(2,1)S(1)} %copy-done.12), channel_id=1, source_target_pairs={{0,1},{1,0},{2,3},{3,2},{4,5},{5,4},{6,7},{7,6},{8,9},{9,8},{10,11... | collective-permute-start | bytes 7372808 | tf_op jit(solution)/shard_map/ppermute | solution.py:1067
  386.4 76.9 %collective-permute-start.11 = (bf16[512,3072]{1,0:T(8,128)(2,1)}, bf16[512,3072]{1,0:T(8,128)(2,1)}, u32[]{:S(2)}, u32[]{:S(2)}) collective-permute-start(bf16[512,3072]{1,0:T(8,128)(2,1)} %get-tuple-element.79), channel_id=1, source_target_pairs={{0,1},{1,0},{2,3},{3,2},{4,5},{5,4},{6,7},{7,6},{8,9},{9,8},{10,11... | collective-permute-start | bytes 9437192 | tf_op jit(solution)/shard_map/ppermute | solution.py:1067
  404.6 49.1 %copy-start.24 = (f32[8,512]{1,0:T(8,128)S(1)}, f32[8,512]{1,0:T(8,128)}, u32[]{:S(2)}) copy-start(f32[8,512]{1,0:T(8,128)} %get-tuple-element.82) | copy-start | bytes 49156
  404.6 49.5 %copy-start.34 = (f32[2]{0:T(128)S(1)}, f32[2]{0:T(128)}, u32[]{:S(2)}) copy-start(f32[2]{0:T(128)} %param.34) | copy-start | bytes 28
  453.6 15.3 %collective-permute-start.10 = (bf16[1200,1024]{1,0:T(8,128)(2,1)}, bf16[1200,1024]{1,0:T(8,128)(2,1)}, u32[]{:S(2)}, u32[]{:S(2)}) collective-permute-start(bf16[1200,1024]{1,0:T(8,128)(2,1)} %get-tuple-element.71.refs_1_), channel_id=1, source_target_pairs={{0,1},{1,0},{2,3},{3,2},{4,5},{5,4},{6,7},{7,6},{8,9},{9,8},{10,11... | collective-permute-start | bytes 7372808 | tf_op jit(solution)/shard_map/ppermute | solution.py:1067
  453.7 5.9 collective-permute-start.12
  459.7 3.6 copy-start.10
  468.9 10.4 %copy-start.8 = (f32[588,1024]{1,0:T(8,128)S(1)}, f32[588,1024]{1,0:T(8,128)}, u32[]{:S(2)}) copy-start(f32[588,1024]{1,0:T(8,128)} %reshape_reshape.6) | copy-start | bytes 7225348
  612.4 5.0 copy-start.17
  612.4 5.0 copy-start.16
  612.4 5.0 copy-start.20
  612.4 5.0 copy-start.21
  613.4 7.6 %copy-start.18 = (bf16[64,2048]{1,0:T(8,128)(2,1)S(1)}, bf16[64,2048]{1,0:T(8,128)(2,1)}, u32[]{:S(2)}) copy-start(bf16[64,2048]{1,0:T(8,128)(2,1)} %reduce-scatter.2.cloned.1.call-done.refs_6_) | copy-start | bytes 786436
  617.4 3.6 copy-start.9
  617.4 3.6 copy-start.13
  617.4 3.6 copy-start.14
  625.8 2.9 copy-start.27
  625.8 2.9 copy-start.30
  625.8 2.9 copy-start.31
  625.8 4.2 copy-start.29
  625.8 4.2 copy-start.32
  625.8 4.2 copy-start.33
  (3 other events, 2.4 us)
Sparse Core Ops, SparseCore 0:
  113.6 74.0 all-gather.1
  384.7 92.7 reduce-scatter.1

commit v4 on v3

--- a/solution.py
+++ b/solution.py
@@ -21,6 +21,10 @@
 ROW_BLOCK = 240
 MOST_VISIBLE = 73
 GATHER_ORDERS = ("hlxy", "hlyx", "hlxy", "hlyx", "yxhl")
+DEC_GATHER_ORDERS = ("xhly", "xyhl")
+DEC_SCATTER_ORDERS = ("ylhx", "ylhx")
+GATHER_AHEAD, GATHER_LAG = 4, (1, 3)
+SCATTER_AHEAD, SCATTER_LAG = 4, (2, 2, 2)
 SCATTER_ORDERS = ("xylh", "yxlh", "xylh", "yxlh", "lhxy")
 
 MESH_ID = pl.DeviceIdType.MESH
@@ -390,7 +394,7 @@
 
 
 HEADS = 16
-TOGETHER = 4
+TOGETHER = 8
 NORM_EPS = 1e-06
 MASKED = -1e30
 LOW = jnp.bfloat16
@@ -449,15 +453,20 @@
     mixture,
     hidden,
     slope,
-    grad_rows,
+    grad_mixture,
+    stream,
+    first,
+    after,
+    grad_low,
+    grad_first,
     grad_visible,
     grad_qkv,
     grad_out,
     grad_up,
     grad_down,
 ):
-    image = pl.program_id(0)
-    rows, width = decoded.shape[1], decoded.shape[2]
+    step = pl.program_id(0)
+    images, rows, width = decoded.shape
     head = width // HEADS
     units = hidden.shape[1]
     part, half = width // 2, units // 2
@@ -466,7 +475,7 @@
     packs = (pack_own, pack_other)
     halves = ((slice(0, half), pack_own), (slice(half, units), pack_other))
 
-    @pl.when(image == 0)
+    @pl.when(step == 0)
     def _():
         for ref in (grad_visible, grad_qkv, grad_out, grad_up, grad_down, grad_gains):
             ref[...] = jnp.zeros_like(ref)
@@ -480,43 +489,47 @@
                     out_t[k * part : (k + 1) * part, :] = piece
 
     packed = target_row.shape[1]
-    cell = lax.broadcasted_iota(jnp.int32, (rows, packed), 0)
-    wanted = jnp.where(cell < length, cell + image * length, -7)
-    chosen = (target_row[...] == wanted).astype(WIDE)
-    seen = jnp.max(chosen, axis=1, keepdims=True)
-    chosen = chosen.astype(LOW)
-    placed_own, placed_other = mm(chosen, visible_own[...]), mm(chosen, visible_other[...])
     left = flag[0] > 0
-    placed = jnp.concatenate(
-        [
-            jnp.where(left, placed_own, placed_other),
-            jnp.where(left, placed_other, placed_own),
-        ],
-        axis=1,
-    )
-    stream = jnp.where(seen > 0.0, placed, mask[...]) + position[...]
-
-    unit_one, scale_one = centre(stream)
-    first = (unit_one * gains[0:1] + gains[1:2]).astype(LOW)
-    qkv_rows[...] = mm(qkv_t[...], first, 1, 1).astype(LOW)
-
+    spans = [slice(k * rows, (k + 1) * rows) for k in range(images)]
+    for k, span in enumerate(spans):
+        number = step * images + k
+        cell = lax.broadcasted_iota(jnp.int32, (rows, packed), 0)
+        wanted = jnp.where(cell < length, cell + number * length, -7)
+        chosen = (target_row[...] == wanted).astype(WIDE)
+        seen = jnp.max(chosen, axis=1, keepdims=True)
+        chosen = chosen.astype(LOW)
+        placed_own, placed_other = mm(chosen, visible_own[...]), mm(chosen, visible_other[...])
+        placed = jnp.concatenate(
+            [
+                jnp.where(left, placed_own, placed_other),
+                jnp.where(left, placed_other, placed_own),
+            ],
+            axis=1,
+        )
+        stream[span, :] = jnp.where(seen > 0.0, placed, mask[...]) + position[...]
+
+    unit_one, scale_one = centre(stream[...])
+    first[...] = (unit_one * gains[0:1] + gains[1:2]).astype(LOW)
     key_index = lax.broadcasted_iota(jnp.int32, (rows, rows), 0)
 
     def lines(which, h):
         return slice(which * width + h * head, which * width + (h + 1) * head)
 
-    for begin in range(0, HEADS, TOGETHER):
-        group = range(begin, begin + TOGETHER)
-        scores = [mm(qkv_rows[lines(1, h), :], qkv_rows[lines(0, h), :], 0, 0) * scaling for h in group]
-        scores = [jnp.where(key_index < length, s, MASKED) for s in scores]
-        weights = [jnp.exp(s - jnp.max(s, axis=0, keepdims=True)) for s in scores]
-        group_shares = [w * (1.0 / jnp.sum(w, axis=0, keepdims=True)) for w in weights]
-        for h, share in zip(group, group_shares):
-            shares[h] = share
-            mixture[lines(0, h), :] = mm(qkv_rows[lines(2, h), :], share.astype(LOW)).astype(LOW)
-    mixed = mixture[...]
-    after = stream + mm(mixed, out_t[...], 0, 0)
-    unit_two, scale_two = centre(after)
+    for k, span in enumerate(spans):
+        qkv, mixed = qkv_rows.at[k], mixture.at[k]
+        qkv[...] = mm(qkv_t[...], first[span, :], 1, 1).astype(LOW)
+        for begin in range(0, HEADS, TOGETHER):
+            group = range(begin, begin + TOGETHER)
+            scores = [mm(qkv[lines(1, h), :], qkv[lines(0, h), :], 0, 0) * scaling for h in group]
+            scores = [jnp.where(key_index < length, s, MASKED) for s in scores]
+            weights = [jnp.exp(s - jnp.max(s, axis=0, keepdims=True)) for s in scores]
+            group_shares = [w * (1.0 / jnp.sum(w, axis=0, keepdims=True)) for w in weights]
+            for h, share in zip(group, group_shares):
+                shares[k, h] = share
+                mixed[lines(0, h), :] = mm(qkv[lines(2, h), :], share.astype(LOW)).astype(LOW)
+        after[span, :] = stream[span, :] + mm(mixed[...], out_t[...], 0, 0)
+
+    unit_two, scale_two = centre(after[...])
     second = (unit_two * gains[2:3] + gains[3:4]).astype(LOW)
     piece = 256
     for c in range(0, units, piece):
@@ -526,59 +539,67 @@
         hidden[:, c : c + piece] = h.astype(LOW)
         slope[:, c : c + piece] = g
     fed = [mm(hidden[:, cut], pack[:, down_at : down_at + half], 1, 1) for cut, pack in halves]
-    decoded[0] = after + (fed[0] + fed[1])
-
-    grad_low = cotangent[0]
-    grad_result = grad_low.astype(WIDE)
-    turned = jnp.transpose(grad_low)
+    result = after[...] + (fed[0] + fed[1])
+    for k, span in enumerate(spans):
+        decoded[k] = result[span]
+
+    for k, span in enumerate(spans):
+        grad_low[span, :] = cotangent[k]
+    turned = jnp.transpose(grad_low[...])
     second_turned = jnp.transpose(second)
     for c in range(0, units, piece):
         cut = slice(c, c + piece)
         grad_down[:, cut] += mm(turned, hidden[:, cut])
         pack, at = packs[c // half], down_at + c % half
-        grad_z = (mm(grad_low, pack[:, at : at + piece]) * slope[:, cut]).astype(LOW)
+        grad_z = (mm(grad_low[...], pack[:, at : at + piece]) * slope[:, cut]).astype(LOW)
         hidden[:, cut] = grad_z
         grad_up[:, cut] += mm(second_turned, grad_z)
     pulled = [mm(hidden[:, cut], pack[:, up_at : up_at + half], 1, 1) for cut, pack in halves]
     grad_second = pulled[0] + pulled[1]
-    grad_after = grad_result + centre_back(unit_two, scale_two, gains[2:3], grad_second)
     grad_gains[2:3] += jnp.sum(grad_second * unit_two, axis=0, keepdims=True)
     grad_gains[3:4] += jnp.sum(grad_second, axis=0, keepdims=True)
-
-    after_low = grad_after.astype(LOW)
-    grad_out[...] += mm(mixed, after_low)
-    grad_rows[...] = mm(out_t[...], after_low, 1, 1).astype(LOW)
-
-    for begin in range(0, HEADS, TOGETHER):
-        group = range(begin, begin + TOGETHER)
-        queries = [qkv_rows[lines(0, h), :] for h in group]
-        keys = [qkv_rows[lines(1, h), :] for h in group]
-        values = [qkv_rows[lines(2, h), :] for h in group]
-        grads_in = [grad_rows[lines(0, h), :] for h in group]
-        grad_shares = [mm(v, g, 0, 0) for v, g in zip(values, grads_in)]
-        grad_values = [mm(g, shares[h].astype(LOW), 1, 1) for g, h in zip(grads_in, group)]
-        grad_scores = []
-        for h, g in zip(group, grad_shares):
-            share = shares[h]
-            inner = jnp.sum(share * g, axis=0, keepdims=True)
-            grad_scores.append((share * (g - inner)).astype(LOW))
-        for k, h in enumerate(group):
-            qkv_rows[lines(0, h), :] = (mm(keys[k], grad_scores[k]) * scaling).astype(LOW)
-            qkv_rows[lines(1, h), :] = (mm(queries[k], grad_scores[k], 1, 1) * scaling).astype(LOW)
-            qkv_rows[lines(2, h), :] = grad_values[k].astype(LOW)
-    grads = qkv_rows[...]
-    grad_qkv[...] += mm(grads, first)
-    grad_first = mm(grads, qkv_t[...], 0, 0)
-    grad_stream = grad_after + centre_back(unit_one, scale_one, gains[0:1], grad_first)
-    grad_gains[0:1] += jnp.sum(grad_first * unit_one, axis=0, keepdims=True)
-    grad_gains[1:2] += jnp.sum(grad_first, axis=0, keepdims=True)
-
-    cell_lane = lax.broadcasted_iota(jnp.int32, (packed, rows), 1)
-    wanted_lane = jnp.where(cell_lane < length, cell_lane + image * length, -7)
-    chosen_back = (target_column[...] == wanted_lane).astype(WIDE).astype(LOW)
-    grad_visible[...] += mm(chosen_back, grad_stream.astype(LOW))
-
-    @pl.when(image == pl.num_programs(0) - 1)
+    after[...] = grad_low[...].astype(WIDE) + centre_back(
+        unit_two, scale_two, gains[2:3], grad_second
+    )
+
+    for k, span in enumerate(spans):
+        qkv, mixed, grad_rows = qkv_rows.at[k], mixture.at[k], grad_mixture.at[k]
+        after_low = after[span, :].astype(LOW)
+        grad_out[...] += mm(mixed[...], after_low)
+        grad_rows[...] = mm(out_t[...], after_low, 1, 1).astype(LOW)
+        for begin in range(0, HEADS, TOGETHER):
+            group = range(begin, begin + TOGETHER)
+            queries = [qkv[lines(0, h), :] for h in group]
+            keys = [qkv[lines(1, h), :] for h in group]
+            values = [qkv[lines(2, h), :] for h in group]
+            grads_in = [grad_rows[lines(0, h), :] for h in group]
+            grad_shares = [mm(v, g, 0, 0) for v, g in zip(values, grads_in)]
+            grad_values = [mm(g, shares[k, h].astype(LOW), 1, 1) for g, h in zip(grads_in, group)]
+            grad_scores = []
+            for h, g in zip(group, grad_shares):
+                share = shares[k, h]
+                inner = jnp.sum(share * g, axis=0, keepdims=True)
+                grad_scores.append((share * (g - inner)).astype(LOW))
+            for n, h in enumerate(group):
+                qkv[lines(0, h), :] = (mm(keys[n], grad_scores[n]) * scaling).astype(LOW)
+                qkv[lines(1, h), :] = (mm(queries[n], grad_scores[n], 1, 1) * scaling).astype(LOW)
+                qkv[lines(2, h), :] = grad_values[n].astype(LOW)
+        grad_qkv[...] += mm(qkv[...], first[span, :])
+        grad_first[span, :] = mm(qkv[...], qkv_t[...], 0, 0)
+
+    unit_one, scale_one = centre(stream[...])
+    pulled = grad_first[...]
+    grad_stream = after[...] + centre_back(unit_one, scale_one, gains[0:1], pulled)
+    grad_gains[0:1] += jnp.sum(pulled * unit_one, axis=0, keepdims=True)
+    grad_gains[1:2] += jnp.sum(pulled, axis=0, keepdims=True)
+
+    for k, span in enumerate(spans):
+        cell_lane = lax.broadcasted_iota(jnp.int32, (packed, rows), 1)
+        wanted_lane = jnp.where(cell_lane < length, cell_lane + (step * images + k) * length, -7)
+        chosen_back = (target_column[...] == wanted_lane).astype(WIDE).astype(LOW)
+        grad_visible[...] += mm(chosen_back, grad_stream[span].astype(LOW))
+
+    @pl.when(step == pl.num_programs(0) - 1)
     def _():
         gathered = grad_visible[...].astype(LOW)
         one, two = gathered[:, :part], gathered[:, part:]
@@ -610,7 +631,9 @@
     def fixed(shape):
         return pl.BlockSpec(shape, lambda i: (0,) * len(shape), pipeline_mode=pl.Buffered(1))
 
-    per_image = pl.BlockSpec((1, rows, width), lambda i: (i, 0, 0))
+    at_once = 2 if images % 2 == 0 else 1
+    per_image = pl.BlockSpec((at_once, rows, width), lambda i: (i, 0, 0))
+    tall = at_once * rows
     grads = [
         ((packed, width // 2), LOW),
         ((packed, width // 2), LOW),
@@ -620,7 +643,7 @@
     ]
     decoded, keep, send, grad_own, grad_other, grad_gains = pl.pallas_call(
         functools.partial(decoder_kernel, length),
-        grid=(images,),
+        grid=(images // at_once,),
         out_shape=[jax.ShapeDtypeStruct((images, rows, width), WIDE)]
         + [jax.ShapeDtypeStruct(s, d) for s, d in grads],
         in_specs=[
@@ -640,12 +663,17 @@
         scratch_shapes=[
             pltpu.VMEM((3 * width, width), LOW),
             pltpu.VMEM((width, width), LOW),
-            pltpu.VMEM((3 * width, rows), LOW),
-            pltpu.VMEM((HEADS, rows, rows), WIDE),
-            pltpu.VMEM((width, rows), LOW),
-            pltpu.VMEM((rows, units), LOW),
-            pltpu.VMEM((rows, units), WIDE),
-            pltpu.VMEM((width, rows), LOW),
+            pltpu.VMEM((at_once, 3 * width, rows), LOW),
+            pltpu.VMEM((at_once, HEADS, rows, rows), WIDE),
+            pltpu.VMEM((at_once, width, rows), LOW),
+            pltpu.VMEM((tall, units), LOW),
+            pltpu.VMEM((tall, units), WIDE),
+            pltpu.VMEM((at_once, width, rows), LOW),
+            pltpu.VMEM((tall, width), WIDE),
+            pltpu.VMEM((tall, width), LOW),
+            pltpu.VMEM((tall, width), WIDE),
+            pltpu.VMEM((tall, width), LOW),
+            pltpu.VMEM((tall, width), WIDE),
             pltpu.VMEM((packed, width), WIDE),
             pltpu.VMEM((3 * width, width), WIDE),
             pltpu.VMEM((width, width), WIDE),
@@ -1071,13 +1099,15 @@
     return lax.axis_size("section") == 2 and lax.axis_size("dp") == 8
 
 
-def plan(widths, pieces, dec_width, dec_pieces, orders):
+def plan(widths, pieces, dec_width, orders, dec_orders):
     enc = chunk_list(widths, pieces, 0, orders)
     dec = [
         (len(widths), b, c, w, o, k)
-        for _, b, c, w, o, k in chunk_list((dec_width,), (dec_pieces,), 1, orders)
+        for _, b, c, w, o, k in chunk_list((dec_width,), (4,), 1, dec_orders)
     ]
-    return enc[:8] + dec + enc[8:]
+    for k, chunk in enumerate(dec):
+        enc.insert(3 * k + 2, chunk)
+    return enc
 
 
 def gather_all(low_enc, low_dec, norms, widths):
@@ -1095,13 +1125,13 @@
     columns = [sum(widths[:k]) for k in range(count + 1)]
     ahead = [low_enc[:, : columns[3]], low_enc[:, columns[4] :]]
     near = (*widths[:3], widths[4])
-    chunks = plan(near, (4, 1, 4, 2), low_dec.shape[1], 4, GATHER_ORDERS)
+    chunks = plan(near, (4, 1, 4, 2), low_dec.shape[1], GATHER_ORDERS, DEC_GATHER_ORDERS)
     outputs = [(low_enc.shape[0], w, LOW) for w in near]
     outputs += [(low_dec.shape[0], low_dec.shape[1], LOW), (8, 128, WIDE)]
     described = [(k // 4, k, c, b, w, o, own) for k, b, c, w, o, own in chunks]
     described.append((2, 5, 0, 0, 128, "hlyx", BOTH))
     shards = [jnp.concatenate(ahead, axis=1), low_dec, norms]
-    results = gather_weights(shards, outputs, described, 1, 4, (1, 3))
+    results = gather_weights(shards, outputs, described, 1, GATHER_AHEAD, GATHER_LAG)
     low_down, norm_rows = lax.optimization_barrier(
         (low_enc[:, columns[3] : columns[4]], results[5])
     )
@@ -1122,21 +1152,20 @@
         norms = scattered(norms)
         local = sum(jnp.sum(v * v) for v in (*parts, dec))
         local = local + jnp.sum(norms * norms) / lax.axis_size("mp")
-        return jnp.concatenate(parts, axis=1), dec, norms, lax.psum(local, (*both, "mp"))
+        total = jnp.full((8, 128), lax.psum(local, (*both, "mp")))
+        return jnp.concatenate([*parts[:3], parts[4]], axis=1), parts[3], dec, norms, total
     down = scattered(enc_parts[3])
     near = (*enc_parts[:3], enc_parts[4])
     near_widths = (*widths[:3], widths[4])
-    chunks = plan(near_widths, (4, 1, 4, 2), dec.shape[1], 4, SCATTER_ORDERS)
+    chunks = plan(near_widths, (4, 1, 4, 2), dec.shape[1], SCATTER_ORDERS, DEC_SCATTER_ORDERS)
     described = [(k, k // 4, b, c, w, o, own) for k, b, c, w, o, own in chunks]
     described.append((5, 2, 0, 0, 128, "xylh", BOTH))
     rows = near[0].shape[0] // 16
     outputs = [(rows, sum(near_widths)), (dec.shape[0] // 16, dec.shape[1]), (8, 128)]
     enc, dec, norms, total = scatter_grads(
-        [*near, dec, norms], down, outputs, described, 2, 4, (2, 2, 2)
-    )
-    cut = sum(widths[:3])
-    enc = jnp.concatenate([enc[:, :cut], down.astype(WIDE), enc[:, cut:]], axis=1)
-    return enc, dec, norms, total[0, 0]
+        [*near, dec, norms], down, outputs, described, 2, SCATTER_AHEAD, SCATTER_LAG
+    )
+    return enc, down, dec, norms, total
 
 
 def pack_norms(enc_rows, dec_rows, blocks):
@@ -1164,22 +1193,58 @@
     return jnp.stack([first, last], axis=1)
 
 
-def update(
-    weight,
-    first_moment,
-    second_moment,
-    gradient,
-    factor,
-    step_rate,
-    fix_first,
-    fix_second,
-    decay_rate,
-):
-    clipped = gradient * factor
+def renewed(weight, first_moment, second_moment, clipped, rate, fix_first, fix_second, decay):
     new_first = BETA_FIRST * first_moment + (1.0 - BETA_FIRST) * clipped
     new_second = BETA_SECOND * second_moment + (1.0 - BETA_SECOND) * clipped * clipped
     stepped = new_first / fix_first / (jnp.sqrt(new_second / fix_second) + ADAM_EPS)
-    return weight - step_rate * (stepped + decay_rate * weight)
+    return weight - rate * (stepped + decay * weight)
+
+
+def renew_kernel(order, scalars, total, near, down, dec, norms, *refs):
+    enc_state, dec_state, enc_norm_state, dec_norm_state = (refs[k : k + 3] for k in (0, 3, 6, 9))
+    new_enc, new_dec, new_enc_norm, new_dec_norm, enc_clip, dec_clip, enc_norm_clip, dec_norm_clip = refs[12:]
+    factor = jnp.minimum(1.0, math.sqrt(PARAMS) / (jnp.sqrt(total[0:1, :]) + 1e-06))
+    fixes = scalars[2], scalars[3]
+
+    def work(blocks, state, new, clip):
+        count = len(blocks)
+        for k, (ref, at) in enumerate(blocks):
+            rows = pl.ds(k, ref.shape[0], stride=count)
+            clipped = ref[:, at : at + 128].astype(WIDE) * factor
+            values = [s[rows, :] for s in state]
+            clip[rows, :] = clipped
+            new[rows, :] = renewed(*values, clipped, scalars[0], *fixes, WEIGHT_DECAY)
+
+    work([((near, down)[which], at) for which, at in order], enc_state, new_enc, enc_clip)
+    work([(dec, at) for at in range(0, dec.shape[1], 128)], dec_state, new_dec, dec_clip)
+    column = 0
+    for state, new, clip in (
+        (enc_norm_state, new_enc_norm, enc_norm_clip),
+        (dec_norm_state, new_dec_norm, dec_norm_clip),
+    ):
+        rows, width = new.shape
+        clipped = norms[0:rows, column : column + width] * factor[:, :width]
+        column += width
+        clip[...] = clipped
+        new[...] = renewed(*[s[...] for s in state], clipped, scalars[1], *fixes, 0.0)
+
+
+def renew_all(scalars, total, near, down, down_at, dec, norms, enc, decoder, enc_norm, dec_norm):
+    order = [(0, at) for at in range(0, near.shape[1], 128)]
+    order[down_at // 128 : down_at // 128] = [(1, at) for at in range(0, down.shape[1], 128)]
+    flat = [[v.reshape(-1, 128) for v in group] for group in (enc, decoder)]
+    groups = [*flat, enc_norm, dec_norm]
+    shapes = [jax.ShapeDtypeStruct(group[0].shape, WIDE) for group in groups] * 2
+    results = pl.pallas_call(
+        functools.partial(renew_kernel, order),
+        in_specs=[pl.BlockSpec(memory_space=pltpu.SMEM)]
+        + [pl.BlockSpec(memory_space=pltpu.VMEM)] * 17,
+        out_specs=[pl.BlockSpec(memory_space=pltpu.VMEM)] * 8,
+        out_shape=shapes,
+        compiler_params=pltpu.CompilerParams(vmem_limit_bytes=40 * 2**20),
+    )(scalars, total, near, down, dec, norms, *[v for group in groups for v in group])
+    given = (enc, decoder, enc_norm, dec_norm) * 2
+    return [r.reshape(group[0].shape) for r, group in zip(results, given)]
 
 
 def per_device(
@@ -1310,64 +1375,37 @@
         jnp.where(decoder_side, dec_gain_grad, 0.0),
         norm_rows.shape[0] // 8,
     )
-    enc_shard, dec_shard, norm_shard, square_total = scatter_all(
+    near_shard, down_shard, dec_shard, norm_shard, square_total = scatter_all(
         (grad_qkv_w, grad_out_w, grad_up_w, grad_down_w, grad_projection),
         dec_grad,
         norm_grads,
         encoder_side,
     )
-    enc_gain_shard, dec_gain_shard = unpack_norms(
-        norm_shard, 1, enc_norms.shape[1], dec_norms.shape[1]
-    )
-    grad_norm = jnp.sqrt(square_total)
-    factor = jnp.minimum(1.0, math.sqrt(PARAMS) / (grad_norm + 1e-06))
     step_value = step_count[0].astype(jnp.float32)
-    fix_first = 1.0 - jnp.power(BETA_FIRST, step_value)
-    fix_second = 1.0 - jnp.power(BETA_SECOND, step_value)
-
-    def renew(weight, first_moment, second_moment, gradient, rate, decay):
-        flat = (-1, 128) if gradient.size % 1024 == 0 else gradient.shape
-        gradient = gradient.reshape(flat)
-        renewed = update(
-            weight.reshape(flat),
-            first_moment.reshape(flat),
-            second_moment.reshape(flat),
-            gradient,
-            factor,
-            rate,
-            fix_first,
-            fix_second,
-            decay,
-        )
-        return renewed.reshape(weight.shape), (gradient * factor).reshape(weight.shape)
-
-    step_rate, norm_rate = learning_rate[0], learning_rate[1]
-    new_enc, enc_clipped = renew(
-        enc_weights, enc_first, enc_second, enc_shard, step_rate, WEIGHT_DECAY
-    )
-    new_dec, dec_clipped = renew(
-        dec_weights, dec_first, dec_second, dec_shard, step_rate, WEIGHT_DECAY
-    )
-    new_enc_norms, enc_norm_clipped = renew(
-        enc_norms, enc_norm_first, enc_norm_second, enc_gain_shard, norm_rate, 0.0
-    )
-    new_dec_norms, dec_norm_clipped = renew(
-        dec_norms, dec_norm_first, dec_norm_second, dec_gain_shard, norm_rate, 0.0
+    scalars = jnp.stack(
+        [
+            learning_rate[0],
+            learning_rate[1],
+            1.0 - jnp.power(BETA_FIRST, step_value),
+            1.0 - jnp.power(BETA_SECOND, step_value),
+        ]
+    )
+    results = renew_all(
+        scalars,
+        square_total,
+        near_shard,
+        down_shard,
+        sum(widths[:3]),
+        dec_shard,
+        norm_shard,
+        (enc_weights, enc_first, enc_second),
+        (dec_weights, dec_first, dec_second),
+        (enc_norms, enc_norm_first, enc_norm_second),
+        (dec_norms, dec_norm_first, dec_norm_second),
     )
     own_grad = lax.dynamic_slice_in_dim(grad_stream, mp_rank * local_rows, local_rows, axis=0)
     act_out = jnp.where(encoder_side, own_grad, decoded.reshape(local_rows, width))[None]
-    return (
-        act_out,
-        new_enc,
-        new_dec,
-        new_enc_norms,
-        new_dec_norms,
-        enc_clipped,
-        dec_clipped,
-        enc_norm_clipped,
-        dec_norm_clipped,
-        grad_norm.reshape(1),
-    )
+    return (act_out, *results, jnp.sqrt(square_total[0, 0]).reshape(1))
 
 
 def solution(mesh):

time: 650 us -> 614 us (0.945)
  Pallas kernels: 465 us -> 449 us
  waiting for transfers between devices: 72.6 us -> 62.6 us
    pallas_call x1, Pallas kernels: 125 us -> 106 us  [scatter_grads(): return call(*views, summed)]
    all_gather x1, waiting for transfers between devices: 25 us -> 15.1 us  [gather_all(): down = lax.all_gather(low_down, ('section', 'dp'), axis=0, tiled=True)]
    pallas_call x1 -> x2, Pallas kernels: 84.3 us -> 75.6 us  [the longest x1 71.4 us: decoder_step(): pl.pallas_call(functools.partial(decoder_kernel, length), grid=(images //...]
    pallas_call x1, Pallas kernels: 48.9 us -> 56.6 us  [encoder_attend_back(): pl.pallas_call(functools.partial(attend_back_kernel, head), in_specs=[pl....]
    unnamed x80 -> x76, local copies, waits for them, and re-layouts: 21.3 us -> 18.9 us
  transfers between devices with their start and end apart: 15 -> 15, of which waited for: 8 -> 8; matrix products, arithmetic and copies ran while one was open for 7% -> 8% of each run, Pallas kernels for 17% -> 20%
where the time goes in v4:
time: 614 us; the launch traced here: 608 us
  Pallas kernels  449 us (73%)
  waiting for transfers between devices  62.6 us (10%)
  local copies, waits for them, and re-layouts  46.9 us (8%)
  other arithmetic  19.4 us (3%)
  between operations  17.4 us (3%)
  starting transfers between devices  7.56 us (1%)
    pallas_call x1, Pallas kernels, scatter_grads(): return call(*views, summed)  106 us
    pallas_call x1, Pallas kernels, gather_weights(): results = call(*shards)  97 us
    pallas_call x1, Pallas kernels, decoder_step(): pl.pallas_call(functools.partial(decoder_kernel, length), grid=(images //...  71.4 us
    pallas_call x1, Pallas kernels, encoder_attend_back(): pl.pallas_call(functools.partial(attend_back_kernel, head), in_specs=[pl....  56.6 us
    pallas_call x1, Pallas kernels, encoder_attend(): pl.pallas_call(functools.partial(attend_kernel, head), in_specs=[pl.Block...  40.6 us
    pallas_call x1, Pallas kernels, encoder_feed_back(): pl.pallas_call(feed_back_kernel, grid=(units // piece,), in_specs=[pl.Blo...  30.7 us
    ppermute x11, waiting for transfers between devices, partner(): lax.ppermute(value, 'mp', [(i, (i + 1) % length) for i in range(length)])  24.4 us
    ppermute x2, waiting for transfers between devices, from_behind(): return lax.ppermute(value, axis, pairs)  23.2 us
  transfers between devices with their start and end apart: 15, of which 8 were waited for; matrix products, arithmetic and copies ran while one was open for 8% of the time, Pallas kernels for 20%

profile of v4, /device:TPU:0, one launch (start us, length us, event | category | flops | bytes accessed | tf_op | source)
XLA Modules:
  0.0 607.7 jit_solution(13628428466795197578)
XLA Ops:
  7.3 1.6 copy.118
  9.8 97.0 %shard_map.249 = (bf16[2,2,2,2,64,1536]{5,4,3,2,1,0:T(8,128)(2,1)S(1)}, bf16[2,2,2,2,64,512]{5,4,3,2,1,0:T(8,128)(2,1)S(1)}, bf16[2,2,2,2,64,2048]{5,4,3,2,1,0:T...) custom-call(bf16[64,4352]{1,0:T(8,128)(2,1)S(1)} %pad_maximum_fusion, ...), custom_call_target="tpu_custom_call" | custom-call | tf_op jit(solution)/shard_map/pallas_call | solution.py:161
  106.8 2.0 copy-done
  108.8 1.6 copy-done.1
  110.4 1.0 copy-done.3
  113.0 1.5 slice_reduce_fusion.1
  116.2 1.1 broadcast_in_dim.71.slots_column
  119.1 0.8 slice.77
  121.1 1.5 reshape.170.gains.refs_5_.refs_4_
  122.6 2.9 maximum_select_fusion
  125.5 1.6 pad.36.stream.refs_0_
  127.2 40.6 %shard_map.250 = (bf16[1200,1024]{1,0:T(8,128)(2,1)}, bf16[1536,1280]{1,0:T(8,128)(2,1)}, bf16[512,1280]{1,0:T(8,128)(2,1)}, f32[8,1280]{1,0:T(8,128)}, bf16[1200,1024]{1,0:T(8,128)(2,1)}) custom-call(s32[5,2]{1,0:T(8,128)} %copy.97.bounds, bf16[1200,1024]{1,0:T(8,128)(2,1)} %pad.36.stream.refs_0_, s32[1,1280]{1,0:T(1,128)} %broadcast_in_dim.61.slots_row, ...), custom_call_target="tpu_custom_call" | custom-call | tf_op jit(solution)/shard_map/pallas_call | solution.py:787
  168.2 4.6 collective-permute-done.1.other
  172.9 15.1 %all-gather.2.cloned.1.call-done.down_w = bf16[1024,2048]{1,0:T(8,128)(2,1)} async-done(((bf16[64,2048]{1,0:T(8,128)(2,1)}), bf16[1024,2048]{1,0:T(8,128)(2,1)}) %all-gather.2.cloned.1.call-update) | async-done | bytes 4194320 | tf_op jit(solution)/shard_map/all_gather | solution.py:1138
  187.9 21.0 %shard_map.251 = (f32[1200,1024]{1,0:T(8,128)}, bf16[1200,1024]{1,0:T(8,128)(2,1)}, bf16[1200,2048]{1,0:T(8,128)(2,1)}, bf16[1200,2048]{1,0:T(8,128)(2,1)}, bf16[1200,1024]{1,0:T(8,128)(2,1)}) custom-call(bf16[1200,1024]{1,0:T(8,128)(2,1)} %pad.36.stream.refs_0_, bf16[1200,1024]{1,0:T(8,128)(2,1)} %get-tuple-element.65.own, ...), custom_call_target="tpu_custom_call" | custom-call | tf_op jit(solution)/shard_map/pallas_call | solution.py:963
  209.5 7.0 %collective-permute-done.2 = bf16[1200,1024]{1,0:T(8,128)(2,1)S(1)} collective-permute-done((bf16[1200,1024]{1,0:T(8,128)(2,1)}, bf16[1200,1024]{1,0:T(8,128)(2,1)S(1)}, u32[]{:S(2)}, u32[]{:S(2)}) %collective-permute-start.2) | collective-permute-done | bytes 2457632 | tf_op jit(solution)/shard_map/ppermute | solution.py:1095
  216.5 4.7 add_convert_fusion.1
  222.7 3.4 collective-permute-start.3
  226.0 9.9 %collective-permute-done.3 = bf16[880,256]{1,0:T(8,128)(2,1)S(1)} collective-permute-done((bf16[880,256]{1,0:T(8,128)(2,1)S(1)}, bf16[880,256]{1,0:T(8,128)(2,1)S(1)}, u32[]{:S(2)}, u32[]{:S(2)}) %collective-permute-start.3) | collective-permute-done | bytes 450592 | tf_op jit(solution)/shard_map/ppermute | solution.py:1090
  238.0 1.0 broadcast_in_dim.70.target_column
  239.0 2.5 reshape_squeeze.3
  241.5 2.5 pad.42.cotangent
  244.6 1.4 reshape.173.gains
  246.1 1.8 pad.41.position
  247.9 71.4 %shard_map.252 = (f32[6,208,512]{2,1,0:T(8,128)}, bf16[896,256]{1,0:T(8,128)(2,1)}, bf16[896,256]{1,0:T(8,128)(2,1)}, bf16[512,3072]{1,0:T(8,128)(2,1)}, bf16[512,3072]{1,0:T(8,128)(2,1)}, /*index=5*/f32[8,512]{1,0:T(8,128)}) custom-call(s32[1]{0:T(128)} %bitcast.15.flag, s32[1,896]{1,0:T(1,128)} %broadcast_in_dim.64.target_row, ...), custom_call_target="tpu_custom_call" | custom-call | tf_op jit(solution)/shard_map/pallas_call | solution.py:644
  319.3 1.1 slice.68
  321.0 1.4 collective-permute-done.6
  322.5 1.1 slice_add_fusion
  323.6 1.3 collective-permute-start.7
  324.9 13.3 %collective-permute-done.7 = bf16[880,256]{1,0:T(8,128)(2,1)S(1)} collective-permute-done((bf16[880,256]{1,0:T(8,128)(2,1)S(1)}, bf16[880,256]{1,0:T(8,128)(2,1)S(1)}, u32[]{:S(2)}, u32[]{:S(2)}) %collective-permute-start.7) | collective-permute-done | bytes 450592 | tf_op jit(solution)/shard_map/ppermute | solution.py:1090
  339.1 4.8 collective-permute-done.8.other.refs_4_
  343.9 30.7 %shard_map.253 = (bf16[1024,2048]{1,0:T(8,128)(2,1)}, bf16[1024,2048]{1,0:T(8,128)(2,1)}, bf16[1200,1024]{1,0:T(8,128)(2,1)}) custom-call(s32[1]{0:T(128)} %bitcast.14.counts, bf16[1200,1024]{1,0:T(8,128)(2,1)} %copy-done.25, bf16[1200,1024]{1,0:T(8,128)(2,1)} %collective-permute-done.8.other.refs_4_, bf16[1200,1024]{1,0:T(8,128)(2,1)} %get-tuple-element.74.second, ...), custom_call_target="tpu_custom_call" | custom-call | tf_op jit(solution)/shard_map/pallas_call | solution.py:1021
  374.7 1.7 copy-done.29
  376.8 6.5 %collective-permute-done.9.refs_2_ = bf16[1200,1024]{1,0:T(8,128)(2,1)} collective-permute-done((bf16[1200,1024]{1,0:T(8,128)(2,1)S(1)}, bf16[1200,1024]{1,0:T(8,128)(2,1)}, u32[]{:S(2)}, u32[]{:S(2)}) %collective-permute-start.9) | collective-permute-done | bytes 2457632 | tf_op jit(solution)/shard_map/ppermute | solution.py:1095
  383.3 11.3 %shard_map.254 = (f32[1200,1024]{1,0:T(8,128)}, bf16[1200,1024]{1,0:T(8,128)(2,1)}, f32[8,1024]{1,0:T(8,128)}) custom-call(f32[1200,1024]{1,0:T(8,128)} %get-tuple-element.68.refs_0_, bf16[1200,1024]{1,0:T(8,128)(2,1)} %get-tuple-element.77.refs_1_, bf16[1200,1024]{1,0:T(8,128)(2,1)} %collective-permute-done.9.refs_2_, bf16[1200,1024]{1,0:T(8,128)(2,1)} %copy-done.25, ...), custom_call_target="tpu_custom_call" | custom-call | tf_op jit(solution)/shard_map/pallas_call | solution.py:1077
  394.7 56.6 %shard_map.255 = (bf16[1024,1536]{1,0:T(8,128)(2,1)}, bf16[1024,512]{1,0:T(8,128)(2,1)}, bf16[1200,1024]{1,0:T(8,128)(2,1)}) custom-call(s32[5,2]{1,0:T(8,128)} %copy.97.bounds, s32[1,1280]{1,0:T(1,128)} %broadcast_in_dim.61.slots_row, s32[1280,1]{1,0:T(8,128)} %broadcast_in_dim.71.slots_column, bf16[1200,1024]{1,0:T(8,128)(2,1)} %get-tuple-element.61.first, ...), custom_call_target="tpu_custom_call" | custom-call | tf_op jit(solution)/shard_map/pallas_call | solution.py:913
  452.7 2.0 slice.69
  454.7 2.2 reshape_reshape.6
  457.0 3.6 convolution_convert_fusion.1
  460.6 4.4 add_convert_fusion
  465.9 10.3 %shard_map.256 = (f32[1200,1024]{1,0:T(8,128)}, f32[8,1024]{1,0:T(8,128)}) custom-call(bf16[1200,1024]{1,0:T(8,128)(2,1)} %pad.36.stream.refs_0_, bf16[1200,1024]{1,0:T(8,128)(2,1)} %get-tuple-element.79.refs_1_, bf16[1200,1024]{1,0:T(8,128)(2,1)} %collective-permute-done.10.refs_2_, f32[1200,1024]{1,0:T(8,128)} %get-tuple-element.80.refs_3_, ...), custom_call_target="tpu_custom_call" | custom-call | tf_op jit(solution)/shard_map/pallas_call | solution.py:1077
  476.2 2.2 select_bitcast_fusion
  478.5 3.9 copy.102
  484.1 105.7 %shard_map.257 = (f32[64,4352]{1,0:T(8,128)}, f32[32,3072]{1,0:T(8,128)}, f32[8,128]{1,0:T(8,128)}, f32[8,128]{1,0:T(8,128)}) custom-call(bf16[2,2,2,2,64,1536]{5,4,3,2,1,0:T(8,128)(2,1)} %bitcast.80, bf16[2,2,2,2,64,512]{5,4,3,2,1,0:T(8,128)(2,1)} %bitcast.81, bf16[2,2,2,2,64,2048]{5,4,3,2,1,0:T(8,128)(2,1)} %bitcast.76, ...), custom_call_target="tpu_custom_call" | custom-call | tf_op jit(solution)/shard_map/pallas_call | solution.py:393
  589.8 1.2 slice.73
  591.8 1.2 copy-done.8
  593.0 1.0 copy-done.15
  595.4 4.1 shard_map.258
  (123 shorter events, 19.3 us)
Async XLA Ops:
  7.2 2.4 copy-start.7
  7.2 2.5 copy-start.17
  7.2 2.5 copy-start.16
  7.2 180.7 %all-gather.2.cloned.1.call-start = ((), (), s32[]{:S(2)}) async-start(), calls=%async_computation.1 | async-start | bytes 4456448 | tf_op jit(solution)/shard_map/all_gather | solution.py:1138
  106.8 2.0 copy-start
  108.8 1.6 copy-start.1
  110.4 1.0 copy-start.3
  111.4 0.8 copy-start.10
  112.8 96.2 %copy-start.4 = (bf16[2,2,2,2,32,3072]{5,4,3,2,1,0:T(8,128)(2,1)}, bf16[2,2,2,2,32,3072]{5,4,3,2,1,0:T(8,128)(2,1)S(1)}, u32[]{:S(2)}) copy-start(bf16[2,2,2,2,32,3072]{5,4,3,2,1,0:T(8,128)(2,1)S(1)} %get-tuple-element.71) | copy-start | bytes 9437188
  112.8 371.2 %reduce-scatter.2.cloned.1.call-start = ((), (), s32[]{:S(2)}) async-start(), calls=%async_computation.2 | async-start | bytes 4456448 | tf_op jit(solution)/shard_map/reduce_scatter | solution.py:1147
  112.9 9.7 %collective-permute-start = (bf16[588,1024]{1,0:T(8,128)(2,1)}, bf16[588,1024]{1,0:T(8,128)(2,1)}, u32[]{:S(2)}, u32[]{:S(2)}) collective-permute-start(bf16[588,1024]{1,0:T(8,128)(2,1)} %bitcast.74), channel_id=1, source_target_pairs={{0,1},{1,0},{2,3},{3,2},{4,5},{5,4},{6,7},{7,6},{8,9},{9,8},{10,11... | collective-permute-start | bytes 3612680 | tf_op jit(solution)/shard_map/ppermute | solution.py:1095
  167.8 5.1 collective-permute-start.1
  208.9 7.6 %collective-permute-start.2 = (bf16[1200,1024]{1,0:T(8,128)(2,1)}, bf16[1200,1024]{1,0:T(8,128)(2,1)S(1)}, u32[]{:S(2)}, u32[]{:S(2)}) collective-permute-start(bf16[1200,1024]{1,0:T(8,128)(2,1)} %get-tuple-element.69), channel_id=1, source_target_pairs={{0,1},{1,0},{2,3},{3,2},{4,5},{5,4},{6,7},{7,6},{8,9},{9,8},{10,11... | collective-permute-start | bytes 7372808 | tf_op jit(solution)/shard_map/ppermute | solution.py:1095
  209.0 38.9 %collective-permute-start.5 = (bf16[512,3072]{1,0:T(8,128)(2,1)S(1)}, bf16[512,3072]{1,0:T(8,128)(2,1)}, u32[]{:S(2)}, u32[]{:S(2)}) collective-permute-start(bf16[512,3072]{1,0:T(8,128)(2,1)S(1)} %bitcast.60), channel_id=1, source_target_pairs={{0,1},{1,0},{2,3},{3,2},{4,5},{5,4},{6,7},{7,6},{8,9},{9,8},{10,11... | collective-permute-start | bytes 9437192 | tf_op jit(solution)/shard_map/ppermute | solution.py:1095
  216.5 4.7 copy-start.11
  221.2 1.5 copy-start.28
  221.2 15.5 %copy-start.33 = (s32[1176]{0:T(1024)S(1)}, s32[1176]{0:T(1024)}, u32[]{:S(2)}) copy-start(s32[1176]{0:T(1024)} %copy-done.32) | copy-start | bytes 14116
  222.7 13.2 %collective-permute-start.3 = (bf16[880,256]{1,0:T(8,128)(2,1)S(1)}, bf16[880,256]{1,0:T(8,128)(2,1)S(1)}, u32[]{:S(2)}, u32[]{:S(2)}) collective-permute-start(bf16[880,256]{1,0:T(8,128)(2,1)S(1)} %fusion.2), channel_id=1, source_target_pairs={{0,16},{1,17},{2,18},{3,19},{4,20},{5,21},{6,22},{7,23},{8,24},{9,... | collective-permute-start | bytes 1351688 | tf_op jit(solution)/shard_map/ppermute | solution.py:1090
  236.7 11.2 %collective-permute-start.4 = (bf16[896,256]{1,0:T(8,128)(2,1)}, bf16[896,256]{1,0:T(8,128)(2,1)}, u32[]{:S(2)}, u32[]{:S(2)}) collective-permute-start(bf16[896,256]{1,0:T(8,128)(2,1)} %pad.40.visible_own), channel_id=1, source_target_pairs={{0,1},{1,0},{2,3},{3,2},{4,5},{5,4},{6,7},{7,6},{8,9},{9,8},{10,11... | collective-permute-start | bytes 1376264 | tf_op jit(solution)/shard_map/ppermute | solution.py:1095
  241.5 2.5 copy-start.31
  319.3 18.9 %copy-start.12 = (bf16[2,2,2,2,64,256]{5,4,3,2,1,0:T(8,128)(2,1)S(1)}, bf16[2,2,2,2,64,256]{5,4,3,2,1,0:T(8,128)(2,1)}, u32[]{:S(2)}) copy-start(bf16[2,2,2,2,64,256]{5,4,3,2,1,0:T(8,128)(2,1)} %copy-done.10) | copy-start | bytes 1572868
  320.4 2.0 collective-permute-start.6
  323.6 14.6 %collective-permute-start.7 = (bf16[880,256]{1,0:T(8,128)(2,1)S(1)}, bf16[880,256]{1,0:T(8,128)(2,1)S(1)}, u32[]{:S(2)}, u32[]{:S(2)}) collective-permute-start(bf16[880,256]{1,0:T(8,128)(2,1)S(1)} %slice_add_fusion), channel_id=1, source_target_pairs={{16,0},{17,1},{18,2},{19,3},{20,4},{21,5},{22,6},{23,7},{24,8},{25... | collective-permute-start | bytes 1351688 | tf_op jit(solution)/shard_map/ppermute | solution.py:1090
  339.0 4.9 copy-start.25
  339.0 4.9 collective-permute-start.8
  374.6 1.7 copy-start.29
  376.3 7.0 %collective-permute-start.9 = (bf16[1200,1024]{1,0:T(8,128)(2,1)S(1)}, bf16[1200,1024]{1,0:T(8,128)(2,1)}, u32[]{:S(2)}, u32[]{:S(2)}) collective-permute-start(bf16[1200,1024]{1,0:T(8,128)(2,1)S(1)} %copy-done.29), channel_id=1, source_target_pairs={{0,1},{1,0},{2,3},{3,2},{4,5},{5,4},{6,7},{7,6},{8,9},{9,8},{10,11... | collective-permute-start | bytes 7372808 | tf_op jit(solution)/shard_map/ppermute | solution.py:1095
  376.5 84.1 %collective-permute-start.11 = (bf16[512,3072]{1,0:T(8,128)(2,1)}, bf16[512,3072]{1,0:T(8,128)(2,1)}, u32[]{:S(2)}, u32[]{:S(2)}) collective-permute-start(bf16[512,3072]{1,0:T(8,128)(2,1)} %get-tuple-element.87), channel_id=1, source_target_pairs={{0,1},{1,0},{2,3},{3,2},{4,5},{5,4},{6,7},{7,6},{8,9},{9,8},{10,11... | collective-permute-start | bytes 9437192 | tf_op jit(solution)/shard_map/ppermute | solution.py:1095
  394.7 57.5 %copy-start.34 = (f32[8,512]{1,0:T(8,128)S(1)}, f32[8,512]{1,0:T(8,128)}, u32[]{:S(2)}) copy-start(f32[8,512]{1,0:T(8,128)} %get-tuple-element.90) | copy-start | bytes 49156
  394.7 58.0 %copy-start.35 = (f32[2]{0:T(128)S(1)}, f32[2]{0:T(128)}, u32[]{:S(2)}) copy-start(f32[2]{0:T(128)} %param.34) | copy-start | bytes 28
  451.3 14.6 %collective-permute-start.10 = (bf16[1200,1024]{1,0:T(8,128)(2,1)}, bf16[1200,1024]{1,0:T(8,128)(2,1)}, u32[]{:S(2)}, u32[]{:S(2)}) collective-permute-start(bf16[1200,1024]{1,0:T(8,128)(2,1)} %get-tuple-element.79.refs_1_), channel_id=1, source_target_pairs={{0,1},{1,0},{2,3},{3,2},{4,5},{5,4},{6,7},{7,6},{8,9},{9,8},{10,11... | collective-permute-start | bytes 7372808 | tf_op jit(solution)/shard_map/ppermute | solution.py:1095
  452.2 4.7 collective-permute-start.12
  457.0 3.6 copy-start.27
  465.9 10.3 %copy-start.26 = (f32[588,1024]{1,0:T(8,128)S(1)}, f32[588,1024]{1,0:T(8,128)}, u32[]{:S(2)}) copy-start(f32[588,1024]{1,0:T(8,128)} %reshape_reshape.6) | copy-start | bytes 7225348
  484.0 107.7 %copy-start.2 = (f32[64,1,6400]{2,1,0:T(1,128)S(1)}, f32[64,1,6400]{2,1,0:T(1,128)}, u32[]{:S(2)}) copy-start(f32[64,1,6400]{2,1,0:T(1,128)} %param.20) | copy-start | bytes 4915204
  484.0 107.7 %copy-start.5 = (f32[64,1,6400]{2,1,0:T(1,128)S(1)}, f32[64,1,6400]{2,1,0:T(1,128)}, u32[]{:S(2)}) copy-start(f32[64,1,6400]{2,1,0:T(1,128)} %param.21) | copy-start | bytes 4915204
  484.0 107.7 %copy-start.6 = (f32[64,1,6400]{2,1,0:T(1,128)S(1)}, f32[64,1,6400]{2,1,0:T(1,128)}, u32[]{:S(2)}) copy-start(f32[64,1,6400]{2,1,0:T(1,128)} %param.22) | copy-start | bytes 4915204
  484.0 107.7 %copy-start.9 = (bf16[64,2048]{1,0:T(8,128)(2,1)S(1)}, bf16[64,2048]{1,0:T(8,128)(2,1)}, u32[]{:S(2)}) copy-start(bf16[64,2048]{1,0:T(8,128)(2,1)} %reduce-scatter.2.cloned.1.call-done.refs_6_.down) | copy-start | bytes 786436
  484.0 107.7 %copy-start.13 = (f32[32,1,3072]{2,1,0:T(1,128)S(1)}, f32[32,1,3072]{2,1,0:T(1,128)}, u32[]{:S(2)}) copy-start(f32[32,1,3072]{2,1,0:T(1,128)} %param.24) | copy-start | bytes 1179652
  484.0 107.7 %copy-start.14 = (f32[32,1,3072]{2,1,0:T(1,128)S(1)}, f32[32,1,3072]{2,1,0:T(1,128)}, u32[]{:S(2)}) copy-start(f32[32,1,3072]{2,1,0:T(1,128)} %param.25) | copy-start | bytes 1179652
  484.0 107.7 %copy-start.21 = (f32[4,64]{1,0:T(4,128)S(1)}, f32[4,64]{1,0:T(4,128)}, u32[]{:S(2)}) copy-start(f32[4,64]{1,0:T(4,128)} %refs_7_.1) | copy-start | bytes 3076
  484.0 107.7 %copy-start.22 = (f32[4,64]{1,0:T(4,128)S(1)}, f32[4,64]{1,0:T(4,128)}, u32[]{:S(2)}) copy-start(f32[4,64]{1,0:T(4,128)} %refs_8_.1) | copy-start | bytes 3076
  484.0 107.7 %copy-start.23 = (f32[4,32]{1,0:T(4,128)S(1)}, f32[4,32]{1,0:T(4,128)}, u32[]{:S(2)}) copy-start(f32[4,32]{1,0:T(4,128)} %refs_10_.1) | copy-start | bytes 1540
  484.1 107.7 %copy-start.24 = (f32[4,32]{1,0:T(4,128)S(1)}, f32[4,32]{1,0:T(4,128)}, u32[]{:S(2)}) copy-start(f32[4,32]{1,0:T(4,128)} %refs_11_.1) | copy-start | bytes 1540
  591.8 1.2 copy-start.8
  593.0 1.0 copy-start.15
  594.0 0.7 copy-start.18
  594.7 0.7 copy-start.19
  (3 other events, 1.8 us)
Sparse Core Ops, SparseCore 0:
  112.9 74.9 all-gather.1
  374.8 93.2 reduce-scatter.1

commit v5 on v4

--- a/solution.py
+++ b/solution.py
@@ -148,7 +148,7 @@
             jax.ShapeDtypeStruct((2, 2, 2, 2, rows, width), dtype) for rows, width, dtype in outputs
         ],
         in_specs=[pl.BlockSpec(memory_space=pltpu.VMEM)] * len(shards),
-        out_specs=[pl.BlockSpec(memory_space=pl.ANY)] * len(outputs),
+        out_specs=[pl.BlockSpec(memory_space=pltpu.HBM)] * len(outputs),
         scratch_shapes=[
             pltpu.SemaphoreType.DMA((count, 4)),
             pltpu.SemaphoreType.DMA((count, 4)),
@@ -211,12 +211,13 @@
     ins, summed, outs = refs[:n_in], refs[n_in], refs[n_in + 1 : n_in + 1 + n_out]
     square_total = refs[n_in + 1 + n_out]
     rest = refs[n_in + n_out + 2 :]
-    send, recv, local, square_send, square_recv, square_mine, square_there = rest[:7]
+    send, recv, local, square_send, square_recv, square_mine, square_there, last, last_there = rest[:9]
     here = Place()
     s = here.s
     count = len(chunks)
+    given, ins = ins[-1], (*ins[:-1], last)
     own, got = [], []
-    position = 7
+    position = 9
     for chunk in chunks:
         order, owner = chunk[5], chunk[6]
         own.append(rest[position])
@@ -316,13 +317,25 @@
         run(roles(i, stage)[1], add)
 
     here.greet()
-    for i in range(count):
+    join = pltpu.make_async_remote_copy(
+        src_ref=given,
+        dst_ref=last_there,
+        send_sem=square_send.at[5],
+        recv_sem=square_recv.at[5],
+        device_id=here.device["c"],
+        device_id_type=MESH_ID,
+    )
+    join.start()
+    for i in range(count - 1):
         run(
             None if chunks[i][6] == BOTH else s == chunks[i][6],
             lambda i=i: load(i).start(),
         )
     for i in range(min(ahead, count)):
         begin(i, 0)
+    join.wait()
+    last[...] = given[...] + last_there[...]
+    load(count - 1).start()
     for step in range(count + sum(lag)):
         for stage in range(3, -1, -1):
             i = step - sum(lag[:stage])
@@ -373,17 +386,19 @@
         out_shape=[
             jax.ShapeDtypeStruct((rows, width), jnp.float32) for rows, width in [*outputs, (8, 128)]
         ],
-        in_specs=[pl.BlockSpec(memory_space=pl.ANY)] * len(parts)
-        + [pl.BlockSpec(memory_space=pltpu.VMEM)],
+        in_specs=[pl.BlockSpec(memory_space=pl.ANY)] * (len(parts) - 1)
+        + [pl.BlockSpec(memory_space=pltpu.VMEM)] * 2,
         out_specs=[pl.BlockSpec(memory_space=pltpu.VMEM)] * (len(outputs) + 1),
         scratch_shapes=[
             pltpu.SemaphoreType.DMA((count, 4)),
             pltpu.SemaphoreType.DMA((count, 4)),
             pltpu.SemaphoreType.DMA((count,)),
-            pltpu.SemaphoreType.DMA((5,)),
-            pltpu.SemaphoreType.DMA((5,)),
+            pltpu.SemaphoreType.DMA((6,)),
+            pltpu.SemaphoreType.DMA((6,)),
             pltpu.VMEM((5, 8, 128), jnp.float32),
             pltpu.VMEM((5, 8, 128), jnp.float32),
+            pltpu.VMEM(views[-1].shape, views[-1].dtype),
+            pltpu.VMEM(views[-1].shape, views[-1].dtype),
             *buffers,
         ],
         compiler_params=pltpu.CompilerParams(
@@ -616,17 +631,12 @@
 
 
 def decoder_step(
-    left, visible_own, visible_other, target, mask, position, gains, pack_own, pack_other, cotangent, images
+    length, left, visible_own, visible_other, target, mask, position, gains, pack_own, pack_other, cotangent
 ):
-    length, width = position.shape
-    rows = -(-length // 16) * 16
+    rows, width = position.shape
     packed = visible_own.shape[0]
-    columns = pack_own.shape[1]
+    images, columns = cotangent.shape[0], pack_own.shape[1]
     units = columns - 2 * width
-    cotangent = jnp.pad(
-        cotangent.reshape(images, length, width), ((0, 0), (0, rows - length), (0, 0))
-    )
-    position = jnp.pad(position, ((0, rows - length), (0, 0)))
 
     def fixed(shape):
         return pl.BlockSpec(shape, lambda i: (0,) * len(shape), pipeline_mode=pl.Buffered(1))
@@ -696,7 +706,6 @@
         pack_other,
         cotangent,
     )
-    decoded = decoded[:, :length].reshape(images * length, width)
     return decoded, keep, send, grad_own, grad_other, grad_gains[:4]
 
 
@@ -1084,6 +1093,47 @@
     )(tokens, own, other, *skip, gains)
 
 
+def finish_kernel(length, flag, tokens, own, other, skip, gains, decoded, result, grad_gains):
+    pulled = own[...].astype(WIDE) + other[...].astype(WIDE)
+    unit, scale = centre(tokens[...].astype(WIDE))
+    grad_gains[...] = jnp.zeros_like(grad_gains)
+    grad_gains[0:1] = jnp.sum(pulled * unit, axis=0, keepdims=True)
+    grad_gains[1:2] = jnp.sum(pulled, axis=0, keepdims=True)
+    rows, width = tokens.shape
+    pieces = width // 128
+
+    @pl.when(flag[0] > 0)
+    def _():
+        grad = skip[...] + centre_back(unit, scale, gains[0:1], pulled)
+        for k in range(pieces):
+            result[pl.ds(k, rows, stride=pieces), :] = grad[:, k * 128 : (k + 1) * 128]
+
+    @pl.when(flag[0] == 0)
+    def _():
+        images, _, columns = decoded.shape
+        count = columns // 128
+        for i in range(images):
+            for k in range(count):
+                result[pl.ds(i * length * count + k, length, stride=count), :] = decoded[
+                    i, 0:length, k * 128 : (k + 1) * 128
+                ]
+
+
+def encoder_finish(encoder_side, tokens, own, other, skip, gains, decoded, length):
+    rows, width = tokens.shape
+    return pl.pallas_call(
+        functools.partial(finish_kernel, length),
+        in_specs=[pl.BlockSpec(memory_space=pltpu.SMEM)]
+        + [pl.BlockSpec(memory_space=pltpu.VMEM)] * 6,
+        out_specs=[pl.BlockSpec(memory_space=pltpu.VMEM)] * 2,
+        out_shape=[
+            jax.ShapeDtypeStruct((rows * width // 128, 128), WIDE),
+            jax.ShapeDtypeStruct((8, width), WIDE),
+        ],
+        compiler_params=pltpu.CompilerParams(vmem_limit_bytes=60 * 2**20),
+    )(encoder_side.astype(jnp.int32).reshape(1), tokens, own, other, skip, gains, decoded)
+
+
 def from_behind(value, axis, by):
     length = lax.axis_size(axis)
     pairs = [(i, i + by) for i in range(length) if 0 <= i + by < length]
@@ -1149,7 +1199,7 @@
     if not is_fast():
         parts = [scattered(jnp.where(encoder_side, p.astype(WIDE), 0.0)) for p in enc_parts]
         dec = scattered(jnp.where(encoder_side, 0.0, dec.astype(WIDE)))
-        norms = scattered(norms)
+        norms = lax.psum(scattered(norms), "mp")
         local = sum(jnp.sum(v * v) for v in (*parts, dec))
         local = local + jnp.sum(norms * norms) / lax.axis_size("mp")
         total = jnp.full((8, 128), lax.psum(local, (*both, "mp")))
@@ -1293,13 +1343,6 @@
     slots = jnp.pad(slot_ids, (0, lanes - real_rows), constant_values=IMG + 1)
     ranges = key_ranges(slots)
 
-    def halves(own, other, axis):
-        return jnp.where(
-            first_half,
-            jnp.concatenate([own, other], axis=axis),
-            jnp.concatenate([other, own], axis=axis),
-        )
-
     (qkv_w, out_w, up_w, down_w, projection), dec_own, norm_rows = gather_all(
         enc_weights[:, 0, :].astype(LOW),
         dec_weights[:, 0, :].astype(LOW),
@@ -1312,40 +1355,52 @@
             norm_rows, norm_rows.shape[0] // 8, enc_norms.shape[1], dec_norms.shape[1]
         )
     )
-    stream = halves(act_in[0], partner(act_in[0]), 0)
+    own_stream, other_stream = act_in[0], partner(act_in[0])
+    stream = jnp.where(
+        first_half,
+        jnp.concatenate([own_stream, other_stream], axis=0),
+        jnp.concatenate([other_stream, own_stream], axis=0),
+    )
     stream = jnp.pad(stream, ((0, rows - real_rows), (0, 0)))
     first, turned, mixture, log_sum, mix_own = encoder_attend(
         stream, slots, ranges, enc_gains, qkv_w, out_w, head
     )
-    after, second, hidden, slope, feed_own = encoder_feed(
-        stream, mix_own, partner(mix_own), enc_gains, up_w, down_w, ROW_BLOCK
-    )
-    encoded = (after + (feed_own.astype(WIDE) + partner(feed_own).astype(WIDE))).astype(LOW)
     shown = min(real_rows, -(-IMG * MOST_VISIBLE // 16) * 16)
     packed = -(-shown // 128) * 128
+    cell_rows = -(-GRID // 16) * 16
+    longer = (0, cell_rows - GRID)
+    seen_target = jnp.pad(target[:shown], (0, packed - shown), constant_values=-1)
+    cotangent = act_in[0].reshape(local_images, GRID, dec_width)
+    cotangent = jnp.pad(cotangent, ((0, 0), longer, (0, 0)))
+    position = jnp.pad(dec_position, (longer, (0, 0)))
+    mix_other, seen_target, cotangent, position, dec_gains = lax.optimization_barrier(
+        (partner(mix_own), seen_target, cotangent, position, dec_gains)
+    )
+    after, second, hidden, slope, feed_own = encoder_feed(
+        stream, mix_own, mix_other, enc_gains, up_w, down_w, ROW_BLOCK
+    )
+    encoded = (after + (feed_own.astype(WIDE) + partner(feed_own).astype(WIDE))).astype(LOW)
     projected = mm(encoded[:shown], projection).astype(LOW)
     arrived = from_behind(projected, "section", 1)
     arrived = jnp.pad(arrived, ((0, packed - shown), (0, 0)))
-    seen_target = jnp.pad(target[:shown], (0, packed - shown), constant_values=-1)
     decoded, grad_keep, grad_send, dec_grad_own, dec_grad_other, dec_gain_grad = decoder_step(
+        GRID,
         first_half,
         arrived,
         partner(arrived),
         seen_target,
         mask_token,
-        dec_position,
+        position,
         dec_gains,
         dec_own,
         partner(dec_own),
-        act_in[0],
-        local_images,
+        cotangent,
     )
     returned = grad_keep[:shown] + partner(grad_send[:shown])
     grad_projected = from_behind(returned, "section", -1)
     grad_projected = jnp.pad(grad_projected, ((0, rows - shown), (0, 0)))
     dec_grad = dec_grad_own.astype(WIDE) + partner(dec_grad_other).astype(WIDE)
     dec_grad = dec_grad.astype(LOW)
-    dec_gain_grad = dec_gain_grad + partner(dec_gain_grad)
 
     grad_projection = mm(encoded, grad_projected, 0, 0).astype(LOW)
     end_own = mm(grad_projected, projection, 1, 1).astype(LOW)
@@ -1366,10 +1421,24 @@
     grad_qkv_w, grad_out_w, start_own = encoder_attend_back(
         slots, ranges, first, turned, mixture, log_sum, grad_low, qkv_w, out_w, head
     )
-    grad_stream, gains_one = encoder_norm_back(
-        stream, start_own, partner(start_own), (grad_after,), enc_gains, 0, ROW_BLOCK, False
-    )
-    enc_gain_grad = jnp.concatenate([gains_one[:2], gains_two[:2]], axis=0)
+    def choose(matrix):
+        top, bottom = matrix[:local_rows], matrix[local_rows:real_rows]
+        return jnp.where(first_half, top, bottom), jnp.where(first_half, bottom, top)
+
+    start_keep, start_send = choose(start_own)
+    act_out, gains_one = encoder_finish(
+        encoder_side,
+        own_stream,
+        start_keep,
+        partner(start_send),
+        choose(grad_after)[0],
+        enc_gains,
+        decoded,
+        GRID,
+    )
+    enc_gain_grad = jnp.concatenate(
+        [gains_one[:2], jnp.where(first_half, gains_two[:2], 0.0)], axis=0
+    )
     norm_grads = pack_norms(
         jnp.where(encoder_side, enc_gain_grad, 0.0),
         jnp.where(decoder_side, dec_gain_grad, 0.0),
@@ -1403,9 +1472,7 @@
         (enc_norms, enc_norm_first, enc_norm_second),
         (dec_norms, dec_norm_first, dec_norm_second),
     )
-    own_grad = lax.dynamic_slice_in_dim(grad_stream, mp_rank * local_rows, local_rows, axis=0)
-    act_out = jnp.where(encoder_side, own_grad, decoded.reshape(local_rows, width))[None]
-    return (act_out, *results, jnp.sqrt(square_total[0, 0]).reshape(1))
+    return (act_out.reshape(act_in.shape), *results, jnp.sqrt(square_total[0, 0]).reshape(1))
 
 
 def solution(mesh):

time: 614 us -> 603 us (0.982); the launches traced: 608 us -> 603 us
  local copies, waits for them, and re-layouts: 46.9 us -> 39.1 us
  other arithmetic: 19.4 us -> 27.1 us
  waiting for transfers between devices: 62.6 us -> 54.9 us
    pallas_call x1, Pallas kernels: 71.4 us -> 84.7 us  [decoder_step(): pl.pallas_call(functools.partial(decoder_kernel, length), grid=(images //...]
    pallas_call x2 -> x1, Pallas kernels: 21.7 us -> 11.3 us  [encoder_norm_back(): pl.pallas_call(kernel, grid=(rows // block,), in_specs=[wide, wide, wide]...]
    ppermute x11 -> x10, waiting for transfers between devices: 24.4 us -> 14.6 us  [partner(): lax.ppermute(value, 'mp', [(i, (i + 1) % length) for i in range(length)])]
    select_n x1 -> x4, other arithmetic: 2.92 us -> 12.5 us  [the longest x1 4.66 us: choose(): jnp.where(first_half, top, bottom)]
    pallas_call x1, Pallas kernels: 106 us -> 114 us  [scatter_grads(): return call(*views, summed)]
    pallas_call x1, Pallas kernels: 56.6 us -> 48.8 us  [encoder_attend_back(): pl.pallas_call(functools.partial(attend_back_kernel, head), in_specs=[pl....]
    pallas_call x0 -> x1, Pallas kernels: none -> 7.36 us  [encoder_finish(): pl.pallas_call(functools.partial(finish_kernel, length), in_specs=[pl.Blo...]
    unnamed x76 -> x75, local copies, waits for them, and re-layouts: 18.9 us -> 13.3 us
  transfers between devices with their start and end apart: 15 -> 14, of which waited for: 8 -> 9; matrix products, arithmetic and copies ran while one was open for 8% -> 9% of each run, Pallas kernels for 20% -> 17%
where the time goes in v5:
time: 603 us
  Pallas kernels  453 us (75%)
  waiting for transfers between devices  54.9 us (9%)
  local copies, waits for them, and re-layouts  39.1 us (6%)
  other arithmetic  27.1 us (4%)
  between operations  17.3 us (3%)
  starting transfers between devices  6.81 us (1%)
    pallas_call x1, Pallas kernels, scatter_grads(): return call(*views, summed)  114 us
    pallas_call x1, Pallas kernels, gather_weights(): results = call(*shards)  97 us
    pallas_call x1, Pallas kernels, decoder_step(): pl.pallas_call(functools.partial(decoder_kernel, length), grid=(images //...  84.7 us
    pallas_call x1, Pallas kernels, encoder_attend_back(): pl.pallas_call(functools.partial(attend_back_kernel, head), in_specs=[pl....  48.8 us
    pallas_call x1, Pallas kernels, encoder_attend(): pl.pallas_call(functools.partial(attend_kernel, head), in_specs=[pl.Block...  34.9 us
    pallas_call x1, Pallas kernels, encoder_feed_back(): pl.pallas_call(feed_back_kernel, grid=(units // piece,), in_specs=[pl.Blo...  30.6 us
    ppermute x2, waiting for transfers between devices, from_behind(): return lax.ppermute(value, axis, pairs)  23.1 us
    pallas_call x1, Pallas kernels, encoder_feed(): pl.pallas_call(feed_kernel, grid=(rows // block,), in_specs=[wide, wide,...  20.5 us
  transfers between devices with their start and end apart: 14, of which 9 were waited for; matrix products, arithmetic and copies ran while one was open for 9% of the time, Pallas kernels for 17%

profile of v5, /device:TPU:0, one launch (start us, length us, event | category | flops | bytes accessed | tf_op | source)
XLA Modules:
  0.0 603.1 jit_solution(13259275162839837192)
XLA Ops:
  7.3 1.6 copy.118
  9.8 97.0 %shard_map.249 = (bf16[2,2,2,2,64,1536]{5,4,3,2,1,0:T(8,128)(2,1)S(1)}, bf16[2,2,2,2,64,512]{5,4,3,2,1,0:T(8,128)(2,1)S(1)}, bf16[2,2,2,2,64,2048]{5,4,3,2,1,0:T...) custom-call(bf16[64,4352]{1,0:T(8,128)(2,1)S(1)} %pad_maximum_fusion, ...), custom_call_target="tpu_custom_call" | custom-call | tf_op jit(solution)/shard_map/pallas_call | solution.py:161
  106.8 2.0 copy-done
  108.8 1.6 copy-done.1
  110.4 1.0 copy-done.3
  112.9 1.6 slice_reduce_fusion
  116.3 1.1 broadcast_in_dim.72.slots_column
  117.4 0.8 fusion.16
  121.2 1.4 reshape.183.gains.refs_5_
  122.7 3.5 maximum_select_fusion
  126.2 1.7 pad.37.stream
  127.8 34.9 %shard_map.250 = (bf16[1200,1024]{1,0:T(8,128)(2,1)}, bf16[1536,1280]{1,0:T(8,128)(2,1)}, bf16[512,1280]{1,0:T(8,128)(2,1)}, f32[8,1280]{1,0:T(8,128)}, bf16[1200,1024]{1,0:T(8,128)(2,1)}) custom-call(s32[5,2]{1,0:T(8,128)} %copy.97.bounds, bf16[1200,1024]{1,0:T(8,128)(2,1)} %pad.37.stream, s32[1,1280]{1,0:T(1,128)} %broadcast_in_dim.62.slots_row, ...), custom_call_target="tpu_custom_call" | custom-call | tf_op jit(solution)/shard_map/pallas_call | solution.py:796
  163.1 2.5 reshape_squeeze.3
  165.6 2.5 pad.40.cotangent
  168.7 1.4 reshape.184.gains
  170.1 1.8 pad.41.position
  171.9 1.3 fusion.12
  173.2 14.5 %all-gather.2.cloned.1.call-done.down_w = bf16[1024,2048]{1,0:T(8,128)(2,1)} async-done(((bf16[64,2048]{1,0:T(8,128)(2,1)}), bf16[1024,2048]{1,0:T(8,128)(2,1)}) %all-gather.2.cloned.1.call-update) | async-done | bytes 4194320 | tf_op jit(solution)/shard_map/all_gather | solution.py:1188
  187.8 20.5 %shard_map.251 = (f32[1200,1024]{1,0:T(8,128)}, bf16[1200,1024]{1,0:T(8,128)(2,1)}, bf16[1200,2048]{1,0:T(8,128)(2,1)}, bf16[1200,2048]{1,0:T(8,128)(2,1)}, bf16[1200,1024]{1,0:T(8,128)(2,1)}) custom-call(bf16[1200,1024]{1,0:T(8,128)(2,1)} %pad.37.stream, bf16[1200,1024]{1,0:T(8,128)(2,1)} %get-tuple-element.70.own, ...), custom_call_target="tpu_custom_call" | custom-call | tf_op jit(solution)/shard_map/pallas_call | solution.py:972
  208.8 7.1 %collective-permute-done.2 = bf16[1200,1024]{1,0:T(8,128)(2,1)S(1)} collective-permute-done((bf16[1200,1024]{1,0:T(8,128)(2,1)}, bf16[1200,1024]{1,0:T(8,128)(2,1)S(1)}, u32[]{:S(2)}, u32[]{:S(2)}) %collective-permute-start.2) | collective-permute-done | bytes 2457632 | tf_op jit(solution)/shard_map/ppermute | solution.py:1145
  215.8 4.7 add_convert_fusion.1
  222.0 3.4 collective-permute-start.3
  225.4 9.9 %collective-permute-done.3 = bf16[880,256]{1,0:T(8,128)(2,1)S(1)} collective-permute-done((bf16[880,256]{1,0:T(8,128)(2,1)S(1)}, bf16[880,256]{1,0:T(8,128)(2,1)S(1)}, u32[]{:S(2)}, u32[]{:S(2)}) %collective-permute-start.3) | collective-permute-done | bytes 450592 | tf_op jit(solution)/shard_map/ppermute | solution.py:1140
  236.7 1.0 broadcast_in_dim.71.target_column
  238.3 84.7 %shard_map.252 = (f32[6,208,512]{2,1,0:T(8,128)}, bf16[896,256]{1,0:T(8,128)(2,1)}, bf16[896,256]{1,0:T(8,128)(2,1)}, bf16[512,3072]{1,0:T(8,128)(2,1)}, bf16[512,3072]{1,0:T(8,128)(2,1)}, /*index=5*/f32[8,512]{1,0:T(8,128)}) custom-call(s32[1]{0:T(128)} %bitcast.16.flag, s32[1,896]{1,0:T(1,128)} %broadcast_in_dim.65.target_row, ...), custom_call_target="tpu_custom_call" | custom-call | tf_op jit(solution)/shard_map/pallas_call | solution.py:654
  323.0 1.1 slice.77
  324.4 1.5 collective-permute-done.6
  326.0 1.1 slice_add_fusion
  327.1 1.3 collective-permute-start.7
  328.4 13.3 %collective-permute-done.7 = bf16[880,256]{1,0:T(8,128)(2,1)S(1)} collective-permute-done((bf16[880,256]{1,0:T(8,128)(2,1)S(1)}, bf16[880,256]{1,0:T(8,128)(2,1)S(1)}, u32[]{:S(2)}, u32[]{:S(2)}) %collective-permute-start.7) | collective-permute-done | bytes 450592 | tf_op jit(solution)/shard_map/ppermute | solution.py:1140
  342.6 4.8 collective-permute-done.8.other.refs_4_
  347.4 30.6 %shard_map.253 = (bf16[1024,2048]{1,0:T(8,128)(2,1)}, bf16[1024,2048]{1,0:T(8,128)(2,1)}, bf16[1200,1024]{1,0:T(8,128)(2,1)}) custom-call(s32[1]{0:T(128)} %bitcast.15.counts, bf16[1200,1024]{1,0:T(8,128)(2,1)} %copy-done.25, bf16[1200,1024]{1,0:T(8,128)(2,1)} %collective-permute-done.8.other.refs_4_, bf16[1200,1024]{1,0:T(8,128)(2,1)} %get-tuple-element.84.second, ...), custom_call_target="tpu_custom_call" | custom-call | tf_op jit(solution)/shard_map/pallas_call | solution.py:1030
  379.4 1.3 slice_select_fusion.1
  380.8 1.4 reshape.169
  382.2 1.4 copy.120
  383.5 3.5 convolution_convert_fusion.1
  387.6 11.3 %shard_map.254 = (f32[1200,1024]{1,0:T(8,128)}, bf16[1200,1024]{1,0:T(8,128)(2,1)}, f32[8,1024]{1,0:T(8,128)}) custom-call(f32[1200,1024]{1,0:T(8,128)} %get-tuple-element.74.refs_0_, bf16[1200,1024]{1,0:T(8,128)(2,1)} %get-tuple-element.87.refs_1_, bf16[1200,1024]{1,0:T(8,128)(2,1)} %collective-permute-done.9.refs_2_, bf16[1200,1024]{1,0:T(8,128)(2,1)} %copy-done.25, ...), custom_call_target="tpu_custom_call" | custom-call | tf_op jit(solution)/shard_map/pallas_call | solution.py:1086
  399.0 48.8 %shard_map.255 = (bf16[1024,1536]{1,0:T(8,128)(2,1)}, bf16[1024,512]{1,0:T(8,128)(2,1)}, bf16[1200,1024]{1,0:T(8,128)(2,1)}) custom-call(s32[5,2]{1,0:T(8,128)} %copy.97.bounds, s32[1,1280]{1,0:T(1,128)} %broadcast_in_dim.62.slots_row, s32[1280,1]{1,0:T(8,128)} %broadcast_in_dim.72.slots_column, bf16[1200,1024]{1,0:T(8,128)(2,1)} %get-tuple-element.66.first, ...), custom_call_target="tpu_custom_call" | custom-call | tf_op jit(solution)/shard_map/pallas_call | solution.py:922
  447.7 3.6 broadcast_select_fusion
  451.5 2.9 add_convert_fusion
  455.2 4.7 slice_select_fusion.skip
  459.9 7.4 %shard_map.256 = (f32[4704,128]{1,0:T(8,128)}, f32[8,1024]{1,0:T(8,128)}) custom-call(s32[1]{0:T(128)} %bitcast.flag, bf16[588,1024]{1,0:T(8,128)(2,1)} %bitcast.76, bf16[588,1024]{1,0:T(8,128)(2,1)} %get-tuple-element.171.own, bf16[588,1024]{1,0:T(8,128)(2,1)} %collective-permute-done.10.other, f32[588,1024]{1,0:T(8,128)} %slice_select_fusion.skip, ...), custom_call_target="tpu_custom_call" | custom-call | tf_op jit(solution)/shard_map/pallas_call | solution.py:1124
  468.9 2.6 reduce-scatter.2.cloned.1.call-done.refs_6_.down
  471.5 113.7 %shard_map.257 = (f32[64,4352]{1,0:T(8,128)}, f32[32,3072]{1,0:T(8,128)}, f32[8,128]{1,0:T(8,128)}, f32[8,128]{1,0:T(8,128)}) custom-call(bf16[2,2,2,2,64,1536]{5,4,3,2,1,0:T(8,128)(2,1)} %bitcast.81, bf16[2,2,2,2,64,512]{5,4,3,2,1,0:T(8,128)(2,1)} %bitcast.82, bf16[2,2,2,2,64,2048]{5,4,3,2,1,0:T(8,128)(2,1)} %bitcast.77, ...), custom_call_target="tpu_custom_call" | custom-call | tf_op jit(solution)/shard_map/pallas_call | solution.py:408
  585.2 1.2 slice.85
  587.2 1.2 copy-done.8
  588.5 1.0 copy-done.15
  590.8 4.1 shard_map.258
  (118 shorter events, 18.9 us)
Async XLA Ops:
  7.2 2.4 copy-start.7
  7.2 2.5 copy-start.17
  7.2 2.5 copy-start.16
  7.2 180.6 %all-gather.2.cloned.1.call-start = ((), (), s32[]{:S(2)}) async-start(), calls=%async_computation.1 | async-start | bytes 4456448 | tf_op jit(solution)/shard_map/all_gather | solution.py:1188
  106.8 2.0 copy-start
  108.8 1.6 copy-start.1
  110.4 1.0 copy-start.3
  111.4 0.8 copy-start.10
  112.1 0.6 copy-start.20
  112.8 95.5 %copy-start.4 = (bf16[2,2,2,2,32,3072]{5,4,3,2,1,0:T(8,128)(2,1)}, bf16[2,2,2,2,32,3072]{5,4,3,2,1,0:T(8,128)(2,1)S(1)}, u32[]{:S(2)}) copy-start(bf16[2,2,2,2,32,3072]{5,4,3,2,1,0:T(8,128)(2,1)S(1)} %get-tuple-element.80) | copy-start | bytes 9437188
  112.8 358.7 %reduce-scatter.2.cloned.1.call-start = ((), (), s32[]{:S(2)}) async-start(), calls=%async_computation.2 | async-start | bytes 4456448 | tf_op jit(solution)/shard_map/reduce_scatter | solution.py:1197
  112.8 9.8 %collective-permute-start = (bf16[588,1024]{1,0:T(8,128)(2,1)}, bf16[588,1024]{1,0:T(8,128)(2,1)}, u32[]{:S(2)}, u32[]{:S(2)}) collective-permute-start(bf16[588,1024]{1,0:T(8,128)(2,1)} %bitcast.74), channel_id=1, source_target_pairs={{0,1},{1,0},{2,3},{3,2},{4,5},{5,4},{6,7},{7,6},{8,9},{9,8},{10,11... | collective-permute-start | bytes 3612680 | tf_op jit(solution)/shard_map/ppermute | solution.py:1145
  162.7 9.2 %copy-start.33 = (s32[1176]{0:T(1024)S(1)}, s32[1176]{0:T(1024)}, u32[]{:S(2)}) copy-start(s32[1176]{0:T(1024)} %copy-done.32) | copy-start | bytes 14116
  162.7 10.5 %collective-permute-start.1 = (bf16[1200,1024]{1,0:T(8,128)(2,1)}, bf16[1200,1024]{1,0:T(8,128)(2,1)}, u32[]{:S(2)}, u32[]{:S(2)}) collective-permute-start(bf16[1200,1024]{1,0:T(8,128)(2,1)} %get-tuple-element.70.own), channel_id=1, source_target_pairs={{0,1},{1,0},{2,3},{3,2},{4,5},{5,4},{6,7},{7,6},{8,9},{9,8},{10,11... | collective-permute-start | bytes 7372808 | tf_op jit(solution)/shard_map/ppermute | solution.py:1145
  165.6 2.5 copy-start.30
  208.2 7.6 %collective-permute-start.2 = (bf16[1200,1024]{1,0:T(8,128)(2,1)}, bf16[1200,1024]{1,0:T(8,128)(2,1)S(1)}, u32[]{:S(2)}, u32[]{:S(2)}) collective-permute-start(bf16[1200,1024]{1,0:T(8,128)(2,1)} %get-tuple-element.76), channel_id=1, source_target_pairs={{0,1},{1,0},{2,3},{3,2},{4,5},{5,4},{6,7},{7,6},{8,9},{9,8},{10,11... | collective-permute-start | bytes 7372808 | tf_op jit(solution)/shard_map/ppermute | solution.py:1145
  208.3 29.4 %collective-permute-start.5 = (bf16[512,3072]{1,0:T(8,128)(2,1)S(1)}, bf16[512,3072]{1,0:T(8,128)(2,1)}, u32[]{:S(2)}, u32[]{:S(2)}) collective-permute-start(bf16[512,3072]{1,0:T(8,128)(2,1)S(1)} %bitcast.60), channel_id=1, source_target_pairs={{0,1},{1,0},{2,3},{3,2},{4,5},{5,4},{6,7},{7,6},{8,9},{9,8},{10,11... | collective-permute-start | bytes 9437192 | tf_op jit(solution)/shard_map/ppermute | solution.py:1145
  215.8 4.7 copy-start.11
  220.5 1.5 copy-start.27
  220.5 15.6 %copy-start.34 = (s32[896]{0:T(1024)S(1)}, s32[896]{0:T(1024)}, u32[]{:S(2)}) copy-start(s32[896]{0:T(1024)} %fusion.12) | copy-start | bytes 10756
  222.0 13.3 %collective-permute-start.3 = (bf16[880,256]{1,0:T(8,128)(2,1)S(1)}, bf16[880,256]{1,0:T(8,128)(2,1)S(1)}, u32[]{:S(2)}, u32[]{:S(2)}) collective-permute-start(bf16[880,256]{1,0:T(8,128)(2,1)S(1)} %fusion.2), channel_id=1, source_target_pairs={{0,16},{1,17},{2,18},{3,19},{4,20},{5,21},{6,22},{7,23},{8,24},{9,... | collective-permute-start | bytes 1351688 | tf_op jit(solution)/shard_map/ppermute | solution.py:1140
  236.1 2.2 collective-permute-start.4
  323.0 18.6 %copy-start.12 = (bf16[2,2,2,2,64,256]{5,4,3,2,1,0:T(8,128)(2,1)S(1)}, bf16[2,2,2,2,64,256]{5,4,3,2,1,0:T(8,128)(2,1)}, u32[]{:S(2)}) copy-start(bf16[2,2,2,2,64,256]{5,4,3,2,1,0:T(8,128)(2,1)} %copy-done.10) | copy-start | bytes 1572868
  324.1 1.9 collective-permute-start.6
  327.1 14.6 %collective-permute-start.7 = (bf16[880,256]{1,0:T(8,128)(2,1)S(1)}, bf16[880,256]{1,0:T(8,128)(2,1)S(1)}, u32[]{:S(2)}, u32[]{:S(2)}) collective-permute-start(bf16[880,256]{1,0:T(8,128)(2,1)S(1)} %slice_add_fusion), channel_id=1, source_target_pairs={{16,0},{17,1},{18,2},{19,3},{20,4},{21,5},{22,6},{23,7},{24,8},{25... | collective-permute-start | bytes 1351688 | tf_op jit(solution)/shard_map/ppermute | solution.py:1140
  341.6 0.8 copy-start.28
  342.5 4.9 copy-start.25
  342.5 4.9 collective-permute-start.8
  378.0 1.4 copy-start.35
  378.0 73.4 %collective-permute-start.11 = (bf16[512,3072]{1,0:T(8,128)(2,1)}, bf16[512,3072]{1,0:T(8,128)(2,1)S(1)}, u32[]{:S(2)}, u32[]{:S(2)}) collective-permute-start(bf16[512,3072]{1,0:T(8,128)(2,1)} %get-tuple-element.97), channel_id=1, source_target_pairs={{0,1},{1,0},{2,3},{3,2},{4,5},{5,4},{6,7},{7,6},{8,9},{9,8},{10,11... | collective-permute-start | bytes 9437192 | tf_op jit(solution)/shard_map/ppermute | solution.py:1145
  378.2 9.4 %collective-permute-start.9 = (bf16[1200,1024]{1,0:T(8,128)(2,1)}, bf16[1200,1024]{1,0:T(8,128)(2,1)}, u32[]{:S(2)}, u32[]{:S(2)}) collective-permute-start(bf16[1200,1024]{1,0:T(8,128)(2,1)} %get-tuple-element.87.refs_1_), channel_id=1, source_target_pairs={{0,1},{1,0},{2,3},{3,2},{4,5},{5,4},{6,7},{7,6},{8,9},{9,8},{10,11... | collective-permute-start | bytes 7372808 | tf_op jit(solution)/shard_map/ppermute | solution.py:1145
  447.7 3.7 copy-start.26
  451.3 8.6 %collective-permute-start.10 = (bf16[588,1024]{1,0:T(8,128)(2,1)}, bf16[588,1024]{1,0:T(8,128)(2,1)}, u32[]{:S(2)}, u32[]{:S(2)}) collective-permute-start(bf16[588,1024]{1,0:T(8,128)(2,1)} %get-tuple-element.170), channel_id=1, source_target_pairs={{0,1},{1,0},{2,3},{3,2},{4,5},{5,4},{6,7},{7,6},{8,9},{9,8},{10,11... | collective-permute-start | bytes 3612680 | tf_op jit(solution)/shard_map/ppermute | solution.py:1145
  459.9 8.3 %copy-start.31 = (f32[4,16,32]{2,0,1:T(4,128)S(1)}, f32[4,16,32]{2,0,1:T(4,128)}, u32[]{:S(2)}) copy-start(f32[4,16,32]{2,0,1:T(4,128)} %copy.120) | copy-start | bytes 24580
  471.5 115.6 %copy-start.2 = (f32[64,1,6400]{2,1,0:T(1,128)S(1)}, f32[64,1,6400]{2,1,0:T(1,128)}, u32[]{:S(2)}) copy-start(f32[64,1,6400]{2,1,0:T(1,128)} %param.20) | copy-start | bytes 4915204
  471.5 115.6 %copy-start.5 = (f32[64,1,6400]{2,1,0:T(1,128)S(1)}, f32[64,1,6400]{2,1,0:T(1,128)}, u32[]{:S(2)}) copy-start(f32[64,1,6400]{2,1,0:T(1,128)} %param.21) | copy-start | bytes 4915204
  471.5 115.7 %copy-start.6 = (f32[64,1,6400]{2,1,0:T(1,128)S(1)}, f32[64,1,6400]{2,1,0:T(1,128)}, u32[]{:S(2)}) copy-start(f32[64,1,6400]{2,1,0:T(1,128)} %param.22) | copy-start | bytes 4915204
  471.5 115.7 %copy-start.9 = (bf16[64,2048]{1,0:T(8,128)(2,1)S(1)}, bf16[64,2048]{1,0:T(8,128)(2,1)}, u32[]{:S(2)}) copy-start(bf16[64,2048]{1,0:T(8,128)(2,1)} %reduce-scatter.2.cloned.1.call-done.refs_6_.down) | copy-start | bytes 786436
  471.5 115.7 %copy-start.13 = (f32[32,1,3072]{2,1,0:T(1,128)S(1)}, f32[32,1,3072]{2,1,0:T(1,128)}, u32[]{:S(2)}) copy-start(f32[32,1,3072]{2,1,0:T(1,128)} %param.24) | copy-start | bytes 1179652
  471.5 115.7 %copy-start.14 = (f32[32,1,3072]{2,1,0:T(1,128)S(1)}, f32[32,1,3072]{2,1,0:T(1,128)}, u32[]{:S(2)}) copy-start(f32[32,1,3072]{2,1,0:T(1,128)} %param.25) | copy-start | bytes 1179652
  471.5 115.7 %copy-start.21 = (f32[4,64]{1,0:T(4,128)S(1)}, f32[4,64]{1,0:T(4,128)}, u32[]{:S(2)}) copy-start(f32[4,64]{1,0:T(4,128)} %refs_7_.1) | copy-start | bytes 3076
  471.5 115.7 %copy-start.22 = (f32[4,64]{1,0:T(4,128)S(1)}, f32[4,64]{1,0:T(4,128)}, u32[]{:S(2)}) copy-start(f32[4,64]{1,0:T(4,128)} %refs_8_.1) | copy-start | bytes 3076
  471.5 115.7 %copy-start.23 = (f32[4,32]{1,0:T(4,128)S(1)}, f32[4,32]{1,0:T(4,128)}, u32[]{:S(2)}) copy-start(f32[4,32]{1,0:T(4,128)} %refs_10_.1) | copy-start | bytes 1540
  471.5 115.7 %copy-start.24 = (f32[4,32]{1,0:T(4,128)S(1)}, f32[4,32]{1,0:T(4,128)}, u32[]{:S(2)}) copy-start(f32[4,32]{1,0:T(4,128)} %refs_11_.1) | copy-start | bytes 1540
  587.2 1.2 copy-start.8
  588.5 1.0 copy-start.15
  589.5 0.7 copy-start.18
  590.1 0.7 copy-start.19
  (2 other events, 1.2 us)
Sparse Core Ops, SparseCore 0:
  112.9 74.7 all-gather.1
  378.2 93.2 reduce-scatter.1

commit v6 on v5

--- a/solution.py
+++ b/solution.py
@@ -23,8 +23,9 @@
 GATHER_ORDERS = ("hlxy", "hlyx", "hlxy", "hlyx", "yxhl")
 DEC_GATHER_ORDERS = ("xhly", "xyhl")
 DEC_SCATTER_ORDERS = ("ylhx", "ylhx")
-GATHER_AHEAD, GATHER_LAG = 4, (1, 3)
-SCATTER_AHEAD, SCATTER_LAG = 4, (2, 2, 2)
+PIECES, DEC_PIECES = (6, 2, 8, 1), 4
+GATHER_AHEAD, GATHER_LAG = 6, (3, 6)
+SCATTER_AHEAD, SCATTER_LAG = 6, (3, 3, 3)
 SCATTER_ORDERS = ("xylh", "yxlh", "xylh", "yxlh", "lhxy")
 
 MESH_ID = pl.DeviceIdType.MESH
@@ -1149,15 +1150,12 @@
     return lax.axis_size("section") == 2 and lax.axis_size("dp") == 8
 
 
-def plan(widths, pieces, dec_width, orders, dec_orders):
-    enc = chunk_list(widths, pieces, 0, orders)
-    dec = [
-        (len(widths), b, c, w, o, k)
-        for _, b, c, w, o, k in chunk_list((dec_width,), (4,), 1, dec_orders)
-    ]
-    for k, chunk in enumerate(dec):
-        enc.insert(3 * k + 2, chunk)
-    return enc
+def plan(widths, dec_width, orders, dec_orders, among):
+    chunks = chunk_list(widths, PIECES, 0, orders)
+    dec = chunk_list((dec_width,), (DEC_PIECES,), 1, dec_orders)
+    for k, (_, b, c, w, o, owner) in enumerate(dec):
+        chunks.insert(3 * k + 2 if among else len(chunks), (len(widths), b, c, w, o, owner))
+    return chunks
 
 
 def gather_all(low_enc, low_dec, norms, widths):
@@ -1175,7 +1173,7 @@
     columns = [sum(widths[:k]) for k in range(count + 1)]
     ahead = [low_enc[:, : columns[3]], low_enc[:, columns[4] :]]
     near = (*widths[:3], widths[4])
-    chunks = plan(near, (4, 1, 4, 2), low_dec.shape[1], GATHER_ORDERS, DEC_GATHER_ORDERS)
+    chunks = plan(near, low_dec.shape[1], GATHER_ORDERS, DEC_GATHER_ORDERS, False)
     outputs = [(low_enc.shape[0], w, LOW) for w in near]
     outputs += [(low_dec.shape[0], low_dec.shape[1], LOW), (8, 128, WIDE)]
     described = [(k // 4, k, c, b, w, o, own) for k, b, c, w, o, own in chunks]
@@ -1207,7 +1205,7 @@
     down = scattered(enc_parts[3])
     near = (*enc_parts[:3], enc_parts[4])
     near_widths = (*widths[:3], widths[4])
-    chunks = plan(near_widths, (4, 1, 4, 2), dec.shape[1], SCATTER_ORDERS, DEC_SCATTER_ORDERS)
+    chunks = plan(near_widths, dec.shape[1], SCATTER_ORDERS, DEC_SCATTER_ORDERS, True)
     described = [(k, k // 4, b, c, w, o, own) for k, b, c, w, o, own in chunks]
     described.append((5, 2, 0, 0, 128, "xylh", BOTH))
     rows = near[0].shape[0] // 16

time: 603 us -> 563 us (0.934)
  Pallas kernels: 453 us -> 408 us
    pallas_call x1, Pallas kernels: 114 us -> 96 us  [scatter_grads(): return call(*views, summed)]
    pallas_call x1, Pallas kernels: 97 us -> 82.8 us  [gather_weights(): results = call(*shards)]
    pallas_call x1, Pallas kernels: 84.7 us -> 71.3 us  [decoder_step(): pl.pallas_call(functools.partial(decoder_kernel, length), grid=(images //...]
  transfers between devices with their start and end apart: 14 -> 14, of which waited for: 9 -> 9; matrix products, arithmetic and copies ran while one was open for 9% -> 9% of each run, Pallas kernels for 17% -> 18%
where the time goes in v6:
time: 563 us; the launch traced here: 559 us
  Pallas kernels  408 us (72%)
  waiting for transfers between devices  56.5 us (10%)
  local copies, waits for them, and re-layouts  39.1 us (7%)
  other arithmetic  27.2 us (5%)
  between operations  17.3 us (3%)
  starting transfers between devices  6.64 us (1%)
    pallas_call x1, Pallas kernels, scatter_grads(): return call(*views, summed)  96 us
    pallas_call x1, Pallas kernels, gather_weights(): results = call(*shards)  82.8 us
    pallas_call x1, Pallas kernels, decoder_step(): pl.pallas_call(functools.partial(decoder_kernel, length), grid=(images //...  71.3 us
    pallas_call x1, Pallas kernels, encoder_attend_back(): pl.pallas_call(functools.partial(attend_back_kernel, head), in_specs=[pl....  48.8 us
    pallas_call x1, Pallas kernels, encoder_attend(): pl.pallas_call(functools.partial(attend_kernel, head), in_specs=[pl.Block...  34.9 us
    pallas_call x1, Pallas kernels, encoder_feed_back(): pl.pallas_call(feed_back_kernel, grid=(units // piece,), in_specs=[pl.Blo...  30.6 us
    ppermute x2, waiting for transfers between devices, from_behind(): return lax.ppermute(value, axis, pairs)  22.9 us
    pallas_call x1, Pallas kernels, encoder_feed(): pl.pallas_call(feed_kernel, grid=(rows // block,), in_specs=[wide, wide,...  20.5 us
  transfers between devices with their start and end apart: 14, of which 9 were waited for; matrix products, arithmetic and copies ran while one was open for 9% of the time, Pallas kernels for 18%

profile of v6, /device:TPU:0, one launch (start us, length us, event | category | flops | bytes accessed | tf_op | source)
XLA Modules:
  0.0 559.4 jit_solution(16119815188082940069)
XLA Ops:
  7.3 1.6 copy.118
  9.8 82.8 %shard_map.249 = (bf16[2,2,2,2,64,1536]{5,4,3,2,1,0:T(8,128)(2,1)S(1)}, bf16[2,2,2,2,64,512]{5,4,3,2,1,0:T(8,128)(2,1)S(1)}, bf16[2,2,2,2,64,2048]{5,4,3,2,1,0:T...) custom-call(bf16[64,4352]{1,0:T(8,128)(2,1)S(1)} %pad_maximum_fusion, ...), custom_call_target="tpu_custom_call" | custom-call | tf_op jit(solution)/shard_map/pallas_call | solution.py:162
  92.6 2.0 copy-done
  94.6 1.6 copy-done.1
  96.2 1.0 copy-done.3
  98.7 1.6 slice_reduce_fusion
  102.1 1.1 broadcast_in_dim.72.slots_column
  105.0 0.8 slice.89
  107.0 1.4 reshape.183.gains.refs_5_
  108.5 3.6 maximum_select_fusion
  112.1 1.7 pad.37.stream
  113.7 34.9 %shard_map.250 = (bf16[1200,1024]{1,0:T(8,128)(2,1)}, bf16[1536,1280]{1,0:T(8,128)(2,1)}, bf16[512,1280]{1,0:T(8,128)(2,1)}, f32[8,1280]{1,0:T(8,128)}, bf16[1200,1024]{1,0:T(8,128)(2,1)}) custom-call(s32[5,2]{1,0:T(8,128)} %copy.97.bounds, bf16[1200,1024]{1,0:T(8,128)(2,1)} %pad.37.stream, s32[1,1280]{1,0:T(1,128)} %broadcast_in_dim.62.slots_row, ...), custom_call_target="tpu_custom_call" | custom-call | tf_op jit(solution)/shard_map/pallas_call | solution.py:797
  149.0 2.5 reshape_squeeze.3
  151.5 2.5 pad.40.cotangent
  154.6 1.4 reshape.184.gains
  156.1 1.8 pad.41.position
  157.8 1.3 fusion.12
  159.2 16.2 %all-gather.2.cloned.1.call-done.down_w = bf16[1024,2048]{1,0:T(8,128)(2,1)} async-done(((bf16[64,2048]{1,0:T(8,128)(2,1)}), bf16[1024,2048]{1,0:T(8,128)(2,1)}) %all-gather.2.cloned.1.call-update) | async-done | bytes 4194320 | tf_op jit(solution)/shard_map/all_gather | solution.py:1186
  175.4 20.5 %shard_map.251 = (f32[1200,1024]{1,0:T(8,128)}, bf16[1200,1024]{1,0:T(8,128)(2,1)}, bf16[1200,2048]{1,0:T(8,128)(2,1)}, bf16[1200,2048]{1,0:T(8,128)(2,1)}, bf16[1200,1024]{1,0:T(8,128)(2,1)}) custom-call(bf16[1200,1024]{1,0:T(8,128)(2,1)} %pad.37.stream, bf16[1200,1024]{1,0:T(8,128)(2,1)} %get-tuple-element.70.own, ...), custom_call_target="tpu_custom_call" | custom-call | tf_op jit(solution)/shard_map/pallas_call | solution.py:973
  196.4 7.1 %collective-permute-done.2 = bf16[1200,1024]{1,0:T(8,128)(2,1)S(1)} collective-permute-done((bf16[1200,1024]{1,0:T(8,128)(2,1)}, bf16[1200,1024]{1,0:T(8,128)(2,1)S(1)}, u32[]{:S(2)}, u32[]{:S(2)}) %collective-permute-start.2) | collective-permute-done | bytes 2457632 | tf_op jit(solution)/shard_map/ppermute | solution.py:1146
  203.5 4.7 add_convert_fusion.1
  209.7 3.4 collective-permute-start.3
  213.1 9.9 %collective-permute-done.3 = bf16[880,256]{1,0:T(8,128)(2,1)S(1)} collective-permute-done((bf16[880,256]{1,0:T(8,128)(2,1)S(1)}, bf16[880,256]{1,0:T(8,128)(2,1)S(1)}, u32[]{:S(2)}, u32[]{:S(2)}) %collective-permute-start.3) | collective-permute-done | bytes 450592 | tf_op jit(solution)/shard_map/ppermute | solution.py:1141
  224.3 1.0 broadcast_in_dim.71.target_column
  225.9 71.3 %shard_map.252 = (f32[6,208,512]{2,1,0:T(8,128)}, bf16[896,256]{1,0:T(8,128)(2,1)}, bf16[896,256]{1,0:T(8,128)(2,1)}, bf16[512,3072]{1,0:T(8,128)(2,1)}, bf16[512,3072]{1,0:T(8,128)(2,1)}, /*index=5*/f32[8,512]{1,0:T(8,128)}) custom-call(s32[1]{0:T(128)} %bitcast.16.flag, s32[1,896]{1,0:T(1,128)} %broadcast_in_dim.65.target_row, ...), custom_call_target="tpu_custom_call" | custom-call | tf_op jit(solution)/shard_map/pallas_call | solution.py:655
  297.2 1.1 slice.77
  298.5 1.7 collective-permute-done.6
  300.2 1.1 slice_add_fusion
  301.3 1.3 collective-permute-start.7
  302.6 13.1 %collective-permute-done.7 = bf16[880,256]{1,0:T(8,128)(2,1)S(1)} collective-permute-done((bf16[880,256]{1,0:T(8,128)(2,1)S(1)}, bf16[880,256]{1,0:T(8,128)(2,1)S(1)}, u32[]{:S(2)}, u32[]{:S(2)}) %collective-permute-start.7) | collective-permute-done | bytes 450592 | tf_op jit(solution)/shard_map/ppermute | solution.py:1141
  316.6 4.8 collective-permute-done.8.other.refs_4_
  321.4 30.6 %shard_map.253 = (bf16[1024,2048]{1,0:T(8,128)(2,1)}, bf16[1024,2048]{1,0:T(8,128)(2,1)}, bf16[1200,1024]{1,0:T(8,128)(2,1)}) custom-call(s32[1]{0:T(128)} %bitcast.15.counts, bf16[1200,1024]{1,0:T(8,128)(2,1)} %copy-done.25, bf16[1200,1024]{1,0:T(8,128)(2,1)} %collective-permute-done.8.other.refs_4_, bf16[1200,1024]{1,0:T(8,128)(2,1)} %get-tuple-element.84.second, ...), custom_call_target="tpu_custom_call" | custom-call | tf_op jit(solution)/shard_map/pallas_call | solution.py:1031
  353.5 1.3 slice_select_fusion.1
  354.8 1.4 reshape.169
  356.2 1.4 copy.120
  357.6 3.5 convolution_convert_fusion.1
  361.7 11.3 %shard_map.254 = (f32[1200,1024]{1,0:T(8,128)}, bf16[1200,1024]{1,0:T(8,128)(2,1)}, f32[8,1024]{1,0:T(8,128)}) custom-call(f32[1200,1024]{1,0:T(8,128)} %get-tuple-element.74.refs_0_, bf16[1200,1024]{1,0:T(8,128)(2,1)} %get-tuple-element.87.refs_1_, bf16[1200,1024]{1,0:T(8,128)(2,1)} %collective-permute-done.9.refs_2_, bf16[1200,1024]{1,0:T(8,128)(2,1)} %copy-done.25, ...), custom_call_target="tpu_custom_call" | custom-call | tf_op jit(solution)/shard_map/pallas_call | solution.py:1087
  373.0 48.8 %shard_map.255 = (bf16[1024,1536]{1,0:T(8,128)(2,1)}, bf16[1024,512]{1,0:T(8,128)(2,1)}, bf16[1200,1024]{1,0:T(8,128)(2,1)}) custom-call(s32[5,2]{1,0:T(8,128)} %copy.97.bounds, s32[1,1280]{1,0:T(1,128)} %broadcast_in_dim.62.slots_row, s32[1280,1]{1,0:T(8,128)} %broadcast_in_dim.72.slots_column, bf16[1200,1024]{1,0:T(8,128)(2,1)} %get-tuple-element.66.first, ...), custom_call_target="tpu_custom_call" | custom-call | tf_op jit(solution)/shard_map/pallas_call | solution.py:923
  421.8 3.6 broadcast_select_fusion
  425.6 2.9 add_convert_fusion
  429.3 4.7 slice_select_fusion.skip
  434.0 7.4 %shard_map.256 = (f32[4704,128]{1,0:T(8,128)}, f32[8,1024]{1,0:T(8,128)}) custom-call(s32[1]{0:T(128)} %bitcast.flag, bf16[588,1024]{1,0:T(8,128)(2,1)} %bitcast.76, bf16[588,1024]{1,0:T(8,128)(2,1)} %get-tuple-element.171.own, bf16[588,1024]{1,0:T(8,128)(2,1)} %collective-permute-done.10.other, f32[588,1024]{1,0:T(8,128)} %slice_select_fusion.skip, ...), custom_call_target="tpu_custom_call" | custom-call | tf_op jit(solution)/shard_map/pallas_call | solution.py:1125
  443.0 2.4 reduce-scatter.2.cloned.1.call-done.refs_6_.down
  445.5 96.0 %shard_map.257 = (f32[64,4352]{1,0:T(8,128)}, f32[32,3072]{1,0:T(8,128)}, f32[8,128]{1,0:T(8,128)}, f32[8,128]{1,0:T(8,128)}) custom-call(bf16[2,2,2,2,64,1536]{5,4,3,2,1,0:T(8,128)(2,1)} %bitcast.81, bf16[2,2,2,2,64,512]{5,4,3,2,1,0:T(8,128)(2,1)} %bitcast.82, bf16[2,2,2,2,64,2048]{5,4,3,2,1,0:T(8,128)(2,1)} %bitcast.77, ...), custom_call_target="tpu_custom_call" | custom-call | tf_op jit(solution)/shard_map/pallas_call | solution.py:409
  541.5 1.2 slice.85
  543.4 1.2 copy-done.8
  544.7 1.0 copy-done.15
  547.0 4.1 shard_map.258
  (118 shorter events, 18.8 us)
Async XLA Ops:
  7.2 2.4 copy-start.7
  7.2 2.5 copy-start.17
  7.2 2.5 copy-start.16
  7.2 168.2 %all-gather.2.cloned.1.call-start = ((), (), s32[]{:S(2)}) async-start(), calls=%async_computation.1 | async-start | bytes 4456448 | tf_op jit(solution)/shard_map/all_gather | solution.py:1186
  92.6 2.0 copy-start
  94.6 1.6 copy-start.1
  96.2 1.0 copy-start.3
  97.2 0.8 copy-start.10
  98.0 0.6 copy-start.20
  98.6 97.3 %copy-start.4 = (bf16[2,2,2,2,32,3072]{5,4,3,2,1,0:T(8,128)(2,1)}, bf16[2,2,2,2,32,3072]{5,4,3,2,1,0:T(8,128)(2,1)S(1)}, u32[]{:S(2)}) copy-start(bf16[2,2,2,2,32,3072]{5,4,3,2,1,0:T(8,128)(2,1)S(1)} %get-tuple-element.80) | copy-start | bytes 9437188
  98.6 346.8 %reduce-scatter.2.cloned.1.call-start = ((), (), s32[]{:S(2)}) async-start(), calls=%async_computation.2 | async-start | bytes 4456448 | tf_op jit(solution)/shard_map/reduce_scatter | solution.py:1195
  98.7 9.8 %collective-permute-start = (bf16[588,1024]{1,0:T(8,128)(2,1)}, bf16[588,1024]{1,0:T(8,128)(2,1)}, u32[]{:S(2)}, u32[]{:S(2)}) collective-permute-start(bf16[588,1024]{1,0:T(8,128)(2,1)} %bitcast.74), channel_id=1, source_target_pairs={{0,1},{1,0},{2,3},{3,2},{4,5},{5,4},{6,7},{7,6},{8,9},{9,8},{10,11... | collective-permute-start | bytes 3612680 | tf_op jit(solution)/shard_map/ppermute | solution.py:1146
  148.6 9.2 %copy-start.33 = (s32[1176]{0:T(1024)S(1)}, s32[1176]{0:T(1024)}, u32[]{:S(2)}) copy-start(s32[1176]{0:T(1024)} %copy-done.32) | copy-start | bytes 14116
  148.6 10.5 %collective-permute-start.1 = (bf16[1200,1024]{1,0:T(8,128)(2,1)}, bf16[1200,1024]{1,0:T(8,128)(2,1)}, u32[]{:S(2)}, u32[]{:S(2)}) collective-permute-start(bf16[1200,1024]{1,0:T(8,128)(2,1)} %get-tuple-element.70.own), channel_id=1, source_target_pairs={{0,1},{1,0},{2,3},{3,2},{4,5},{5,4},{6,7},{7,6},{8,9},{9,8},{10,11... | collective-permute-start | bytes 7372808 | tf_op jit(solution)/shard_map/ppermute | solution.py:1146
  151.5 2.5 copy-start.30
  195.9 7.6 %collective-permute-start.2 = (bf16[1200,1024]{1,0:T(8,128)(2,1)}, bf16[1200,1024]{1,0:T(8,128)(2,1)S(1)}, u32[]{:S(2)}, u32[]{:S(2)}) collective-permute-start(bf16[1200,1024]{1,0:T(8,128)(2,1)} %get-tuple-element.76), channel_id=1, source_target_pairs={{0,1},{1,0},{2,3},{3,2},{4,5},{5,4},{6,7},{7,6},{8,9},{9,8},{10,11... | collective-permute-start | bytes 7372808 | tf_op jit(solution)/shard_map/ppermute | solution.py:1146
  195.9 29.3 %collective-permute-start.5 = (bf16[512,3072]{1,0:T(8,128)(2,1)S(1)}, bf16[512,3072]{1,0:T(8,128)(2,1)}, u32[]{:S(2)}, u32[]{:S(2)}) collective-permute-start(bf16[512,3072]{1,0:T(8,128)(2,1)S(1)} %bitcast.60), channel_id=1, source_target_pairs={{0,1},{1,0},{2,3},{3,2},{4,5},{5,4},{6,7},{7,6},{8,9},{9,8},{10,11... | collective-permute-start | bytes 9437192 | tf_op jit(solution)/shard_map/ppermute | solution.py:1146
  203.5 4.7 copy-start.11
  208.2 1.5 copy-start.27
  208.2 15.5 %copy-start.34 = (s32[896]{0:T(1024)S(1)}, s32[896]{0:T(1024)}, u32[]{:S(2)}) copy-start(s32[896]{0:T(1024)} %fusion.12) | copy-start | bytes 10756
  209.7 13.2 %collective-permute-start.3 = (bf16[880,256]{1,0:T(8,128)(2,1)S(1)}, bf16[880,256]{1,0:T(8,128)(2,1)S(1)}, u32[]{:S(2)}, u32[]{:S(2)}) collective-permute-start(bf16[880,256]{1,0:T(8,128)(2,1)S(1)} %fusion.2), channel_id=1, source_target_pairs={{0,16},{1,17},{2,18},{3,19},{4,20},{5,21},{6,22},{7,23},{8,24},{9,... | collective-permute-start | bytes 1351688 | tf_op jit(solution)/shard_map/ppermute | solution.py:1141
  223.7 2.2 collective-permute-start.4
  297.2 18.5 %copy-start.12 = (bf16[2,2,2,2,64,256]{5,4,3,2,1,0:T(8,128)(2,1)S(1)}, bf16[2,2,2,2,64,256]{5,4,3,2,1,0:T(8,128)(2,1)}, u32[]{:S(2)}) copy-start(bf16[2,2,2,2,64,256]{5,4,3,2,1,0:T(8,128)(2,1)} %copy-done.10) | copy-start | bytes 1572868
  298.3 1.9 collective-permute-start.6
  301.3 14.4 %collective-permute-start.7 = (bf16[880,256]{1,0:T(8,128)(2,1)S(1)}, bf16[880,256]{1,0:T(8,128)(2,1)S(1)}, u32[]{:S(2)}, u32[]{:S(2)}) collective-permute-start(bf16[880,256]{1,0:T(8,128)(2,1)S(1)} %slice_add_fusion), channel_id=1, source_target_pairs={{16,0},{17,1},{18,2},{19,3},{20,4},{21,5},{22,6},{23,7},{24,8},{25... | collective-permute-start | bytes 1351688 | tf_op jit(solution)/shard_map/ppermute | solution.py:1141
  315.7 0.8 copy-start.28
  316.5 4.9 copy-start.25
  316.6 4.9 collective-permute-start.8
  352.1 1.4 copy-start.35
  352.1 73.4 %collective-permute-start.11 = (bf16[512,3072]{1,0:T(8,128)(2,1)}, bf16[512,3072]{1,0:T(8,128)(2,1)S(1)}, u32[]{:S(2)}, u32[]{:S(2)}) collective-permute-start(bf16[512,3072]{1,0:T(8,128)(2,1)} %get-tuple-element.97), channel_id=1, source_target_pairs={{0,1},{1,0},{2,3},{3,2},{4,5},{5,4},{6,7},{7,6},{8,9},{9,8},{10,11... | collective-permute-start | bytes 9437192 | tf_op jit(solution)/shard_map/ppermute | solution.py:1146
  352.3 9.4 %collective-permute-start.9 = (bf16[1200,1024]{1,0:T(8,128)(2,1)}, bf16[1200,1024]{1,0:T(8,128)(2,1)}, u32[]{:S(2)}, u32[]{:S(2)}) collective-permute-start(bf16[1200,1024]{1,0:T(8,128)(2,1)} %get-tuple-element.87.refs_1_), channel_id=1, source_target_pairs={{0,1},{1,0},{2,3},{3,2},{4,5},{5,4},{6,7},{7,6},{8,9},{9,8},{10,11... | collective-permute-start | bytes 7372808 | tf_op jit(solution)/shard_map/ppermute | solution.py:1146
  421.8 3.8 copy-start.26
  425.4 8.6 %collective-permute-start.10 = (bf16[588,1024]{1,0:T(8,128)(2,1)}, bf16[588,1024]{1,0:T(8,128)(2,1)}, u32[]{:S(2)}, u32[]{:S(2)}) collective-permute-start(bf16[588,1024]{1,0:T(8,128)(2,1)} %get-tuple-element.170), channel_id=1, source_target_pairs={{0,1},{1,0},{2,3},{3,2},{4,5},{5,4},{6,7},{7,6},{8,9},{9,8},{10,11... | collective-permute-start | bytes 3612680 | tf_op jit(solution)/shard_map/ppermute | solution.py:1146
  434.0 8.3 %copy-start.31 = (f32[4,16,32]{2,0,1:T(4,128)S(1)}, f32[4,16,32]{2,0,1:T(4,128)}, u32[]{:S(2)}) copy-start(f32[4,16,32]{2,0,1:T(4,128)} %copy.120) | copy-start | bytes 24580
  445.4 97.9 %copy-start.2 = (f32[64,1,6400]{2,1,0:T(1,128)S(1)}, f32[64,1,6400]{2,1,0:T(1,128)}, u32[]{:S(2)}) copy-start(f32[64,1,6400]{2,1,0:T(1,128)} %param.20) | copy-start | bytes 4915204
  445.4 97.9 %copy-start.5 = (f32[64,1,6400]{2,1,0:T(1,128)S(1)}, f32[64,1,6400]{2,1,0:T(1,128)}, u32[]{:S(2)}) copy-start(f32[64,1,6400]{2,1,0:T(1,128)} %param.21) | copy-start | bytes 4915204
  445.4 97.9 %copy-start.6 = (f32[64,1,6400]{2,1,0:T(1,128)S(1)}, f32[64,1,6400]{2,1,0:T(1,128)}, u32[]{:S(2)}) copy-start(f32[64,1,6400]{2,1,0:T(1,128)} %param.22) | copy-start | bytes 4915204
  445.4 97.9 %copy-start.9 = (bf16[64,2048]{1,0:T(8,128)(2,1)S(1)}, bf16[64,2048]{1,0:T(8,128)(2,1)}, u32[]{:S(2)}) copy-start(bf16[64,2048]{1,0:T(8,128)(2,1)} %reduce-scatter.2.cloned.1.call-done.refs_6_.down) | copy-start | bytes 786436
  445.4 97.9 %copy-start.13 = (f32[32,1,3072]{2,1,0:T(1,128)S(1)}, f32[32,1,3072]{2,1,0:T(1,128)}, u32[]{:S(2)}) copy-start(f32[32,1,3072]{2,1,0:T(1,128)} %param.24) | copy-start | bytes 1179652
  445.4 98.0 %copy-start.14 = (f32[32,1,3072]{2,1,0:T(1,128)S(1)}, f32[32,1,3072]{2,1,0:T(1,128)}, u32[]{:S(2)}) copy-start(f32[32,1,3072]{2,1,0:T(1,128)} %param.25) | copy-start | bytes 1179652
  445.4 97.9 %copy-start.21 = (f32[4,64]{1,0:T(4,128)S(1)}, f32[4,64]{1,0:T(4,128)}, u32[]{:S(2)}) copy-start(f32[4,64]{1,0:T(4,128)} %refs_7_.1) | copy-start | bytes 3076
  445.5 97.9 %copy-start.22 = (f32[4,64]{1,0:T(4,128)S(1)}, f32[4,64]{1,0:T(4,128)}, u32[]{:S(2)}) copy-start(f32[4,64]{1,0:T(4,128)} %refs_8_.1) | copy-start | bytes 3076
  445.5 97.9 %copy-start.23 = (f32[4,32]{1,0:T(4,128)S(1)}, f32[4,32]{1,0:T(4,128)}, u32[]{:S(2)}) copy-start(f32[4,32]{1,0:T(4,128)} %refs_10_.1) | copy-start | bytes 1540
  445.5 97.9 %copy-start.24 = (f32[4,32]{1,0:T(4,128)S(1)}, f32[4,32]{1,0:T(4,128)}, u32[]{:S(2)}) copy-start(f32[4,32]{1,0:T(4,128)} %refs_11_.1) | copy-start | bytes 1540
  543.4 1.2 copy-start.8
  544.7 1.0 copy-start.15
  545.7 0.7 copy-start.18
  546.4 0.7 copy-start.19
  (2 other events, 1.2 us)
Sparse Core Ops, SparseCore 0:
  98.7 76.6 all-gather.1
  352.2 93.1 reduce-scatter.1

commit v7 on v6

--- a/solution.py
+++ b/solution.py
@@ -32,6 +32,9 @@
 EVERY = slice(None)
 BOTH = -1
 DIMS = "xhly"
+NEAR_WAYS = ("x", "y", "c", "xy", "xc", "yc", "xyc")
+LINE_WAYS = ("h", "l", "hl")
+FAR = ("c", "xy", "xc", "yc", "xyc", "hl")
 
 
 class Place:
@@ -45,16 +48,24 @@
             "h": (s, depth + 4 - 8 * high, core),
             "l": (s, depth + 2 - 4 * low, core),
             "y": (s, depth + 1 - 2 * y, core),
-            "c": (s, depth, 1 - core),
         }
 
-    def greet(self):
+    def across(self, flips):
+        other = {d: 1 - self.at[d] if d in flips else self.at[d] for d in DIMS}
+        core = 1 - self.core if "c" in flips else self.core
+        return other["x"], 4 * other["h"] + 2 * other["l"] + other["y"], core
+
+    def greet(self, more=()):
         barrier = pltpu.get_barrier_semaphore()
+        for flips in more:
+            pl.semaphore_signal(
+                barrier, inc=1, device_id=self.across(flips), device_id_type=MESH_ID
+            )
         for name in self.device:
             pl.semaphore_signal(
                 barrier, inc=1, device_id=self.device[name], device_id_type=MESH_ID
             )
-        pl.semaphore_wait(barrier, len(self.device))
+        pl.semaphore_wait(barrier, len(self.device) + len(more))
 
 
 def run(condition, action):
@@ -317,13 +328,13 @@
 
         run(roles(i, stage)[1], add)
 
-    here.greet()
+    here.greet(FAR)
     join = pltpu.make_async_remote_copy(
         src_ref=given,
         dst_ref=last_there,
-        send_sem=square_send.at[5],
-        recv_sem=square_recv.at[5],
-        device_id=here.device["c"],
+        send_sem=square_send.at[11],
+        recv_sem=square_recv.at[11],
+        device_id=here.across("c"),
         device_id_type=MESH_ID,
     )
     join.start()
@@ -358,19 +369,49 @@
     for k, out in enumerate(outs):
         value = value + squares(out) * (1.0 / cores if k == n_out - 1 else 1.0)
     value = jnp.broadcast_to(jnp.sum(value, keepdims=True), (8, 128))
-    for k, axis in enumerate("cyxlh"):
-        square_mine[k] = value
-        move = pltpu.make_async_remote_copy(
-            src_ref=square_mine.at[k],
-            dst_ref=square_there.at[k],
-            send_sem=square_send.at[k],
-            recv_sem=square_recv.at[k],
-            device_id=here.device[axis],
-            device_id_type=MESH_ID,
-        )
-        move.start()
-        move.wait()
-        value = value + square_there[k]
+    begin = 0
+    for bits, ways in (("xyc", NEAR_WAYS), ("hl", LINE_WAYS)):
+        names = {**here.at, "c": here.core}
+
+        def number(flips):
+            total = 0
+            for bit in bits:
+                total = 2 * total + (1 - names[bit] if bit in flips else names[bit])
+            return total
+
+        mine = square_mine.at[0 if begin == 0 else 1]
+        mine[...] = value
+        moves = []
+        for k, flips in enumerate(ways):
+            moves.append(
+                pltpu.make_async_remote_copy(
+                    src_ref=mine,
+                    dst_ref=square_there.at[begin + number("")],
+                    send_sem=square_send.at[begin + k],
+                    recv_sem=square_recv.at[begin + k],
+                    device_id=here.across(flips),
+                    device_id_type=MESH_ID,
+                )
+            )
+            moves[-1].start()
+        square_there[begin + number("")] = value
+        for k, flips in enumerate(ways):
+            moves[k].wait_send()
+            slot = square_there.at[begin + number(flips)]
+            pltpu.make_async_remote_copy(
+                src_ref=slot,
+                dst_ref=slot,
+                send_sem=square_send.at[begin + k],
+                recv_sem=square_recv.at[begin + k],
+                device_id=here.across(flips),
+                device_id_type=MESH_ID,
+            ).wait_recv()
+        value = square_there[begin]
+        for k in range(1, len(ways) + 1):
+            value = value + square_there[begin + k]
+        begin += len(ways)
+        if begin == 7:
+            begin = 8
     square_total[...] = value
 
 
@@ -394,10 +435,10 @@
             pltpu.SemaphoreType.DMA((count, 4)),
             pltpu.SemaphoreType.DMA((count, 4)),
             pltpu.SemaphoreType.DMA((count,)),
-            pltpu.SemaphoreType.DMA((6,)),
-            pltpu.SemaphoreType.DMA((6,)),
-            pltpu.VMEM((5, 8, 128), jnp.float32),
-            pltpu.VMEM((5, 8, 128), jnp.float32),
+            pltpu.SemaphoreType.DMA((12,)),
+            pltpu.SemaphoreType.DMA((12,)),
+            pltpu.VMEM((2, 8, 128), jnp.float32),
+            pltpu.VMEM((12, 8, 128), jnp.float32),
             pltpu.VMEM(views[-1].shape, views[-1].dtype),
             pltpu.VMEM(views[-1].shape, views[-1].dtype),
             *buffers,

time: 563 us -> 565 us (level)
  Pallas kernels: 408 us -> 417 us
  waiting for transfers between devices: 56.5 us -> 48.5 us
    pallas_call x1, Pallas kernels: 48.8 us -> 56.5 us  [encoder_attend_back(): pl.pallas_call(functools.partial(attend_back_kernel, head), in_specs=[pl....]
    pallas_call x1, Pallas kernels: 34.9 us -> 40.6 us  [encoder_attend(): pl.pallas_call(functools.partial(attend_kernel, head), in_specs=[pl.Block...]
  transfers between devices with their start and end apart: 14 -> 14, of which waited for: 9 -> 8; matrix products, arithmetic and copies ran while one was open for 9% -> 9% of each run, Pallas kernels for 18% -> 21%
where the time goes in v7:
time: 565 us; the launch traced here: 561 us
  Pallas kernels  417 us (74%)
  waiting for transfers between devices  48.5 us (9%)
  local copies, waits for them, and re-layouts  39.1 us (7%)
  other arithmetic  27.2 us (5%)
  between operations  17.3 us (3%)
  starting transfers between devices  6.64 us (1%)
    pallas_call x1, Pallas kernels, scatter_grads(): return call(*views, summed)  92 us
    pallas_call x1, Pallas kernels, gather_weights(): results = call(*shards)  82.8 us
    pallas_call x1, Pallas kernels, decoder_step(): pl.pallas_call(functools.partial(decoder_kernel, length), grid=(images //...  71.3 us
    pallas_call x1, Pallas kernels, encoder_attend_back(): pl.pallas_call(functools.partial(attend_back_kernel, head), in_specs=[pl....  56.5 us
    pallas_call x1, Pallas kernels, encoder_attend(): pl.pallas_call(functools.partial(attend_kernel, head), in_specs=[pl.Block...  40.6 us
    pallas_call x1, Pallas kernels, encoder_feed_back(): pl.pallas_call(feed_back_kernel, grid=(units // piece,), in_specs=[pl.Blo...  30.6 us
    ppermute x2, waiting for transfers between devices, from_behind(): return lax.ppermute(value, axis, pairs)  22.9 us
    pallas_call x1, Pallas kernels, encoder_feed(): pl.pallas_call(feed_kernel, grid=(rows // block,), in_specs=[wide, wide,...  20.5 us
  transfers between devices with their start and end apart: 14, of which 8 were waited for; matrix products, arithmetic and copies ran while one was open for 9% of the time, Pallas kernels for 21%

profile of v7, /device:TPU:0, one launch (start us, length us, event | category | flops | bytes accessed | tf_op | source)
XLA Modules:
  0.0 561.1 jit_solution(10661791058846405226)
XLA Ops:
  7.3 1.6 copy.118
  9.8 82.8 %shard_map.249 = (bf16[2,2,2,2,64,1536]{5,4,3,2,1,0:T(8,128)(2,1)S(1)}, bf16[2,2,2,2,64,512]{5,4,3,2,1,0:T(8,128)(2,1)S(1)}, bf16[2,2,2,2,64,2048]{5,4,3,2,1,0:T...) custom-call(bf16[64,4352]{1,0:T(8,128)(2,1)S(1)} %pad_maximum_fusion, ...), custom_call_target="tpu_custom_call" | custom-call | tf_op jit(solution)/shard_map/pallas_call | solution.py:173
  92.6 2.0 copy-done
  94.6 1.6 copy-done.1
  96.2 1.0 copy-done.3
  98.7 1.6 slice_reduce_fusion
  102.1 1.1 broadcast_in_dim.72.slots_column
  103.2 0.8 fusion.16
  105.0 0.8 slice.89
  107.0 1.4 reshape.183.gains.refs_5_
  108.5 3.6 maximum_select_fusion
  112.1 1.7 pad.37.stream
  113.7 40.6 %shard_map.250 = (bf16[1200,1024]{1,0:T(8,128)(2,1)}, bf16[1536,1280]{1,0:T(8,128)(2,1)}, bf16[512,1280]{1,0:T(8,128)(2,1)}, f32[8,1280]{1,0:T(8,128)}, bf16[1200,1024]{1,0:T(8,128)(2,1)}) custom-call(s32[5,2]{1,0:T(8,128)} %copy.97.bounds, bf16[1200,1024]{1,0:T(8,128)(2,1)} %pad.37.stream, s32[1,1280]{1,0:T(1,128)} %broadcast_in_dim.62.slots_row, ...), custom_call_target="tpu_custom_call" | custom-call | tf_op jit(solution)/shard_map/pallas_call | solution.py:838
  154.6 2.5 reshape_squeeze.3
  157.1 2.5 pad.40.cotangent
  160.3 1.4 reshape.184.gains
  161.7 1.8 pad.41.position
  163.5 1.3 fusion.12
  164.8 10.7 %all-gather.2.cloned.1.call-done.down_w = bf16[1024,2048]{1,0:T(8,128)(2,1)} async-done(((bf16[64,2048]{1,0:T(8,128)(2,1)}), bf16[1024,2048]{1,0:T(8,128)(2,1)}) %all-gather.2.cloned.1.call-update) | async-done | bytes 4194320 | tf_op jit(solution)/shard_map/all_gather | solution.py:1227
  175.5 20.5 %shard_map.251 = (f32[1200,1024]{1,0:T(8,128)}, bf16[1200,1024]{1,0:T(8,128)(2,1)}, bf16[1200,2048]{1,0:T(8,128)(2,1)}, bf16[1200,2048]{1,0:T(8,128)(2,1)}, bf16[1200,1024]{1,0:T(8,128)(2,1)}) custom-call(bf16[1200,1024]{1,0:T(8,128)(2,1)} %pad.37.stream, bf16[1200,1024]{1,0:T(8,128)(2,1)} %get-tuple-element.70.own, ...), custom_call_target="tpu_custom_call" | custom-call | tf_op jit(solution)/shard_map/pallas_call | solution.py:1014
  196.6 7.1 %collective-permute-done.2 = bf16[1200,1024]{1,0:T(8,128)(2,1)S(1)} collective-permute-done((bf16[1200,1024]{1,0:T(8,128)(2,1)}, bf16[1200,1024]{1,0:T(8,128)(2,1)S(1)}, u32[]{:S(2)}, u32[]{:S(2)}) %collective-permute-start.2) | collective-permute-done | bytes 2457632 | tf_op jit(solution)/shard_map/ppermute | solution.py:1187
  203.7 4.7 add_convert_fusion.1
  209.8 3.4 collective-permute-start.3
  213.2 9.9 %collective-permute-done.3 = bf16[880,256]{1,0:T(8,128)(2,1)S(1)} collective-permute-done((bf16[880,256]{1,0:T(8,128)(2,1)S(1)}, bf16[880,256]{1,0:T(8,128)(2,1)S(1)}, u32[]{:S(2)}, u32[]{:S(2)}) %collective-permute-start.3) | collective-permute-done | bytes 450592 | tf_op jit(solution)/shard_map/ppermute | solution.py:1182
  224.5 1.0 broadcast_in_dim.71.target_column
  226.0 71.3 %shard_map.252 = (f32[6,208,512]{2,1,0:T(8,128)}, bf16[896,256]{1,0:T(8,128)(2,1)}, bf16[896,256]{1,0:T(8,128)(2,1)}, bf16[512,3072]{1,0:T(8,128)(2,1)}, bf16[512,3072]{1,0:T(8,128)(2,1)}, /*index=5*/f32[8,512]{1,0:T(8,128)}) custom-call(s32[1]{0:T(128)} %bitcast.16.flag, s32[1,896]{1,0:T(1,128)} %broadcast_in_dim.65.target_row, ...), custom_call_target="tpu_custom_call" | custom-call | tf_op jit(solution)/shard_map/pallas_call | solution.py:696
  297.4 1.1 slice.77
  298.7 1.7 collective-permute-done.6
  300.4 1.1 slice_add_fusion
  301.5 1.3 collective-permute-start.7
  302.8 13.1 %collective-permute-done.7 = bf16[880,256]{1,0:T(8,128)(2,1)S(1)} collective-permute-done((bf16[880,256]{1,0:T(8,128)(2,1)S(1)}, bf16[880,256]{1,0:T(8,128)(2,1)S(1)}, u32[]{:S(2)}, u32[]{:S(2)}) %collective-permute-start.7) | collective-permute-done | bytes 450592 | tf_op jit(solution)/shard_map/ppermute | solution.py:1182
  316.8 4.8 collective-permute-done.8.other.refs_4_
  321.6 30.6 %shard_map.253 = (bf16[1024,2048]{1,0:T(8,128)(2,1)}, bf16[1024,2048]{1,0:T(8,128)(2,1)}, bf16[1200,1024]{1,0:T(8,128)(2,1)}) custom-call(s32[1]{0:T(128)} %bitcast.15.counts, bf16[1200,1024]{1,0:T(8,128)(2,1)} %copy-done.25, bf16[1200,1024]{1,0:T(8,128)(2,1)} %collective-permute-done.8.other.refs_4_, bf16[1200,1024]{1,0:T(8,128)(2,1)} %get-tuple-element.84.second, ...), custom_call_target="tpu_custom_call" | custom-call | tf_op jit(solution)/shard_map/pallas_call | solution.py:1072
  353.7 1.3 slice_select_fusion.1
  355.0 1.4 reshape.169
  356.4 1.4 copy.120
  357.7 3.5 convolution_convert_fusion.1
  361.8 11.4 %shard_map.254 = (f32[1200,1024]{1,0:T(8,128)}, bf16[1200,1024]{1,0:T(8,128)(2,1)}, f32[8,1024]{1,0:T(8,128)}) custom-call(f32[1200,1024]{1,0:T(8,128)} %get-tuple-element.74.refs_0_, bf16[1200,1024]{1,0:T(8,128)(2,1)} %get-tuple-element.87.refs_1_, bf16[1200,1024]{1,0:T(8,128)(2,1)} %collective-permute-done.9.refs_2_, bf16[1200,1024]{1,0:T(8,128)(2,1)} %copy-done.25, ...), custom_call_target="tpu_custom_call" | custom-call | tf_op jit(solution)/shard_map/pallas_call | solution.py:1128
  373.2 56.5 %shard_map.255 = (bf16[1024,1536]{1,0:T(8,128)(2,1)}, bf16[1024,512]{1,0:T(8,128)(2,1)}, bf16[1200,1024]{1,0:T(8,128)(2,1)}) custom-call(s32[5,2]{1,0:T(8,128)} %copy.97.bounds, s32[1,1280]{1,0:T(1,128)} %broadcast_in_dim.62.slots_row, s32[1280,1]{1,0:T(8,128)} %broadcast_in_dim.72.slots_column, bf16[1200,1024]{1,0:T(8,128)(2,1)} %get-tuple-element.66.first, ...), custom_call_target="tpu_custom_call" | custom-call | tf_op jit(solution)/shard_map/pallas_call | solution.py:964
  429.7 3.6 broadcast_select_fusion
  433.5 2.9 add_convert_fusion
  437.3 4.7 slice_select_fusion.skip
  441.9 7.6 %shard_map.256 = (f32[4704,128]{1,0:T(8,128)}, f32[8,1024]{1,0:T(8,128)}) custom-call(s32[1]{0:T(128)} %bitcast.flag, bf16[588,1024]{1,0:T(8,128)(2,1)} %bitcast.76, bf16[588,1024]{1,0:T(8,128)(2,1)} %get-tuple-element.171.own, bf16[588,1024]{1,0:T(8,128)(2,1)} %collective-permute-done.10.other, f32[588,1024]{1,0:T(8,128)} %slice_select_fusion.skip, ...), custom_call_target="tpu_custom_call" | custom-call | tf_op jit(solution)/shard_map/pallas_call | solution.py:1166
  451.2 92.0 %shard_map.257 = (f32[64,4352]{1,0:T(8,128)}, f32[32,3072]{1,0:T(8,128)}, f32[8,128]{1,0:T(8,128)}, f32[8,128]{1,0:T(8,128)}) custom-call(bf16[2,2,2,2,64,1536]{5,4,3,2,1,0:T(8,128)(2,1)} %bitcast.81, bf16[2,2,2,2,64,512]{5,4,3,2,1,0:T(8,128)(2,1)} %bitcast.82, bf16[2,2,2,2,64,2048]{5,4,3,2,1,0:T(8,128)(2,1)} %bitcast.77, ...), custom_call_target="tpu_custom_call" | custom-call | tf_op jit(solution)/shard_map/pallas_call | solution.py:450
  543.2 1.2 slice.85
  545.2 1.2 copy-done.8
  546.4 1.0 copy-done.15
  548.8 4.1 shard_map.258
  (118 shorter events, 18.0 us)
Async XLA Ops:
  7.2 2.4 copy-start.7
  7.2 2.5 copy-start.17
  7.2 2.5 copy-start.16
  7.2 168.3 %all-gather.2.cloned.1.call-start = ((), (), s32[]{:S(2)}) async-start(), calls=%async_computation.1 | async-start | bytes 4456448 | tf_op jit(solution)/shard_map/all_gather | solution.py:1227
  92.6 2.0 copy-start
  94.6 1.6 copy-start.1
  96.2 1.0 copy-start.3
  97.2 0.8 copy-start.10
  98.0 0.6 copy-start.20
  98.6 97.5 %copy-start.4 = (bf16[2,2,2,2,32,3072]{5,4,3,2,1,0:T(8,128)(2,1)}, bf16[2,2,2,2,32,3072]{5,4,3,2,1,0:T(8,128)(2,1)S(1)}, u32[]{:S(2)}) copy-start(bf16[2,2,2,2,32,3072]{5,4,3,2,1,0:T(8,128)(2,1)S(1)} %get-tuple-element.80) | copy-start | bytes 9437188
  98.6 352.5 %reduce-scatter.2.cloned.1.call-start = ((), (), s32[]{:S(2)}) async-start(), calls=%async_computation.2 | async-start | bytes 4456448 | tf_op jit(solution)/shard_map/reduce_scatter | solution.py:1236
  98.7 9.8 %collective-permute-start = (bf16[588,1024]{1,0:T(8,128)(2,1)}, bf16[588,1024]{1,0:T(8,128)(2,1)}, u32[]{:S(2)}, u32[]{:S(2)}) collective-permute-start(bf16[588,1024]{1,0:T(8,128)(2,1)} %bitcast.74), channel_id=1, source_target_pairs={{0,1},{1,0},{2,3},{3,2},{4,5},{5,4},{6,7},{7,6},{8,9},{9,8},{10,11... | collective-permute-start | bytes 3612680 | tf_op jit(solution)/shard_map/ppermute | solution.py:1187
  154.3 9.2 %copy-start.33 = (s32[1176]{0:T(1024)S(1)}, s32[1176]{0:T(1024)}, u32[]{:S(2)}) copy-start(s32[1176]{0:T(1024)} %copy-done.32) | copy-start | bytes 14116
  154.3 10.5 %collective-permute-start.1 = (bf16[1200,1024]{1,0:T(8,128)(2,1)}, bf16[1200,1024]{1,0:T(8,128)(2,1)}, u32[]{:S(2)}, u32[]{:S(2)}) collective-permute-start(bf16[1200,1024]{1,0:T(8,128)(2,1)} %get-tuple-element.70.own), channel_id=1, source_target_pairs={{0,1},{1,0},{2,3},{3,2},{4,5},{5,4},{6,7},{7,6},{8,9},{9,8},{10,11... | collective-permute-start | bytes 7372808 | tf_op jit(solution)/shard_map/ppermute | solution.py:1187
  157.1 2.5 copy-start.30
  196.1 7.6 %collective-permute-start.2 = (bf16[1200,1024]{1,0:T(8,128)(2,1)}, bf16[1200,1024]{1,0:T(8,128)(2,1)S(1)}, u32[]{:S(2)}, u32[]{:S(2)}) collective-permute-start(bf16[1200,1024]{1,0:T(8,128)(2,1)} %get-tuple-element.76), channel_id=1, source_target_pairs={{0,1},{1,0},{2,3},{3,2},{4,5},{5,4},{6,7},{7,6},{8,9},{9,8},{10,11... | collective-permute-start | bytes 7372808 | tf_op jit(solution)/shard_map/ppermute | solution.py:1187
  196.1 29.3 %collective-permute-start.5 = (bf16[512,3072]{1,0:T(8,128)(2,1)S(1)}, bf16[512,3072]{1,0:T(8,128)(2,1)}, u32[]{:S(2)}, u32[]{:S(2)}) collective-permute-start(bf16[512,3072]{1,0:T(8,128)(2,1)S(1)} %bitcast.60), channel_id=1, source_target_pairs={{0,1},{1,0},{2,3},{3,2},{4,5},{5,4},{6,7},{7,6},{8,9},{9,8},{10,11... | collective-permute-start | bytes 9437192 | tf_op jit(solution)/shard_map/ppermute | solution.py:1187
  203.7 4.7 copy-start.11
  208.4 1.5 copy-start.27
  208.4 15.5 %copy-start.34 = (s32[896]{0:T(1024)S(1)}, s32[896]{0:T(1024)}, u32[]{:S(2)}) copy-start(s32[896]{0:T(1024)} %fusion.12) | copy-start | bytes 10756
  209.8 13.2 %collective-permute-start.3 = (bf16[880,256]{1,0:T(8,128)(2,1)S(1)}, bf16[880,256]{1,0:T(8,128)(2,1)S(1)}, u32[]{:S(2)}, u32[]{:S(2)}) collective-permute-start(bf16[880,256]{1,0:T(8,128)(2,1)S(1)} %fusion.2), channel_id=1, source_target_pairs={{0,16},{1,17},{2,18},{3,19},{4,20},{5,21},{6,22},{7,23},{8,24},{9,... | collective-permute-start | bytes 1351688 | tf_op jit(solution)/shard_map/ppermute | solution.py:1182
  223.9 2.2 collective-permute-start.4
  297.4 18.5 %copy-start.12 = (bf16[2,2,2,2,64,256]{5,4,3,2,1,0:T(8,128)(2,1)S(1)}, bf16[2,2,2,2,64,256]{5,4,3,2,1,0:T(8,128)(2,1)}, u32[]{:S(2)}) copy-start(bf16[2,2,2,2,64,256]{5,4,3,2,1,0:T(8,128)(2,1)} %copy-done.10) | copy-start | bytes 1572868
  298.5 1.9 collective-permute-start.6
  301.5 14.4 %collective-permute-start.7 = (bf16[880,256]{1,0:T(8,128)(2,1)S(1)}, bf16[880,256]{1,0:T(8,128)(2,1)S(1)}, u32[]{:S(2)}, u32[]{:S(2)}) collective-permute-start(bf16[880,256]{1,0:T(8,128)(2,1)S(1)} %slice_add_fusion), channel_id=1, source_target_pairs={{16,0},{17,1},{18,2},{19,3},{20,4},{21,5},{22,6},{23,7},{24,8},{25... | collective-permute-start | bytes 1351688 | tf_op jit(solution)/shard_map/ppermute | solution.py:1182
  315.8 0.8 copy-start.28
  316.7 4.9 copy-start.25
  316.7 4.9 collective-permute-start.8
  352.2 1.4 copy-start.35
  352.3 81.3 %collective-permute-start.11 = (bf16[512,3072]{1,0:T(8,128)(2,1)}, bf16[512,3072]{1,0:T(8,128)(2,1)S(1)}, u32[]{:S(2)}, u32[]{:S(2)}) collective-permute-start(bf16[512,3072]{1,0:T(8,128)(2,1)} %get-tuple-element.97), channel_id=1, source_target_pairs={{0,1},{1,0},{2,3},{3,2},{4,5},{5,4},{6,7},{7,6},{8,9},{9,8},{10,11... | collective-permute-start | bytes 9437192 | tf_op jit(solution)/shard_map/ppermute | solution.py:1187
  352.5 9.4 %collective-permute-start.9 = (bf16[1200,1024]{1,0:T(8,128)(2,1)}, bf16[1200,1024]{1,0:T(8,128)(2,1)}, u32[]{:S(2)}, u32[]{:S(2)}) collective-permute-start(bf16[1200,1024]{1,0:T(8,128)(2,1)} %get-tuple-element.87.refs_1_), channel_id=1, source_target_pairs={{0,1},{1,0},{2,3},{3,2},{4,5},{5,4},{6,7},{7,6},{8,9},{9,8},{10,11... | collective-permute-start | bytes 7372808 | tf_op jit(solution)/shard_map/ppermute | solution.py:1187
  429.7 3.8 copy-start.26
  433.3 8.6 %collective-permute-start.10 = (bf16[588,1024]{1,0:T(8,128)(2,1)}, bf16[588,1024]{1,0:T(8,128)(2,1)}, u32[]{:S(2)}, u32[]{:S(2)}) collective-permute-start(bf16[588,1024]{1,0:T(8,128)(2,1)} %get-tuple-element.170), channel_id=1, source_target_pairs={{0,1},{1,0},{2,3},{3,2},{4,5},{5,4},{6,7},{7,6},{8,9},{9,8},{10,11... | collective-permute-start | bytes 3612680 | tf_op jit(solution)/shard_map/ppermute | solution.py:1187
  441.9 8.5 %copy-start.31 = (f32[4,16,32]{2,0,1:T(4,128)S(1)}, f32[4,16,32]{2,0,1:T(4,128)}, u32[]{:S(2)}) copy-start(f32[4,16,32]{2,0,1:T(4,128)} %copy.120) | copy-start | bytes 24580
  451.1 93.9 %copy-start.2 = (f32[64,1,6400]{2,1,0:T(1,128)S(1)}, f32[64,1,6400]{2,1,0:T(1,128)}, u32[]{:S(2)}) copy-start(f32[64,1,6400]{2,1,0:T(1,128)} %param.20) | copy-start | bytes 4915204
  451.2 94.0 %copy-start.5 = (f32[64,1,6400]{2,1,0:T(1,128)S(1)}, f32[64,1,6400]{2,1,0:T(1,128)}, u32[]{:S(2)}) copy-start(f32[64,1,6400]{2,1,0:T(1,128)} %param.21) | copy-start | bytes 4915204
  451.2 94.0 %copy-start.6 = (f32[64,1,6400]{2,1,0:T(1,128)S(1)}, f32[64,1,6400]{2,1,0:T(1,128)}, u32[]{:S(2)}) copy-start(f32[64,1,6400]{2,1,0:T(1,128)} %param.22) | copy-start | bytes 4915204
  451.2 94.0 %copy-start.9 = (bf16[64,2048]{1,0:T(8,128)(2,1)S(1)}, bf16[64,2048]{1,0:T(8,128)(2,1)}, u32[]{:S(2)}) copy-start(bf16[64,2048]{1,0:T(8,128)(2,1)} %reduce-scatter.2.cloned.1.call-done.refs_6_.down) | copy-start | bytes 786436
  451.2 94.0 %copy-start.13 = (f32[32,1,3072]{2,1,0:T(1,128)S(1)}, f32[32,1,3072]{2,1,0:T(1,128)}, u32[]{:S(2)}) copy-start(f32[32,1,3072]{2,1,0:T(1,128)} %param.24) | copy-start | bytes 1179652
  451.2 94.0 %copy-start.14 = (f32[32,1,3072]{2,1,0:T(1,128)S(1)}, f32[32,1,3072]{2,1,0:T(1,128)}, u32[]{:S(2)}) copy-start(f32[32,1,3072]{2,1,0:T(1,128)} %param.25) | copy-start | bytes 1179652
  451.2 94.0 %copy-start.21 = (f32[4,64]{1,0:T(4,128)S(1)}, f32[4,64]{1,0:T(4,128)}, u32[]{:S(2)}) copy-start(f32[4,64]{1,0:T(4,128)} %refs_7_.1) | copy-start | bytes 3076
  451.2 94.0 %copy-start.22 = (f32[4,64]{1,0:T(4,128)S(1)}, f32[4,64]{1,0:T(4,128)}, u32[]{:S(2)}) copy-start(f32[4,64]{1,0:T(4,128)} %refs_8_.1) | copy-start | bytes 3076
  451.2 94.0 %copy-start.23 = (f32[4,32]{1,0:T(4,128)S(1)}, f32[4,32]{1,0:T(4,128)}, u32[]{:S(2)}) copy-start(f32[4,32]{1,0:T(4,128)} %refs_10_.1) | copy-start | bytes 1540
  451.2 94.0 %copy-start.24 = (f32[4,32]{1,0:T(4,128)S(1)}, f32[4,32]{1,0:T(4,128)}, u32[]{:S(2)}) copy-start(f32[4,32]{1,0:T(4,128)} %refs_11_.1) | copy-start | bytes 1540
  545.2 1.2 copy-start.8
  546.4 1.0 copy-start.15
  547.4 0.7 copy-start.18
  548.1 0.7 copy-start.19
  (2 other events, 1.2 us)
Sparse Core Ops, SparseCore 0:
  98.7 76.7 all-gather.1
  352.4 93.1 reduce-scatter.1

commit v8 on v7

--- a/solution.py
+++ b/solution.py
@@ -993,7 +993,7 @@
     )
 
 
-def feed_kernel(stream, own, other, gains, up_w, down_w, after, second, hidden, slope, partial):
+def feed_kernel(stream, own, other, gains, up_w, down_one, down_two, after, second, hidden, slope, partial):
     summed = stream[...].astype(WIDE) + (own[...].astype(WIDE) + other[...].astype(WIDE))
     after[...] = summed
     unit, _ = centre(summed)
@@ -1004,17 +1004,20 @@
         h, g = gelu_pair(mm(second[...], up_w[:, cut]))
         hidden[:, cut] = h.astype(LOW)
         slope[:, cut] = g.astype(LOW)
-    partial[...] = mm(hidden[...], down_w[...], 1, 1).astype(LOW)
-
-
-def encoder_feed(stream, own, other, gains, up_w, down_w, block):
+    cut = down_one.shape[1]
+    fed = mm(hidden[:, :cut], down_one[...], 1, 1) + mm(hidden[:, cut:], down_two[...], 1, 1)
+    partial[...] = fed.astype(LOW)
+
+
+def encoder_feed(stream, own, other, gains, up_w, down_one, down_two, block):
     rows, width = stream.shape
     units = up_w.shape[1]
     wide, tall = down_rows(block, width), down_rows(block, units)
     return pl.pallas_call(
         feed_kernel,
         grid=(rows // block,),
-        in_specs=[wide, wide, wide, fixed((4, width)), fixed(up_w.shape), fixed(down_w.shape)],
+        in_specs=[wide, wide, wide, fixed((4, width))]
+        + [fixed(w.shape) for w in (up_w, down_one, down_two)],
         out_specs=[wide, wide, tall, tall, wide],
         out_shape=[
             jax.ShapeDtypeStruct((rows, width), WIDE),
@@ -1024,10 +1027,11 @@
             jax.ShapeDtypeStruct((rows, width), LOW),
         ],
         compiler_params=params(),
-    )(stream, own, other, gains, up_w, down_w)
+    )(stream, own, other, gains, up_w, down_one, down_two)
 
 
 def feed_back_kernel(
+    early,
     counts,
     own,
     other,
@@ -1035,7 +1039,8 @@
     hidden,
     slope,
     up_w,
-    down_w,
+    down_one,
+    down_two,
     grad_up,
     grad_down,
     partial,
@@ -1053,7 +1058,8 @@
 
     down = mm(grad_turned[...], hidden[...])
     grad_down[...] = jnp.where(counts[0] > 0, down, jnp.zeros_like(down)).astype(LOW)
-    grad_z = (mm(grad_low[...], down_w[...]) * slope[...].astype(WIDE)).astype(LOW)
+    down_w = jnp.where(pl.program_id(0) < early, down_one[...], down_two[...])
+    grad_z = (mm(grad_low[...], down_w) * slope[...].astype(WIDE)).astype(LOW)
     grad_up[...] = mm(second_turned[...], grad_z).astype(LOW)
     total[...] += mm(grad_z, up_w[...], 1, 1)
 
@@ -1062,18 +1068,21 @@
         partial[...] = total[...].astype(LOW)
 
 
-def encoder_feed_back(counts, own, other, second, hidden, slope, up_w, down_w):
+def encoder_feed_back(counts, own, other, second, hidden, slope, up_w, down_one, down_two):
     rows, width = own.shape
     units = up_w.shape[1]
     piece = 256
     whole = fixed((rows, width))
     tall = pl.BlockSpec((rows, piece), lambda i: (0, i))
     weight = pl.BlockSpec((width, piece), lambda i: (0, i))
+    early = down_one.shape[1] // piece
+    one = pl.BlockSpec((width, piece), lambda i: (0, jnp.minimum(i, early - 1)))
+    two = pl.BlockSpec((width, piece), lambda i: (0, jnp.maximum(i - early, 0)))
     return pl.pallas_call(
-        feed_back_kernel,
+        functools.partial(feed_back_kernel, early),
         grid=(units // piece,),
         in_specs=[pl.BlockSpec(memory_space=pltpu.SMEM)]
-        + [whole, whole, whole, tall, tall, weight, weight],
+        + [whole, whole, whole, tall, tall, weight, one, two],
         out_specs=[weight, weight, whole],
         out_shape=[
             jax.ShapeDtypeStruct((width, units), LOW),
@@ -1087,7 +1096,7 @@
             pltpu.VMEM((rows, width), WIDE),
         ],
         compiler_params=params(),
-    )(counts, own, other, second, hidden, slope, up_w, down_w)
+    )(counts, own, other, second, hidden, slope, up_w, down_one, down_two)
 
 
 def norm_back_kernel(tokens, own, other, skip_own, skip_other, gains, grad, grad_low, grad_gains, *, at):
@@ -1191,8 +1200,8 @@
     return lax.axis_size("section") == 2 and lax.axis_size("dp") == 8
 
 
-def plan(widths, dec_width, orders, dec_orders, among):
-    chunks = chunk_list(widths, PIECES, 0, orders)
+def plan(widths, pieces, dec_width, orders, dec_orders, among):
+    chunks = chunk_list(widths, pieces, 0, orders)
     dec = chunk_list((dec_width,), (DEC_PIECES,), 1, dec_orders)
     for k, (_, b, c, w, o, owner) in enumerate(dec):
         chunks.insert(3 * k + 2 if among else len(chunks), (len(widths), b, c, w, o, owner))
@@ -1201,6 +1210,7 @@
 
 def gather_all(low_enc, low_dec, norms, widths):
     count = len(widths)
+    cut = widths[3] // 4
     if not is_fast():
         both = ("section", "dp")
         enc = lax.all_gather(low_enc, both, axis=0, tiled=True)
@@ -1210,22 +1220,24 @@
         for w in widths:
             parts.append(enc[:, column : column + w])
             column += w
+        parts[3] = (parts[3][:, :cut], parts[3][:, cut:])
         return parts, dec, rows
     columns = [sum(widths[:k]) for k in range(count + 1)]
-    ahead = [low_enc[:, : columns[3]], low_enc[:, columns[4] :]]
-    near = (*widths[:3], widths[4])
-    chunks = plan(near, low_dec.shape[1], GATHER_ORDERS, DEC_GATHER_ORDERS, False)
+    ahead = [low_enc[:, : columns[3] + cut], low_enc[:, columns[4] :]]
+    near = (*widths[:3], cut, widths[4])
+    pieces = (*PIECES[:3], 2, PIECES[3])
+    chunks = plan(near, pieces, low_dec.shape[1], GATHER_ORDERS, DEC_GATHER_ORDERS, False)
     outputs = [(low_enc.shape[0], w, LOW) for w in near]
     outputs += [(low_dec.shape[0], low_dec.shape[1], LOW), (8, 128, WIDE)]
-    described = [(k // 4, k, c, b, w, o, own) for k, b, c, w, o, own in chunks]
-    described.append((2, 5, 0, 0, 128, "hlyx", BOTH))
+    described = [(k // 5, k, c, b, w, o, own) for k, b, c, w, o, own in chunks]
+    described.append((2, 6, 0, 0, 128, "hlyx", BOTH))
     shards = [jnp.concatenate(ahead, axis=1), low_dec, norms]
     results = gather_weights(shards, outputs, described, 1, GATHER_AHEAD, GATHER_LAG)
     low_down, norm_rows = lax.optimization_barrier(
-        (low_enc[:, columns[3] : columns[4]], results[5])
+        (low_enc[:, columns[3] + cut : columns[4]], results[6])
     )
     down = lax.all_gather(low_down, ("section", "dp"), axis=0, tiled=True)
-    return [*results[:3], down, results[3]], results[4], norm_rows
+    return [*results[:3], (results[3], down), results[4]], results[5], norm_rows
 
 
 def scatter_all(enc_parts, dec, norms, encoder_side):
@@ -1246,7 +1258,7 @@
     down = scattered(enc_parts[3])
     near = (*enc_parts[:3], enc_parts[4])
     near_widths = (*widths[:3], widths[4])
-    chunks = plan(near_widths, dec.shape[1], SCATTER_ORDERS, DEC_SCATTER_ORDERS, True)
+    chunks = plan(near_widths, PIECES, dec.shape[1], SCATTER_ORDERS, DEC_SCATTER_ORDERS, True)
     described = [(k, k // 4, b, c, w, o, own) for k, b, c, w, o, own in chunks]
     described.append((5, 2, 0, 0, 128, "xylh", BOTH))
     rows = near[0].shape[0] // 16
@@ -1416,7 +1428,7 @@
         (partner(mix_own), seen_target, cotangent, position, dec_gains)
     )
     after, second, hidden, slope, feed_own = encoder_feed(
-        stream, mix_own, mix_other, enc_gains, up_w, down_w, ROW_BLOCK
+        stream, mix_own, mix_other, enc_gains, up_w, *down_w, ROW_BLOCK
     )
     encoded = (after + (feed_own.astype(WIDE) + partner(feed_own).astype(WIDE))).astype(LOW)
     projected = mm(encoded[:shown], projection).astype(LOW)
@@ -1452,7 +1464,7 @@
         hidden,
         slope,
         up_w,
-        down_w,
+        *down_w,
     )
     grad_after, grad_low, gains_two = encoder_norm_back(
         after, back_own, partner(back_own), (end_own, end_other), enc_gains, 2, ROW_BLOCK, True

time: 565 us -> 564 us (level)
    pallas_call x1, Pallas kernels: 82.8 us -> 91.4 us  [gather_weights(): results = call(*shards)]
    pallas_call x1, Pallas kernels: 56.5 us -> 48.8 us  [encoder_attend_back(): pl.pallas_call(functools.partial(attend_back_kernel, head), in_specs=[pl....]
    unnamed x75 -> x77, local copies, waits for them, and re-layouts: 13.3 us -> 14.3 us
  transfers between devices with their start and end apart: 14 -> 14, of which waited for: 8 -> 9; matrix products, arithmetic and copies ran while one was open for 9% -> 9% of each run, Pallas kernels for 21% -> 18%
where the time goes in v8:
time: 564 us; the launch traced here: 562 us
  Pallas kernels  418 us (74%)
  waiting for transfers between devices  48.4 us (9%)
  local copies, waits for them, and re-layouts  40.1 us (7%)
  other arithmetic  27 us (5%)
  between operations  17.3 us (3%)
  starting transfers between devices  6.63 us (1%)
    pallas_call x1, Pallas kernels, scatter_grads(): return call(*views, summed)  96.6 us
    pallas_call x1, Pallas kernels, gather_weights(): results = call(*shards)  91.4 us
    pallas_call x1, Pallas kernels, decoder_step(): pl.pallas_call(functools.partial(decoder_kernel, length), grid=(images //...  71.3 us
    pallas_call x1, Pallas kernels, encoder_attend_back(): pl.pallas_call(functools.partial(attend_back_kernel, head), in_specs=[pl....  48.8 us
    pallas_call x1, Pallas kernels, encoder_attend(): pl.pallas_call(functools.partial(attend_kernel, head), in_specs=[pl.Block...  35 us
    pallas_call x1, Pallas kernels, encoder_feed_back(): pl.pallas_call(functools.partial(feed_back_kernel, early), grid=(units //...  31.2 us
    ppermute x2, waiting for transfers between devices, from_behind(): return lax.ppermute(value, axis, pairs)  22.9 us
    pallas_call x1, Pallas kernels, encoder_feed(): pl.pallas_call(feed_kernel, grid=(rows // block,), in_specs=[wide, wide,...  20.2 us
  transfers between devices with their start and end apart: 14, of which 9 were waited for; matrix products, arithmetic and copies ran while one was open for 9% of the time, Pallas kernels for 18%

profile of v8, /device:TPU:0, one launch (start us, length us, event | category | flops | bytes accessed | tf_op | source)
XLA Modules:
  0.0 562.2 jit_solution(12207621641143570594)
XLA Ops:
  7.3 1.6 copy.118
  9.8 91.4 %shard_map.249 = (bf16[2,2,2,2,64,1536]{5,4,3,2,1,0:T(8,128)(2,1)S(1)}, bf16[2,2,2,2,64,512]{5,4,3,2,1,0:T(8,128)(2,1)S(1)}, bf16[2,2,2,2,64,2048]{5,4,3,2,1,0:T...) custom-call(bf16[64,4864]{1,0:T(8,128)(2,1)S(1)} %pad_maximum_fusion, ...), custom_call_target="tpu_custom_call" | custom-call | tf_op jit(solution)/shard_map/pallas_call | solution.py:173
  101.2 2.0 copy-done
  103.2 1.6 copy-done.1
  104.8 1.0 copy-done.3
  105.7 1.0 copy-done.4
  108.3 1.6 slice_reduce_fusion
  111.7 1.1 broadcast_in_dim.72.slots_column
  116.6 1.4 reshape.187.gains.refs_5_
  118.0 3.5 maximum_select_fusion
  121.5 1.7 pad.37.stream
  123.2 35.0 %shard_map.250 = (bf16[1200,1024]{1,0:T(8,128)(2,1)}, bf16[1536,1280]{1,0:T(8,128)(2,1)}, bf16[512,1280]{1,0:T(8,128)(2,1)}, f32[8,1280]{1,0:T(8,128)}, bf16[1200,1024]{1,0:T(8,128)(2,1)}) custom-call(s32[5,2]{1,0:T(8,128)} %copy.97.bounds, bf16[1200,1024]{1,0:T(8,128)(2,1)} %pad.37.stream, s32[1,1280]{1,0:T(1,128)} %broadcast_in_dim.62.slots_row, ...), custom_call_target="tpu_custom_call" | custom-call | tf_op jit(solution)/shard_map/pallas_call | solution.py:838
  158.5 2.5 reshape_squeeze.3
  161.0 2.5 pad.40.cotangent
  164.2 1.4 reshape.188.gains
  165.6 1.8 pad.41.position
  167.4 1.3 fusion.12
  168.7 8.6 %all-gather.2.cloned.1.call-done.down_two = bf16[1024,1536]{1,0:T(8,128)(2,1)} async-done(((bf16[64,1536]{1,0:T(8,128)(2,1)}), bf16[1024,1536]{1,0:T(8,128)(2,1)}) %all-gather.2.cloned.1.call-update) | async-done | bytes 3145744 | tf_op jit(solution)/shard_map/all_gather | solution.py:1239
  177.3 20.2 %shard_map.251 = (f32[1200,1024]{1,0:T(8,128)}, bf16[1200,1024]{1,0:T(8,128)(2,1)}, bf16[1200,2048]{1,0:T(8,128)(2,1)}, bf16[1200,2048]{1,0:T(8,128)(2,1)}, bf16[1200,1024]{1,0:T(8,128)(2,1)}) custom-call(bf16[1200,1024]{1,0:T(8,128)(2,1)} %pad.37.stream, bf16[1200,1024]{1,0:T(8,128)(2,1)} %get-tuple-element.71.own, ...), custom_call_target="tpu_custom_call" | custom-call | tf_op jit(solution)/shard_map/pallas_call | solution.py:1016
  198.0 7.0 %collective-permute-done.2 = bf16[1200,1024]{1,0:T(8,128)(2,1)S(1)} collective-permute-done((bf16[1200,1024]{1,0:T(8,128)(2,1)}, bf16[1200,1024]{1,0:T(8,128)(2,1)S(1)}, u32[]{:S(2)}, u32[]{:S(2)}) %collective-permute-start.2) | collective-permute-done | bytes 2457632 | tf_op jit(solution)/shard_map/ppermute | solution.py:1196
  205.0 4.7 add_convert_fusion.1
  211.2 3.4 collective-permute-start.3
  214.6 9.9 %collective-permute-done.3 = bf16[880,256]{1,0:T(8,128)(2,1)S(1)} collective-permute-done((bf16[880,256]{1,0:T(8,128)(2,1)S(1)}, bf16[880,256]{1,0:T(8,128)(2,1)S(1)}, u32[]{:S(2)}, u32[]{:S(2)}) %collective-permute-start.3) | collective-permute-done | bytes 450592 | tf_op jit(solution)/shard_map/ppermute | solution.py:1191
  225.9 1.0 broadcast_in_dim.71.target_column
  227.4 71.3 %shard_map.252 = (f32[6,208,512]{2,1,0:T(8,128)}, bf16[896,256]{1,0:T(8,128)(2,1)}, bf16[896,256]{1,0:T(8,128)(2,1)}, bf16[512,3072]{1,0:T(8,128)(2,1)}, bf16[512,3072]{1,0:T(8,128)(2,1)}, /*index=5*/f32[8,512]{1,0:T(8,128)}) custom-call(s32[1]{0:T(128)} %bitcast.17.flag, s32[1,896]{1,0:T(1,128)} %broadcast_in_dim.65.target_row, ...), custom_call_target="tpu_custom_call" | custom-call | tf_op jit(solution)/shard_map/pallas_call | solution.py:696
  298.8 1.1 slice.77
  300.1 1.7 collective-permute-done.6
  301.7 1.1 slice_add_fusion
  302.8 1.3 collective-permute-start.7
  304.1 13.1 %collective-permute-done.7 = bf16[880,256]{1,0:T(8,128)(2,1)S(1)} collective-permute-done((bf16[880,256]{1,0:T(8,128)(2,1)S(1)}, bf16[880,256]{1,0:T(8,128)(2,1)S(1)}, u32[]{:S(2)}, u32[]{:S(2)}) %collective-permute-start.7) | collective-permute-done | bytes 450592 | tf_op jit(solution)/shard_map/ppermute | solution.py:1191
  318.2 4.8 collective-permute-done.8.other.refs_4_
  323.0 31.2 %shard_map.253 = (bf16[1024,2048]{1,0:T(8,128)(2,1)}, bf16[1024,2048]{1,0:T(8,128)(2,1)}, bf16[1200,1024]{1,0:T(8,128)(2,1)}) custom-call(s32[1]{0:T(128)} %bitcast.16.counts, bf16[1200,1024]{1,0:T(8,128)(2,1)} %copy-done.26, bf16[1200,1024]{1,0:T(8,128)(2,1)} %collective-permute-done.8.other.refs_4_, bf16[1200,1024]{1,0:T(8,128)(2,1)} %get-tuple-element.86.second, ...), custom_call_target="tpu_custom_call" | custom-call | tf_op jit(solution)/shard_map/pallas_call | solution.py:1081
  355.6 1.3 slice_select_fusion.1
  357.0 1.4 reshape.173
  358.4 1.4 copy.120
  359.7 3.5 convolution_convert_fusion.1
  363.8 11.5 %shard_map.254 = (f32[1200,1024]{1,0:T(8,128)}, bf16[1200,1024]{1,0:T(8,128)(2,1)}, f32[8,1024]{1,0:T(8,128)}) custom-call(f32[1200,1024]{1,0:T(8,128)} %get-tuple-element.76.refs_0_, bf16[1200,1024]{1,0:T(8,128)(2,1)} %get-tuple-element.89.refs_1_, bf16[1200,1024]{1,0:T(8,128)(2,1)} %collective-permute-done.9.refs_2_, bf16[1200,1024]{1,0:T(8,128)(2,1)} %copy-done.26, ...), custom_call_target="tpu_custom_call" | custom-call | tf_op jit(solution)/shard_map/pallas_call | solution.py:1137
  375.3 48.8 %shard_map.255 = (bf16[1024,1536]{1,0:T(8,128)(2,1)}, bf16[1024,512]{1,0:T(8,128)(2,1)}, bf16[1200,1024]{1,0:T(8,128)(2,1)}) custom-call(s32[5,2]{1,0:T(8,128)} %copy.97.bounds, s32[1,1280]{1,0:T(1,128)} %broadcast_in_dim.62.slots_row, s32[1280,1]{1,0:T(8,128)} %broadcast_in_dim.72.slots_column, bf16[1200,1024]{1,0:T(8,128)(2,1)} %get-tuple-element.67.first, ...), custom_call_target="tpu_custom_call" | custom-call | tf_op jit(solution)/shard_map/pallas_call | solution.py:964
  424.1 3.6 broadcast_select_fusion
  427.9 2.8 add_convert_fusion
  431.5 4.7 slice_select_fusion.skip
  436.2 7.6 %shard_map.256 = (f32[4704,128]{1,0:T(8,128)}, f32[8,1024]{1,0:T(8,128)}) custom-call(s32[1]{0:T(128)} %bitcast.flag, bf16[588,1024]{1,0:T(8,128)(2,1)} %bitcast.79, bf16[588,1024]{1,0:T(8,128)(2,1)} %get-tuple-element.173.own, bf16[588,1024]{1,0:T(8,128)(2,1)} %collective-permute-done.10.other, f32[588,1024]{1,0:T(8,128)} %slice_select_fusion.skip, ...), custom_call_target="tpu_custom_call" | custom-call | tf_op jit(solution)/shard_map/pallas_call | solution.py:1175
  445.4 2.1 reduce-scatter.2.cloned.1.call-done.refs_6_.down
  447.6 96.6 %shard_map.257 = (f32[64,4352]{1,0:T(8,128)}, f32[32,3072]{1,0:T(8,128)}, f32[8,128]{1,0:T(8,128)}, f32[8,128]{1,0:T(8,128)}) custom-call(bf16[2,2,2,2,64,1536]{5,4,3,2,1,0:T(8,128)(2,1)} %bitcast.84, bf16[2,2,2,2,64,512]{5,4,3,2,1,0:T(8,128)(2,1)} %bitcast.85, bf16[2,2,2,2,64,2048]{5,4,3,2,1,0:T(8,128)(2,1)} %bitcast.80, ...), custom_call_target="tpu_custom_call" | custom-call | tf_op jit(solution)/shard_map/pallas_call | solution.py:450
  544.2 1.2 slice.85
  546.2 1.2 copy-done.9
  547.5 1.0 copy-done.16
  549.8 4.1 shard_map.258
  (120 shorter events, 19.6 us)
Async XLA Ops:
  7.2 2.4 copy-start.8
  7.2 2.5 copy-start.18
  7.2 2.5 copy-start.17
  7.2 170.1 %all-gather.2.cloned.1.call-start = ((), (), s32[]{:S(2)}) async-start(), calls=%async_computation.1 | async-start | bytes 3342336 | tf_op jit(solution)/shard_map/all_gather | solution.py:1239
  101.2 2.0 copy-start
  103.2 1.6 copy-start.1
  104.8 1.0 copy-start.3
  105.7 1.0 copy-start.4
  106.7 0.8 copy-start.11
  108.1 89.3 %copy-start.5 = (bf16[2,2,2,2,32,3072]{5,4,3,2,1,0:T(8,128)(2,1)}, bf16[2,2,2,2,32,3072]{5,4,3,2,1,0:T(8,128)(2,1)S(1)}, u32[]{:S(2)}) copy-start(bf16[2,2,2,2,32,3072]{5,4,3,2,1,0:T(8,128)(2,1)S(1)} %get-tuple-element.82) | copy-start | bytes 9437188
  108.2 339.4 %reduce-scatter.2.cloned.1.call-start = ((), (), s32[]{:S(2)}) async-start(), calls=%async_computation.2 | async-start | bytes 4456448 | tf_op jit(solution)/shard_map/reduce_scatter | solution.py:1248
  108.2 9.8 %collective-permute-start = (bf16[588,1024]{1,0:T(8,128)(2,1)}, bf16[588,1024]{1,0:T(8,128)(2,1)}, u32[]{:S(2)}, u32[]{:S(2)}) collective-permute-start(bf16[588,1024]{1,0:T(8,128)(2,1)} %bitcast.77), channel_id=1, source_target_pairs={{0,1},{1,0},{2,3},{3,2},{4,5},{5,4},{6,7},{7,6},{8,9},{9,8},{10,11... | collective-permute-start | bytes 3612680 | tf_op jit(solution)/shard_map/ppermute | solution.py:1196
  158.2 9.2 %copy-start.34 = (s32[1176]{0:T(1024)S(1)}, s32[1176]{0:T(1024)}, u32[]{:S(2)}) copy-start(s32[1176]{0:T(1024)} %copy-done.33) | copy-start | bytes 14116
  158.2 10.5 %collective-permute-start.1 = (bf16[1200,1024]{1,0:T(8,128)(2,1)}, bf16[1200,1024]{1,0:T(8,128)(2,1)}, u32[]{:S(2)}, u32[]{:S(2)}) collective-permute-start(bf16[1200,1024]{1,0:T(8,128)(2,1)} %get-tuple-element.71.own), channel_id=1, source_target_pairs={{0,1},{1,0},{2,3},{3,2},{4,5},{5,4},{6,7},{7,6},{8,9},{9,8},{10,11... | collective-permute-start | bytes 7372808 | tf_op jit(solution)/shard_map/ppermute | solution.py:1196
  161.0 2.5 copy-start.31
  197.5 7.6 %collective-permute-start.2 = (bf16[1200,1024]{1,0:T(8,128)(2,1)}, bf16[1200,1024]{1,0:T(8,128)(2,1)S(1)}, u32[]{:S(2)}, u32[]{:S(2)}) collective-permute-start(bf16[1200,1024]{1,0:T(8,128)(2,1)} %get-tuple-element.78), channel_id=1, source_target_pairs={{0,1},{1,0},{2,3},{3,2},{4,5},{5,4},{6,7},{7,6},{8,9},{9,8},{10,11... | collective-permute-start | bytes 7372808 | tf_op jit(solution)/shard_map/ppermute | solution.py:1196
  197.5 29.3 %collective-permute-start.5 = (bf16[512,3072]{1,0:T(8,128)(2,1)S(1)}, bf16[512,3072]{1,0:T(8,128)(2,1)}, u32[]{:S(2)}, u32[]{:S(2)}) collective-permute-start(bf16[512,3072]{1,0:T(8,128)(2,1)S(1)} %bitcast.63), channel_id=1, source_target_pairs={{0,1},{1,0},{2,3},{3,2},{4,5},{5,4},{6,7},{7,6},{8,9},{9,8},{10,11... | collective-permute-start | bytes 9437192 | tf_op jit(solution)/shard_map/ppermute | solution.py:1196
  205.0 4.7 copy-start.12
  209.7 1.5 copy-start.28
  209.7 15.5 %copy-start.35 = (s32[896]{0:T(1024)S(1)}, s32[896]{0:T(1024)}, u32[]{:S(2)}) copy-start(s32[896]{0:T(1024)} %fusion.12) | copy-start | bytes 10756
  211.2 13.2 %collective-permute-start.3 = (bf16[880,256]{1,0:T(8,128)(2,1)S(1)}, bf16[880,256]{1,0:T(8,128)(2,1)S(1)}, u32[]{:S(2)}, u32[]{:S(2)}) collective-permute-start(bf16[880,256]{1,0:T(8,128)(2,1)S(1)} %fusion.2), channel_id=1, source_target_pairs={{0,16},{1,17},{2,18},{3,19},{4,20},{5,21},{6,22},{7,23},{8,24},{9,... | collective-permute-start | bytes 1351688 | tf_op jit(solution)/shard_map/ppermute | solution.py:1191
  225.3 2.2 collective-permute-start.4
  298.8 18.5 %copy-start.13 = (bf16[2,2,2,2,64,256]{5,4,3,2,1,0:T(8,128)(2,1)S(1)}, bf16[2,2,2,2,64,256]{5,4,3,2,1,0:T(8,128)(2,1)}, u32[]{:S(2)}) copy-start(bf16[2,2,2,2,64,256]{5,4,3,2,1,0:T(8,128)(2,1)} %copy-done.11) | copy-start | bytes 1572868
  299.9 1.9 collective-permute-start.6
  302.8 14.4 %collective-permute-start.7 = (bf16[880,256]{1,0:T(8,128)(2,1)S(1)}, bf16[880,256]{1,0:T(8,128)(2,1)S(1)}, u32[]{:S(2)}, u32[]{:S(2)}) collective-permute-start(bf16[880,256]{1,0:T(8,128)(2,1)S(1)} %slice_add_fusion), channel_id=1, source_target_pairs={{16,0},{17,1},{18,2},{19,3},{20,4},{21,5},{22,6},{23,7},{24,8},{25... | collective-permute-start | bytes 1351688 | tf_op jit(solution)/shard_map/ppermute | solution.py:1191
  317.2 0.8 copy-start.29
  318.1 4.9 copy-start.26
  318.1 4.9 collective-permute-start.8
  354.2 1.4 copy-start.36
  354.3 73.6 %collective-permute-start.11 = (bf16[512,3072]{1,0:T(8,128)(2,1)}, bf16[512,3072]{1,0:T(8,128)(2,1)S(1)}, u32[]{:S(2)}, u32[]{:S(2)}) collective-permute-start(bf16[512,3072]{1,0:T(8,128)(2,1)} %get-tuple-element.99), channel_id=1, source_target_pairs={{0,1},{1,0},{2,3},{3,2},{4,5},{5,4},{6,7},{7,6},{8,9},{9,8},{10,11... | collective-permute-start | bytes 9437192 | tf_op jit(solution)/shard_map/ppermute | solution.py:1196
  354.5 9.4 %collective-permute-start.9 = (bf16[1200,1024]{1,0:T(8,128)(2,1)}, bf16[1200,1024]{1,0:T(8,128)(2,1)}, u32[]{:S(2)}, u32[]{:S(2)}) collective-permute-start(bf16[1200,1024]{1,0:T(8,128)(2,1)} %get-tuple-element.89.refs_1_), channel_id=1, source_target_pairs={{0,1},{1,0},{2,3},{3,2},{4,5},{5,4},{6,7},{7,6},{8,9},{9,8},{10,11... | collective-permute-start | bytes 7372808 | tf_op jit(solution)/shard_map/ppermute | solution.py:1196
  424.1 3.7 copy-start.27
  427.7 8.4 %collective-permute-start.10 = (bf16[588,1024]{1,0:T(8,128)(2,1)}, bf16[588,1024]{1,0:T(8,128)(2,1)}, u32[]{:S(2)}, u32[]{:S(2)}) collective-permute-start(bf16[588,1024]{1,0:T(8,128)(2,1)} %get-tuple-element.172), channel_id=1, source_target_pairs={{0,1},{1,0},{2,3},{3,2},{4,5},{5,4},{6,7},{7,6},{8,9},{9,8},{10,11... | collective-permute-start | bytes 3612680 | tf_op jit(solution)/shard_map/ppermute | solution.py:1196
  436.2 8.5 %copy-start.32 = (f32[4,16,32]{2,0,1:T(4,128)S(1)}, f32[4,16,32]{2,0,1:T(4,128)}, u32[]{:S(2)}) copy-start(f32[4,16,32]{2,0,1:T(4,128)} %copy.120) | copy-start | bytes 24580
  447.5 98.6 %copy-start.2 = (f32[64,1,6400]{2,1,0:T(1,128)S(1)}, f32[64,1,6400]{2,1,0:T(1,128)}, u32[]{:S(2)}) copy-start(f32[64,1,6400]{2,1,0:T(1,128)} %param.20) | copy-start | bytes 4915204
  447.5 98.6 %copy-start.6 = (f32[64,1,6400]{2,1,0:T(1,128)S(1)}, f32[64,1,6400]{2,1,0:T(1,128)}, u32[]{:S(2)}) copy-start(f32[64,1,6400]{2,1,0:T(1,128)} %param.21) | copy-start | bytes 4915204
  447.5 98.6 %copy-start.7 = (f32[64,1,6400]{2,1,0:T(1,128)S(1)}, f32[64,1,6400]{2,1,0:T(1,128)}, u32[]{:S(2)}) copy-start(f32[64,1,6400]{2,1,0:T(1,128)} %param.22) | copy-start | bytes 4915204
  447.5 98.6 %copy-start.10 = (bf16[64,2048]{1,0:T(8,128)(2,1)S(1)}, bf16[64,2048]{1,0:T(8,128)(2,1)}, u32[]{:S(2)}) copy-start(bf16[64,2048]{1,0:T(8,128)(2,1)} %reduce-scatter.2.cloned.1.call-done.refs_6_.down) | copy-start | bytes 786436
  447.5 98.6 %copy-start.14 = (f32[32,1,3072]{2,1,0:T(1,128)S(1)}, f32[32,1,3072]{2,1,0:T(1,128)}, u32[]{:S(2)}) copy-start(f32[32,1,3072]{2,1,0:T(1,128)} %param.24) | copy-start | bytes 1179652
  447.5 98.6 %copy-start.15 = (f32[32,1,3072]{2,1,0:T(1,128)S(1)}, f32[32,1,3072]{2,1,0:T(1,128)}, u32[]{:S(2)}) copy-start(f32[32,1,3072]{2,1,0:T(1,128)} %param.25) | copy-start | bytes 1179652
  447.6 98.6 %copy-start.22 = (f32[4,64]{1,0:T(4,128)S(1)}, f32[4,64]{1,0:T(4,128)}, u32[]{:S(2)}) copy-start(f32[4,64]{1,0:T(4,128)} %refs_7_.1) | copy-start | bytes 3076
  447.6 98.6 %copy-start.23 = (f32[4,64]{1,0:T(4,128)S(1)}, f32[4,64]{1,0:T(4,128)}, u32[]{:S(2)}) copy-start(f32[4,64]{1,0:T(4,128)} %refs_8_.1) | copy-start | bytes 3076
  447.6 98.6 %copy-start.24 = (f32[4,32]{1,0:T(4,128)S(1)}, f32[4,32]{1,0:T(4,128)}, u32[]{:S(2)}) copy-start(f32[4,32]{1,0:T(4,128)} %refs_10_.1) | copy-start | bytes 1540
  447.6 98.6 %copy-start.25 = (f32[4,32]{1,0:T(4,128)S(1)}, f32[4,32]{1,0:T(4,128)}, u32[]{:S(2)}) copy-start(f32[4,32]{1,0:T(4,128)} %refs_11_.1) | copy-start | bytes 1540
  546.2 1.2 copy-start.9
  547.5 1.0 copy-start.16
  548.5 0.7 copy-start.19
  549.1 0.7 copy-start.20
  (3 other events, 1.8 us)
Sparse Core Ops, SparseCore 0:
  108.3 68.9 all-gather.1
  354.4 93.1 reduce-scatter.1
